TPU v7x, 32 devices: a whole 2x2x4 slice. The times are simulated.
32 devices in a mesh: gx: 4 (over y, x), gy: 8 (over z, core).
Axes of the slice: x: 2, y: 2, z: 4, core: 2. Of those that a mesh axis runs over, the one named last changes fastest.
Arguments:
- populations: float32 [19, 8, 32, 4096], P(None, None, 'gx', 'gy'), may hold values from 0 to 1, as said below
- solid: int32 [8, 32, 4096], P(None, 'gx', 'gy'), may hold values from 0 to 1, as said below
- panel_cells: int32 [32, 8], P(('gx', 'gy')), may hold values from 0 to 4095
- panel_counts: int32 [32], P(('gx', 'gy')), may hold values from 0 to 8, as said below
- owner: int32 [32], replicated, may hold values from 0 to 31, each once
- retarded: bfloat16 [32, 8, 4, 256, 256], P(('gx', 'gy')), may hold values from -2 to 2
Outputs:
- fields: float32 [4, 8, 32, 4096], P(None, None, 'gx', 'gy')
- owned_signal: float32 [256, 256], P(('gx', 'gy'))
Inputs may be any that keep to these rules, and one draw needn't show every extreme that they name: `populations`: every population is positive and every cell's density lies between 0.7 and 1.3. 1 marks a solid cell; a solid column runs from the ground up. `panel_counts`: some tile has all 8 slots live; many tiles have none. `owner`: each listener block is owned by one tile.
All inputs are finite; a program needn't handle non-finite values.
Results may differ from a plain program's by a relative error of at most 0.0039.
Values sent between devices are 32-bit elements; how exact they have to be, the bound alone decides.
No kernel may reach another device: no remote copies, remote signals or barrier semaphores. Data moves between devices by JAX's collectives and lax.ppermute only.
A program may use at most 384 MiB of HBM per device.

v0:
```python
import jax
import jax.numpy as jnp
from jax import lax
from jax.sharding import PartitionSpec as P

STEPS = 8


VELOCITIES = (
    (0, 0, 0),
    (1, 0, 0),
    (-1, 0, 0),
    (0, 1, 0),
    (0, -1, 0),
    (0, 0, 1),
    (0, 0, -1),
    (1, 1, 0),
    (-1, -1, 0),
    (1, -1, 0),
    (-1, 1, 0),
    (1, 0, 1),
    (-1, 0, -1),
    (1, 0, -1),
    (-1, 0, 1),
    (0, 1, 1),
    (0, -1, -1),
    (0, 1, -1),
    (0, -1, 1),
)
WEIGHTS = (1.0 / 3.0,) + (1.0 / 18.0,) * 6 + (1.0 / 36.0,) * 12
relax_rate = 1.6


def extended(shard, sides, width):
    for axis, dim in sides:
        devices, length = (lax.axis_size(axis), shard.shape[dim])
        up = [(i, (i + 1) % devices) for i in range(devices)]
        down = [(j, i) for i, j in up]
        last = lax.slice_in_dim(shard, length - width, length, axis=dim)
        initial = lax.slice_in_dim(shard, 0, width, axis=dim)
        before = lax.ppermute(last, axis, up)
        after = lax.ppermute(initial, axis, down)
        shard = jnp.concatenate([before, shard, after], axis=dim)
    return shard


def opposite(member):
    if member == 0:
        return 0
    return member + 1 if member % 2 == 1 else member - 1


def moment(state, axis_number):
    total = jnp.zeros_like(state[0])
    for member, velocity in enumerate(VELOCITIES):
        if velocity[axis_number] > 0:
            total = total + state[member]
        elif velocity[axis_number] < 0:
            total = total - state[member]
    return total


def moments_of(state):
    return jnp.stack([jnp.sum(state, axis=0), moment(state, 0), moment(state, 1), moment(state, 2)])


def collide(state):
    density = jnp.sum(state, axis=0)
    speed_x = moment(state, 0) / density
    speed_y = moment(state, 1) / density
    speed_z = moment(state, 2) / density
    speed_sq = speed_x * speed_x + speed_y * speed_y + speed_z * speed_z
    relaxed = []
    for member, velocity in enumerate(VELOCITIES):
        along = velocity[0] * speed_x + velocity[1] * speed_y + velocity[2] * speed_z
        balance = (
            WEIGHTS[member] * density * (1.0 + 3.0 * along + 4.5 * along * along - 1.5 * speed_sq)
        )
        relaxed.append(state[member] - relax_rate * (state[member] - balance))
    return jnp.stack(relaxed)


def shift_vertical(field, step_z, fill):
    if step_z == 0:
        return field
    border = jnp.full_like(field[:1], fill)
    if step_z > 0:
        return jnp.concatenate([border, field[:-1]], axis=0)
    return jnp.concatenate([field[1:], border], axis=0)


def stream(relaxed, walls):
    span_x = relaxed.shape[2] - 2
    span_y = relaxed.shape[3] - 2
    read = []
    for member, velocity in enumerate(VELOCITIES):
        step_x, step_y, step_z = velocity
        source = relaxed[
            member, :, 1 - step_x : 1 - step_x + span_x, 1 - step_y : 1 - step_y + span_y
        ]
        blocked = walls[:, 1 - step_x : 1 - step_x + span_x, 1 - step_y : 1 - step_y + span_y]
        source = shift_vertical(source, step_z, 0.0)
        blocked = shift_vertical(blocked, step_z, 1)
        reflected = relaxed[opposite(member), :, 1 : 1 + span_x, 1 : 1 + span_y]
        read.append(jnp.where(blocked > 0, reflected, source))
    return jnp.stack(read)


def on_device(populations, solid, panel_cells, panel_counts, owner, retarded):
    state = populations
    walls = extended(solid, (("gx", 1), ("gy", 2)), 1)
    for step in range(STEPS):
        relaxed = collide(state)
        padded = extended(relaxed, (("gx", 2), ("gy", 3)), 1)
        state = stream(padded, walls)
    fields = moments_of(state)
    column = jnp.mean(fields, axis=1)
    slots = panel_cells.shape[1]
    flat = column.reshape(4, column.shape[1] * column.shape[2])
    picked = jnp.take(flat, panel_cells[0], axis=1)
    offset = jnp.array([1.0, 0.0, 0.0, 0.0], dtype=jnp.float32)[:, None]
    live = jnp.arange(slots, dtype=jnp.int32)[None, :] < panel_counts[0]
    sources = jnp.where(live, picked - offset, 0.0).T.astype(jnp.bfloat16)
    listeners = retarded.shape[3]
    bins = retarded.shape[4]
    rows_gx = lax.axis_size("gx")
    rows_gy = lax.axis_size("gy")
    tiles = rows_gx * rows_gy
    block = listeners // tiles
    partial_value = jnp.dot(
        sources.reshape(1, slots * 4),
        retarded[0].reshape(slots * 4, listeners * bins),
        preferred_element_type=jnp.float32,
    )
    ordered = partial_value.reshape(tiles, block, bins)[owner]
    stacked = ordered.reshape(tiles * block, bins)
    owned_signal = lax.psum_scatter(stacked, ("gx", "gy"), scatter_dimension=0, tiled=True)
    return (fields, owned_signal)


def solution(mesh):
    in_specs = (
        P(None, None, "gx", "gy"),
        P(None, "gx", "gy"),
        P(("gx", "gy"), None),
        P(("gx", "gy")),
        P(),
        P(("gx", "gy"), None, None, None, None),
    )
    out_specs = (P(None, None, "gx", "gy"), P(("gx", "gy"), None))
    return jax.shard_map(
        on_device, mesh=mesh, in_specs=in_specs, out_specs=out_specs, check_vma=False
    )
```

profile of v0, /device:TPU:0, one launch (start us, length us, event | category | flops | bytes accessed | tf_op | source)
XLA Modules:
  0.0 562.9 jit_solution(12949528974472472849)
XLA Ops:
  13.4 2.9 collective-permute-start.1
  23.6 8.4 %collective-permute-done = s32[8,1,512]{2,1,0:T(1,128)S(1)} collective-permute-done((s32[8,1,512]{2,1,0:T(1,128)S(1)}, s32[8,1,512]{2,1,0:T(1,128)S(1)}, u32[]{:S(2)}, u32[]{:S(2)}) %collective-permute-start) | collective-permute-done | bytes 16416 | tf_op jit(solution)/shard_map/ppermute | solution.py:41
  32.6 3.5 collective-permute-start.6
  42.5 3.5 pad_maximum_fusion.21
  49.8 4.1 collective-permute-start.7
  63.2 4.3 constant_dynamic-update-slice_fusion.38
  84.7 6.2 %collective-permute-done.8 = f32[19,8,1,512]{3,2,1,0:T(1,128)S(1)} collective-permute-done((f32[19,8,1,512]{3,2,1,0:T(1,128)S(1)}, f32[19,8,1,512]{3,2,1,0:T(1,128)S(1)}, u32[]{:S(2)}, u32[]{:S(2)}) %collective-permute-start.8) | collective-permute-done | bytes 311328 | tf_op jit(solution)/shard_map/ppermute | solution.py:41
  91.0 3.2 collective-permute-done.9
  100.4 3.7 collective-permute-start.11
  131.3 7.0 %collective-permute-done.12 = f32[19,8,1,512]{3,2,1,0:T(1,128)S(1)} collective-permute-done((f32[19,8,1,512]{3,2,1,0:T(1,128)S(1)}, f32[19,8,1,512]{3,2,1,0:T(1,128)S(1)}, u32[]{:S(2)}, u32[]{:S(2)}) %collective-permute-start.12) | collective-permute-done | bytes 311328 | tf_op jit(solution)/shard_map/ppermute | solution.py:41
  138.2 2.9 collective-permute-done.13
  143.3 2.7 copy.83
  148.5 4.6 collective-permute-start.15
  153.9 3.0 copy.84
  156.9 3.0 copy.86
  181.6 6.6 %collective-permute-done.16 = f32[19,8,1,512]{3,2,1,0:T(1,128)S(1)} collective-permute-done((f32[19,8,1,512]{3,2,1,0:T(1,128)S(1)}, f32[19,8,1,512]{3,2,1,0:T(1,128)S(1)}, u32[]{:S(2)}, u32[]{:S(2)}) %collective-permute-start.16) | collective-permute-done | bytes 311328 | tf_op jit(solution)/shard_map/ppermute | solution.py:41
  188.2 3.2 collective-permute-done.17
  193.6 2.7 copy.87
  198.8 3.9 collective-permute-start.19
  203.5 3.0 copy.88
  206.5 3.0 copy.90
  231.2 7.0 %collective-permute-done.20 = f32[19,8,1,512]{3,2,1,0:T(1,128)S(1)} collective-permute-done((f32[19,8,1,512]{3,2,1,0:T(1,128)S(1)}, f32[19,8,1,512]{3,2,1,0:T(1,128)S(1)}, u32[]{:S(2)}, u32[]{:S(2)}) %collective-permute-start.20) | collective-permute-done | bytes 311328 | tf_op jit(solution)/shard_map/ppermute | solution.py:41
  238.1 3.4 collective-permute-done.21
  243.8 2.7 copy.91
  249.0 4.0 collective-permute-start.23
  253.8 3.0 copy.92
  256.8 3.0 copy.94
  281.5 7.0 %collective-permute-done.24 = f32[19,8,1,512]{3,2,1,0:T(1,128)S(1)} collective-permute-done((f32[19,8,1,512]{3,2,1,0:T(1,128)S(1)}, f32[19,8,1,512]{3,2,1,0:T(1,128)S(1)}, u32[]{:S(2)}, u32[]{:S(2)}) %collective-permute-start.24) | collective-permute-done | bytes 311328 | tf_op jit(solution)/shard_map/ppermute | solution.py:41
  288.5 4.2 collective-permute-done.25
  294.9 2.7 copy.95
  300.1 3.7 collective-permute-start.27
  304.6 3.0 copy.96
  307.6 3.0 copy.98
  333.0 6.3 %collective-permute-done.28 = f32[19,8,1,512]{3,2,1,0:T(1,128)S(1)} collective-permute-done((f32[19,8,1,512]{3,2,1,0:T(1,128)S(1)}, f32[19,8,1,512]{3,2,1,0:T(1,128)S(1)}, u32[]{:S(2)}, u32[]{:S(2)}) %collective-permute-start.28) | collective-permute-done | bytes 311328 | tf_op jit(solution)/shard_map/ppermute | solution.py:41
  339.2 3.2 collective-permute-done.29
  344.7 2.7 copy.99
  349.9 3.7 collective-permute-start.31
  354.4 3.0 copy.100
  357.4 3.0 copy.102
  382.1 6.7 %collective-permute-done.32 = f32[19,8,1,512]{3,2,1,0:T(1,128)S(1)} collective-permute-done((f32[19,8,1,512]{3,2,1,0:T(1,128)S(1)}, f32[19,8,1,512]{3,2,1,0:T(1,128)S(1)}, u32[]{:S(2)}, u32[]{:S(2)}) %collective-permute-start.32) | collective-permute-done | bytes 311328 | tf_op jit(solution)/shard_map/ppermute | solution.py:41
  388.8 3.2 collective-permute-done.33
  394.3 2.7 copy.103
  396.9 2.5 copy.105
  399.5 3.8 collective-permute-start.35
  404.0 3.0 copy.104
  407.0 3.1 copy.106
  416.5 4.6 fusion
  422.5 133.3 %reduce-scatter.2.cloned.1.call-done = f32[8,256]{1,0:T(8,128)} async-done(((f32[256,256]{1,0:T(8,128)}), f32[8,256]{1,0:T(8,128)}) %reduce-scatter.2.cloned.1.call-update) | async-done | bytes 8208 | tf_op jit(solution)/shard_map/reduce_scatter | solution.py:137
  (840 shorter events, 228.6 us)
Async XLA Ops:
  7.2 548.6 %reduce-scatter.2.cloned.1.call-start = ((), (), s32[]{:S(2)}) async-start(), calls=%async_computation.1 | async-start | bytes 270336 | tf_op jit(solution)/shard_map/reduce_scatter | solution.py:137
  13.4 29.1 %collective-permute-start.1 = (f32[19,8,1,512]{3,2,1,0:T(1,128)}, f32[19,8,1,512]{3,2,1,0:T(1,128)S(1)}, u32[]{:S(2)}, u32[]{:S(2)}) collective-permute-start(f32[19,8,1,512]{3,2,1,0:T(1,128)} %get-tuple-element.584), channel_id=1, source_target_pairs={{0,8},{8,16},{16,24},{24,0},{1,9},{9,17},{17,25},{25,1},{2,10},{10... | collective-permute-start | bytes 933896 | tf_op jit(solution)/shard_map/ppermute | solution.py:41
  16.3 26.2 %collective-permute-start.3 = (f32[19,8,1,512]{3,2,1,0:T(1,128)}, f32[19,8,1,512]{3,2,1,0:T(1,128)S(1)}, u32[]{:S(2)}, u32[]{:S(2)}) collective-permute-start(f32[19,8,1,512]{3,2,1,0:T(1,128)} %get-tuple-element.583), channel_id=1, source_target_pairs={{8,0},{16,8},{24,16},{0,24},{9,1},{17,9},{25,17},{1,25},{10,2},{18... | collective-permute-start | bytes 933896 | tf_op jit(solution)/shard_map/ppermute | solution.py:42
  17.3 14.7 %collective-permute-start = (s32[8,1,512]{2,1,0:T(1,128)S(1)}, s32[8,1,512]{2,1,0:T(1,128)S(1)}, u32[]{:S(2)}, u32[]{:S(2)}) collective-permute-start(s32[8,1,512]{2,1,0:T(1,128)S(1)} %get-tuple-element.602), channel_id=1, source_target_pairs={{0,8},{8,16},{16,24},{24,0},{1,9},{9,17},{17,25},{25,1},{2,10},{10... | collective-permute-start | bytes 49160 | tf_op jit(solution)/shard_map/ppermute | solution.py:41
  18.4 14.0 %collective-permute-start.2 = (s32[8,1,512]{2,1,0:T(1,128)S(1)}, s32[8,1,512]{2,1,0:T(1,128)S(1)}, u32[]{:S(2)}, u32[]{:S(2)}) collective-permute-start(s32[8,1,512]{2,1,0:T(1,128)S(1)} %get-tuple-element.601), channel_id=1, source_target_pairs={{8,0},{16,8},{24,16},{0,24},{9,1},{17,9},{25,17},{1,25},{10,2},{18... | collective-permute-start | bytes 49160 | tf_op jit(solution)/shard_map/ppermute | solution.py:42
  32.5 7.8 %collective-permute-start.4 = (s32[8,10,1]{2,1,0:T(8,128)S(1)}, s32[8,10,1]{2,1,0:T(8,128)}, u32[]{:S(2)}, u32[]{:S(2)}) collective-permute-start(s32[8,10,1]{2,1,0:T(8,128)S(1)} %get-tuple-element.596), channel_id=1, source_target_pairs={{0,1},{1,2},{2,3},{3,4},{4,5},{5,6},{6,7},{7,0},{8,9},{9,10},{10,1... | collective-permute-start | bytes 968 | tf_op jit(solution)/shard_map/ppermute | solution.py:41
  32.6 7.7 %collective-permute-start.6 = (s32[8,10,1]{2,1,0:T(8,128)S(1)}, s32[8,10,1]{2,1,0:T(8,128)}, u32[]{:S(2)}, u32[]{:S(2)}) collective-permute-start(s32[8,10,1]{2,1,0:T(8,128)S(1)} %get-tuple-element.595), channel_id=1, source_target_pairs={{1,0},{2,1},{3,2},{4,3},{5,4},{6,5},{7,6},{0,7},{9,8},{10,9},{11,1... | collective-permute-start | bytes 968 | tf_op jit(solution)/shard_map/ppermute | solution.py:42
  47.8 7.8 %collective-permute-start.5 = (f32[19,8,10,1]{0,1,3,2:T(8,128)S(1)}, f32[19,8,10,1]{0,1,3,2:T(8,128)S(1)}, u32[]{:S(2)}, u32[]{:S(2)}) collective-permute-start(f32[19,8,10,1]{0,1,3,2:T(8,128)S(1)} %copy.75), channel_id=1, source_target_pairs={{0,1},{1,2},{2,3},{3,4},{4,5},{5,6},{6,7},{7,0},{8,9},{9,10},{10,1... | collective-permute-start | bytes 18248 | tf_op jit(solution)/shard_map/ppermute | solution.py:41
  49.8 8.1 %collective-permute-start.7 = (f32[19,8,10,1]{0,1,3,2:T(8,128)S(1)}, f32[19,8,10,1]{0,1,3,2:T(8,128)S(1)}, u32[]{:S(2)}, u32[]{:S(2)}) collective-permute-start(f32[19,8,10,1]{0,1,3,2:T(8,128)S(1)} %copy.77), channel_id=1, source_target_pairs={{1,0},{2,1},{3,2},{4,3},{5,4},{6,5},{7,6},{0,7},{9,8},{10,9},{11,1... | collective-permute-start | bytes 18248 | tf_op jit(solution)/shard_map/ppermute | solution.py:42
  79.8 16.6 %copy-start.1 = (f32[19,8,8,512]{3,2,1,0:T(8,128)}, f32[19,8,8,512]{3,2,1,0:T(8,128)S(1)}, u32[]{:S(2)}) copy-start(f32[19,8,8,512]{3,2,1,0:T(8,128)S(1)} %get-tuple-element.383) | copy-start | bytes 7471108
  80.4 10.5 %collective-permute-start.8 = (f32[19,8,1,512]{3,2,1,0:T(1,128)S(1)}, f32[19,8,1,512]{3,2,1,0:T(1,128)S(1)}, u32[]{:S(2)}, u32[]{:S(2)}) collective-permute-start(f32[19,8,1,512]{3,2,1,0:T(1,128)S(1)} %get-tuple-element.581), channel_id=1, source_target_pairs={{0,8},{8,16},{16,24},{24,0},{1,9},{9,17},{17,25},{25,1},{2,10},{10... | collective-permute-start | bytes 933896 | tf_op jit(solution)/shard_map/ppermute | solution.py:41
  82.0 12.2 %collective-permute-start.9 = (f32[19,8,1,512]{3,2,1,0:T(1,128)S(1)}, f32[19,8,1,512]{3,2,1,0:T(1,128)S(1)}, u32[]{:S(2)}, u32[]{:S(2)}) collective-permute-start(f32[19,8,1,512]{3,2,1,0:T(1,128)S(1)} %get-tuple-element.580), channel_id=1, source_target_pairs={{8,0},{16,8},{24,16},{0,24},{9,1},{17,9},{25,17},{1,25},{10,2},{18... | collective-permute-start | bytes 933896 | tf_op jit(solution)/shard_map/ppermute | solution.py:42
  98.5 6.4 %collective-permute-start.10 = (f32[19,8,10,1]{0,1,3,2:T(8,128)S(1)}, f32[19,8,10,1]{0,1,3,2:T(8,128)S(1)}, u32[]{:S(2)}, u32[]{:S(2)}) collective-permute-start(f32[19,8,10,1]{0,1,3,2:T(8,128)S(1)} %copy.79), channel_id=1, source_target_pairs={{0,1},{1,2},{2,3},{3,4},{4,5},{5,6},{6,7},{7,0},{8,9},{9,10},{10,1... | collective-permute-start | bytes 18248 | tf_op jit(solution)/shard_map/ppermute | solution.py:41
  100.4 6.7 %collective-permute-start.11 = (f32[19,8,10,1]{0,1,3,2:T(8,128)S(1)}, f32[19,8,10,1]{0,1,3,2:T(8,128)S(1)}, u32[]{:S(2)}, u32[]{:S(2)}) collective-permute-start(f32[19,8,10,1]{0,1,3,2:T(8,128)S(1)} %copy.81), channel_id=1, source_target_pairs={{1,0},{2,1},{3,2},{4,3},{5,4},{6,5},{7,6},{0,7},{9,8},{10,9},{11,1... | collective-permute-start | bytes 18248 | tf_op jit(solution)/shard_map/ppermute | solution.py:42
  126.4 17.0 %copy-start.3 = (f32[19,8,8,512]{3,2,1,0:T(8,128)}, f32[19,8,8,512]{3,2,1,0:T(8,128)S(1)}, u32[]{:S(2)}) copy-start(f32[19,8,8,512]{3,2,1,0:T(8,128)S(1)} %get-tuple-element.323) | copy-start | bytes 7471108
  127.0 11.3 %collective-permute-start.12 = (f32[19,8,1,512]{3,2,1,0:T(1,128)S(1)}, f32[19,8,1,512]{3,2,1,0:T(1,128)S(1)}, u32[]{:S(2)}, u32[]{:S(2)}) collective-permute-start(f32[19,8,1,512]{3,2,1,0:T(1,128)S(1)} %get-tuple-element.578), channel_id=1, source_target_pairs={{0,8},{8,16},{16,24},{24,0},{1,9},{9,17},{17,25},{25,1},{2,10},{10... | collective-permute-start | bytes 933896 | tf_op jit(solution)/shard_map/ppermute | solution.py:41
  127.7 13.4 %collective-permute-start.13 = (f32[19,8,1,512]{3,2,1,0:T(1,128)S(1)}, f32[19,8,1,512]{3,2,1,0:T(1,128)S(1)}, u32[]{:S(2)}, u32[]{:S(2)}) collective-permute-start(f32[19,8,1,512]{3,2,1,0:T(1,128)S(1)} %get-tuple-element.577), channel_id=1, source_target_pairs={{8,0},{16,8},{24,16},{0,24},{9,1},{17,9},{25,17},{1,25},{10,2},{18... | collective-permute-start | bytes 933896 | tf_op jit(solution)/shard_map/ppermute | solution.py:42
  146.0 7.9 %collective-permute-start.14 = (f32[19,8,10,1]{0,1,3,2:T(8,128)}, f32[19,8,10,1]{0,1,3,2:T(8,128)}, u32[]{:S(2)}, u32[]{:S(2)}) collective-permute-start(f32[19,8,10,1]{0,1,3,2:T(8,128)} %copy.83), channel_id=1, source_target_pairs={{0,1},{1,2},{2,3},{3,4},{4,5},{5,6},{6,7},{7,0},{8,9},{9,10},{10,1... | collective-permute-start | bytes 18248 | tf_op jit(solution)/shard_map/ppermute | solution.py:41
  148.5 8.3 %collective-permute-start.15 = (f32[19,8,10,1]{0,1,3,2:T(8,128)}, f32[19,8,10,1]{0,1,3,2:T(8,128)}, u32[]{:S(2)}, u32[]{:S(2)}) collective-permute-start(f32[19,8,10,1]{0,1,3,2:T(8,128)} %copy.85), channel_id=1, source_target_pairs={{1,0},{2,1},{3,2},{4,3},{5,4},{6,5},{7,6},{0,7},{9,8},{10,9},{11,1... | collective-permute-start | bytes 18248 | tf_op jit(solution)/shard_map/ppermute | solution.py:42
  167.5 13.4 %copy-start.99 = (f32[8,8,512]{2,1,0:T(8,128)}, f32[8,8,512]{2,1,0:T(8,128)S(1)}, u32[]{:S(2)}) copy-start(f32[8,8,512]{2,1,0:T(8,128)S(1)} %get-tuple-element.290) | copy-start | bytes 393220
  176.7 16.9 %copy-start.5 = (f32[19,8,8,512]{3,2,1,0:T(8,128)}, f32[19,8,8,512]{3,2,1,0:T(8,128)S(1)}, u32[]{:S(2)}) copy-start(f32[19,8,8,512]{3,2,1,0:T(8,128)S(1)} %get-tuple-element.263) | copy-start | bytes 7471108
  177.3 10.9 %collective-permute-start.16 = (f32[19,8,1,512]{3,2,1,0:T(1,128)S(1)}, f32[19,8,1,512]{3,2,1,0:T(1,128)S(1)}, u32[]{:S(2)}, u32[]{:S(2)}) collective-permute-start(f32[19,8,1,512]{3,2,1,0:T(1,128)S(1)} %get-tuple-element.575), channel_id=1, source_target_pairs={{0,8},{8,16},{16,24},{24,0},{1,9},{9,17},{17,25},{25,1},{2,10},{10... | collective-permute-start | bytes 933896 | tf_op jit(solution)/shard_map/ppermute | solution.py:41
  178.8 12.5 %collective-permute-start.17 = (f32[19,8,1,512]{3,2,1,0:T(1,128)S(1)}, f32[19,8,1,512]{3,2,1,0:T(1,128)S(1)}, u32[]{:S(2)}, u32[]{:S(2)}) collective-permute-start(f32[19,8,1,512]{3,2,1,0:T(1,128)S(1)} %get-tuple-element.574), channel_id=1, source_target_pairs={{8,0},{16,8},{24,16},{0,24},{9,1},{17,9},{25,17},{1,25},{10,2},{18... | collective-permute-start | bytes 933896 | tf_op jit(solution)/shard_map/ppermute | solution.py:42
  196.3 7.2 %collective-permute-start.18 = (f32[19,8,10,1]{0,1,3,2:T(8,128)}, f32[19,8,10,1]{0,1,3,2:T(8,128)}, u32[]{:S(2)}, u32[]{:S(2)}) collective-permute-start(f32[19,8,10,1]{0,1,3,2:T(8,128)} %copy.87), channel_id=1, source_target_pairs={{0,1},{1,2},{2,3},{3,4},{4,5},{5,6},{6,7},{7,0},{8,9},{9,10},{10,1... | collective-permute-start | bytes 18248 | tf_op jit(solution)/shard_map/ppermute | solution.py:41
  198.8 7.7 %collective-permute-start.19 = (f32[19,8,10,1]{0,1,3,2:T(8,128)}, f32[19,8,10,1]{0,1,3,2:T(8,128)}, u32[]{:S(2)}, u32[]{:S(2)}) collective-permute-start(f32[19,8,10,1]{0,1,3,2:T(8,128)} %copy.89), channel_id=1, source_target_pairs={{1,0},{2,1},{3,2},{4,3},{5,4},{6,5},{7,6},{0,7},{9,8},{10,9},{11,1... | collective-permute-start | bytes 18248 | tf_op jit(solution)/shard_map/ppermute | solution.py:42
  217.1 13.4 %copy-start.101 = (f32[8,8,512]{2,1,0:T(8,128)}, f32[8,8,512]{2,1,0:T(8,128)S(1)}, u32[]{:S(2)}) copy-start(f32[8,8,512]{2,1,0:T(8,128)S(1)} %get-tuple-element.230) | copy-start | bytes 393220
  226.3 17.5 %copy-start.7 = (f32[19,8,8,512]{3,2,1,0:T(8,128)}, f32[19,8,8,512]{3,2,1,0:T(8,128)S(1)}, u32[]{:S(2)}) copy-start(f32[19,8,8,512]{3,2,1,0:T(8,128)S(1)} %get-tuple-element.203) | copy-start | bytes 7471108
  226.9 11.2 %collective-permute-start.20 = (f32[19,8,1,512]{3,2,1,0:T(1,128)S(1)}, f32[19,8,1,512]{3,2,1,0:T(1,128)S(1)}, u32[]{:S(2)}, u32[]{:S(2)}) collective-permute-start(f32[19,8,1,512]{3,2,1,0:T(1,128)S(1)} %get-tuple-element.572), channel_id=1, source_target_pairs={{0,8},{8,16},{16,24},{24,0},{1,9},{9,17},{17,25},{25,1},{2,10},{10... | collective-permute-start | bytes 933896 | tf_op jit(solution)/shard_map/ppermute | solution.py:41
  227.6 13.9 %collective-permute-start.21 = (f32[19,8,1,512]{3,2,1,0:T(1,128)S(1)}, f32[19,8,1,512]{3,2,1,0:T(1,128)S(1)}, u32[]{:S(2)}, u32[]{:S(2)}) collective-permute-start(f32[19,8,1,512]{3,2,1,0:T(1,128)S(1)} %get-tuple-element.571), channel_id=1, source_target_pairs={{8,0},{16,8},{24,16},{0,24},{9,1},{17,9},{25,17},{1,25},{10,2},{18... | collective-permute-start | bytes 933896 | tf_op jit(solution)/shard_map/ppermute | solution.py:42
  246.5 7.3 %collective-permute-start.22 = (f32[19,8,10,1]{0,1,3,2:T(8,128)}, f32[19,8,10,1]{0,1,3,2:T(8,128)}, u32[]{:S(2)}, u32[]{:S(2)}) collective-permute-start(f32[19,8,10,1]{0,1,3,2:T(8,128)} %copy.91), channel_id=1, source_target_pairs={{0,1},{1,2},{2,3},{3,4},{4,5},{5,6},{6,7},{7,0},{8,9},{9,10},{10,1... | collective-permute-start | bytes 18248 | tf_op jit(solution)/shard_map/ppermute | solution.py:41
  249.0 7.8 %collective-permute-start.23 = (f32[19,8,10,1]{0,1,3,2:T(8,128)}, f32[19,8,10,1]{0,1,3,2:T(8,128)}, u32[]{:S(2)}, u32[]{:S(2)}) collective-permute-start(f32[19,8,10,1]{0,1,3,2:T(8,128)} %copy.93), channel_id=1, source_target_pairs={{1,0},{2,1},{3,2},{4,3},{5,4},{6,5},{7,6},{0,7},{9,8},{10,9},{11,1... | collective-permute-start | bytes 18248 | tf_op jit(solution)/shard_map/ppermute | solution.py:42
  276.6 18.3 %copy-start.9 = (f32[19,8,8,512]{3,2,1,0:T(8,128)}, f32[19,8,8,512]{3,2,1,0:T(8,128)S(1)}, u32[]{:S(2)}) copy-start(f32[19,8,8,512]{3,2,1,0:T(8,128)S(1)} %get-tuple-element.143) | copy-start | bytes 7471108
  277.2 11.2 %collective-permute-start.24 = (f32[19,8,1,512]{3,2,1,0:T(1,128)S(1)}, f32[19,8,1,512]{3,2,1,0:T(1,128)S(1)}, u32[]{:S(2)}, u32[]{:S(2)}) collective-permute-start(f32[19,8,1,512]{3,2,1,0:T(1,128)S(1)} %get-tuple-element.569), channel_id=1, source_target_pairs={{0,8},{8,16},{16,24},{24,0},{1,9},{9,17},{17,25},{25,1},{2,10},{10... | collective-permute-start | bytes 933896 | tf_op jit(solution)/shard_map/ppermute | solution.py:41
  278.7 13.9 %collective-permute-start.25 = (f32[19,8,1,512]{3,2,1,0:T(1,128)S(1)}, f32[19,8,1,512]{3,2,1,0:T(1,128)S(1)}, u32[]{:S(2)}, u32[]{:S(2)}) collective-permute-start(f32[19,8,1,512]{3,2,1,0:T(1,128)S(1)} %get-tuple-element.568), channel_id=1, source_target_pairs={{8,0},{16,8},{24,16},{0,24},{9,1},{17,9},{25,17},{1,25},{10,2},{18... | collective-permute-start | bytes 933896 | tf_op jit(solution)/shard_map/ppermute | solution.py:42
  297.6 7.0 %collective-permute-start.26 = (f32[19,8,10,1]{0,1,3,2:T(8,128)}, f32[19,8,10,1]{0,1,3,2:T(8,128)}, u32[]{:S(2)}, u32[]{:S(2)}) collective-permute-start(f32[19,8,10,1]{0,1,3,2:T(8,128)} %copy.95), channel_id=1, source_target_pairs={{0,1},{1,2},{2,3},{3,4},{4,5},{5,6},{6,7},{7,0},{8,9},{9,10},{10,1... | collective-permute-start | bytes 18248 | tf_op jit(solution)/shard_map/ppermute | solution.py:41
  300.1 7.5 %collective-permute-start.27 = (f32[19,8,10,1]{0,1,3,2:T(8,128)}, f32[19,8,10,1]{0,1,3,2:T(8,128)}, u32[]{:S(2)}, u32[]{:S(2)}) collective-permute-start(f32[19,8,10,1]{0,1,3,2:T(8,128)} %copy.97), channel_id=1, source_target_pairs={{1,0},{2,1},{3,2},{4,3},{5,4},{6,5},{7,6},{0,7},{9,8},{10,9},{11,1... | collective-permute-start | bytes 18248 | tf_op jit(solution)/shard_map/ppermute | solution.py:42
  318.2 14.1 %copy-start.93 = (f32[8,8,512]{2,1,0:T(8,128)}, f32[8,8,512]{2,1,0:T(8,128)S(1)}, u32[]{:S(2)}) copy-start(f32[8,8,512]{2,1,0:T(8,128)S(1)} %get-tuple-element.110) | copy-start | bytes 393220
  327.4 17.3 %copy-start.11 = (f32[19,8,8,512]{3,2,1,0:T(8,128)}, f32[19,8,8,512]{3,2,1,0:T(8,128)S(1)}, u32[]{:S(2)}) copy-start(f32[19,8,8,512]{3,2,1,0:T(8,128)S(1)} %get-tuple-element.83) | copy-start | bytes 7471108
  328.0 11.2 %collective-permute-start.28 = (f32[19,8,1,512]{3,2,1,0:T(1,128)S(1)}, f32[19,8,1,512]{3,2,1,0:T(1,128)S(1)}, u32[]{:S(2)}, u32[]{:S(2)}) collective-permute-start(f32[19,8,1,512]{3,2,1,0:T(1,128)S(1)} %get-tuple-element.566), channel_id=1, source_target_pairs={{0,8},{8,16},{16,24},{24,0},{1,9},{9,17},{17,25},{25,1},{2,10},{10... | collective-permute-start | bytes 933896 | tf_op jit(solution)/shard_map/ppermute | solution.py:41
  328.7 13.7 %collective-permute-start.29 = (f32[19,8,1,512]{3,2,1,0:T(1,128)S(1)}, f32[19,8,1,512]{3,2,1,0:T(1,128)S(1)}, u32[]{:S(2)}, u32[]{:S(2)}) collective-permute-start(f32[19,8,1,512]{3,2,1,0:T(1,128)S(1)} %get-tuple-element.565), channel_id=1, source_target_pairs={{8,0},{16,8},{24,16},{0,24},{9,1},{17,9},{25,17},{1,25},{10,2},{18... | collective-permute-start | bytes 933896 | tf_op jit(solution)/shard_map/ppermute | solution.py:42
  347.3 7.0 %collective-permute-start.30 = (f32[19,8,10,1]{0,1,3,2:T(8,128)}, f32[19,8,10,1]{0,1,3,2:T(8,128)}, u32[]{:S(2)}, u32[]{:S(2)}) collective-permute-start(f32[19,8,10,1]{0,1,3,2:T(8,128)} %copy.99), channel_id=1, source_target_pairs={{0,1},{1,2},{2,3},{3,4},{4,5},{5,6},{6,7},{7,0},{8,9},{9,10},{10,1... | collective-permute-start | bytes 18248 | tf_op jit(solution)/shard_map/ppermute | solution.py:41
  349.9 7.5 %collective-permute-start.31 = (f32[19,8,10,1]{0,1,3,2:T(8,128)}, f32[19,8,10,1]{0,1,3,2:T(8,128)}, u32[]{:S(2)}, u32[]{:S(2)}) collective-permute-start(f32[19,8,10,1]{0,1,3,2:T(8,128)} %copy.101), channel_id=1, source_target_pairs={{1,0},{2,1},{3,2},{4,3},{5,4},{6,5},{7,6},{0,7},{9,8},{10,9},{11,1... | collective-permute-start | bytes 18248 | tf_op jit(solution)/shard_map/ppermute | solution.py:42
  368.1 13.4 %copy-start.81 = (f32[8,8,512]{2,1,0:T(8,128)}, f32[8,8,512]{2,1,0:T(8,128)S(1)}, u32[]{:S(2)}) copy-start(f32[8,8,512]{2,1,0:T(8,128)S(1)} %get-tuple-element.50) | copy-start | bytes 393220
  377.2 17.1 %copy-start.13 = (f32[19,8,8,512]{3,2,1,0:T(8,128)}, f32[19,8,8,512]{3,2,1,0:T(8,128)S(1)}, u32[]{:S(2)}) copy-start(f32[19,8,8,512]{3,2,1,0:T(8,128)S(1)} %get-tuple-element.23) | copy-start | bytes 7471108
  377.8 11.0 %collective-permute-start.32 = (f32[19,8,1,512]{3,2,1,0:T(1,128)S(1)}, f32[19,8,1,512]{3,2,1,0:T(1,128)S(1)}, u32[]{:S(2)}, u32[]{:S(2)}) collective-permute-start(f32[19,8,1,512]{3,2,1,0:T(1,128)S(1)} %get-tuple-element.562), channel_id=1, source_target_pairs={{0,8},{8,16},{16,24},{24,0},{1,9},{9,17},{17,25},{25,1},{2,10},{10... | collective-permute-start | bytes 933896 | tf_op jit(solution)/shard_map/ppermute | solution.py:41
  379.4 12.6 %collective-permute-start.33 = (f32[19,8,1,512]{3,2,1,0:T(1,128)S(1)}, f32[19,8,1,512]{3,2,1,0:T(1,128)S(1)}, u32[]{:S(2)}, u32[]{:S(2)}) collective-permute-start(f32[19,8,1,512]{3,2,1,0:T(1,128)S(1)} %get-tuple-element.563), channel_id=1, source_target_pairs={{8,0},{16,8},{24,16},{0,24},{9,1},{17,9},{25,17},{1,25},{10,2},{18... | collective-permute-start | bytes 933896 | tf_op jit(solution)/shard_map/ppermute | solution.py:42
  396.9 7.1 %collective-permute-start.34 = (f32[19,8,10,1]{0,1,3,2:T(8,128)}, f32[19,8,10,1]{0,1,3,2:T(8,128)}, u32[]{:S(2)}, u32[]{:S(2)}) collective-permute-start(f32[19,8,10,1]{0,1,3,2:T(8,128)} %copy.103), channel_id=1, source_target_pairs={{0,1},{1,2},{2,3},{3,4},{4,5},{5,6},{6,7},{7,0},{8,9},{9,10},{10,1... | collective-permute-start | bytes 18248 | tf_op jit(solution)/shard_map/ppermute | solution.py:41
  399.5 7.6 %collective-permute-start.35 = (f32[19,8,10,1]{0,1,3,2:T(8,128)}, f32[19,8,10,1]{0,1,3,2:T(8,128)}, u32[]{:S(2)}, u32[]{:S(2)}) collective-permute-start(f32[19,8,10,1]{0,1,3,2:T(8,128)} %copy.105), channel_id=1, source_target_pairs={{1,0},{2,1},{3,2},{4,3},{5,4},{6,5},{7,6},{0,7},{9,8},{10,9},{11,1... | collective-permute-start | bytes 18248 | tf_op jit(solution)/shard_map/ppermute | solution.py:42
  (266 other events, 740.8 us)
Sparse Core Ops, SparseCore 0:
  422.6 133.1 reduce-scatter.1
where the time goes:
time: 569 us; the launch traced here: 563 us
  waiting for transfers between devices  212 us (37%)
  other arithmetic  148 us (26%)
  local copies, waits for them, and re-layouts  118 us (21%)
  starting transfers between devices  62.9 us (11%)
  between operations  17.6 us (3%)
    reduce_scatter x1, waiting for transfers between devices, on_device(): lax.psum_scatter(stacked, ('gx', 'gy'), scatter_dimension=0, tiled=True)  133 us
    unnamed x144, other arithmetic  97.2 us
    ppermute x18, waiting for transfers between devices, extended(): before = lax.ppermute(last, axis, up)  55.2 us
    ppermute x18, starting transfers between devices, extended(): after = lax.ppermute(initial, axis, down)  50.2 us
    slice x16, local copies, waits for them, and re-layouts, extended(): initial = lax.slice_in_dim(shard, 0, width, axis=dim)  24.3 us
    ppermute x18, waiting for transfers between devices, extended(): after = lax.ppermute(initial, axis, down)  23.7 us
    ppermute x8, local copies, waits for them, and re-layouts, extended(): after = lax.ppermute(initial, axis, down)  22.7 us
    ppermute x8, local copies, waits for them, and re-layouts, extended(): before = lax.ppermute(last, axis, up)  22.6 us
  transfers between devices with their start and end apart: 37, of which 17 were waited for; matrix products, arithmetic and copies ran while one was open for 12% of the time, Pallas kernels for 0%

commit v1 on v0

v1 whole, which is shorter than its diff:
```python
import functools

import jax
import jax.numpy as jnp
from jax import lax
from jax.experimental import pallas as pl
from jax.experimental.pallas import tpu as pltpu
from jax.sharding import PartitionSpec as P

STEPS = 8
HALO = STEPS
LANES = 128
RELAX = 1.6

VELOCITIES = (
    (0, 0, 0),
    (1, 0, 0),
    (-1, 0, 0),
    (0, 1, 0),
    (0, -1, 0),
    (0, 0, 1),
    (0, 0, -1),
    (1, 1, 0),
    (-1, -1, 0),
    (1, -1, 0),
    (-1, 1, 0),
    (1, 0, 1),
    (-1, 0, -1),
    (1, 0, -1),
    (-1, 0, 1),
    (0, 1, 1),
    (0, -1, -1),
    (0, 1, -1),
    (0, -1, 1),
)
Q = len(VELOCITIES)
VMEM = pl.BlockSpec(memory_space=pltpu.VMEM)
SMEM = pl.BlockSpec(memory_space=pltpu.SMEM)
ANY = pl.BlockSpec(memory_space=pl.ANY)
F32 = jnp.float32


def opposite(member):
    if member == 0:
        return 0
    return member + 1 if member % 2 == 1 else member - 1


def moments(f):
    plus = [f[k] + f[k + 1] for k in range(1, Q, 2)]
    minus = [f[k] - f[k + 1] for k in range(1, Q, 2)]
    density = (
        (f[0] + (plus[0] + plus[1]))
        + ((plus[2] + plus[3]) + (plus[4] + plus[5]))
        + ((plus[6] + plus[7]) + plus[8])
    )
    m1, m3, m5, m7, m9, m11, m13, m15, m17 = minus
    jx = (m1 + (m7 + m9)) + (m11 + m13)
    jy = (m3 + (m7 - m9)) + (m15 + m17)
    jz = (m5 + (m11 - m13)) + (m15 - m17)
    return density, jx, jy, jz


def collide(f):
    density, jx, jy, jz = moments(f)
    guess = pl.reciprocal(density, approx=True)
    inv = guess * (2.0 - density * guess)
    inv = inv * (2.0 - density * inv)
    square = jx * jx + jy * jy + jz * jz
    base = RELAX * density - (1.5 * RELAX) * (square * inv)
    keep = 1.0 - RELAX
    out = [None] * Q
    out[0] = keep * f[0] + (1.0 / 3.0) * base
    for weight, members in ((1.0 / 18.0, range(1, 7, 2)), (1.0 / 36.0, range(7, Q, 2))):
        odd_scale = 3.0 * RELAX * weight
        ox, oy, oz = odd_scale * jx, odd_scale * jy, odd_scale * jz
        even_scale = (4.5 * RELAX * weight / (odd_scale * odd_scale)) * inv
        even_base = weight * base
        for k in members:
            cx, cy, cz = VELOCITIES[k]
            odd = None
            for c, o in ((cx, ox), (cy, oy), (cz, oz)):
                if c > 0:
                    odd = o if odd is None else odd + o
                elif c < 0:
                    odd = odd - o
            even = even_base + (odd * odd) * even_scale
            out[k] = keep * f[k] + (even + odd)
            out[k + 1] = keep * f[k + 1] + (even - odd)
    return out


def roll(value, shift, axis):
    size = value.shape[axis]
    if isinstance(shift, int):
        shift = shift % size
        return value if shift == 0 else pltpu.roll(value, shift, axis)
    return pltpu.roll(value, lax.rem(shift + 4 * size, size), axis)


def lane_iota():
    return lax.broadcasted_iota(jnp.int32, (8, LANES), 1)


def level_limits():
    z = lax.broadcasted_iota(jnp.int32, (8, LANES), 0)
    up = z - 1
    down = jnp.where(z == 7, -1, z + 1)
    return {0: z.astype(F32), 1: up.astype(F32), -1: down.astype(F32)}


def pulled(load, height, limits):
    here = [load(k, 0) for k in range(Q)]
    f = [here[0]] + [None] * (Q - 1)
    for cx in (-1, 0, 1):
        for cy in (-1, 0, 1):
            members = [k for k in range(1, Q) if VELOCITIES[k][0] == cx and VELOCITIES[k][1] == cy]
            if not members:
                continue
            high = height(cy, cx)
            for k in members:
                cz = VELOCITIES[k][2]
                source = here[k] if cx == 0 else load(k, cx)
                source = roll(roll(source, cz, 0), cy, 1)
                f[k] = jnp.where(limits[cz] < high, here[opposite(k)], source)
    return f


def pack_kernel(n, width, me_ref, pop_ref, solid_ref, *refs):
    blocks, (tiles, sems) = refs[:n], refs[n:]
    me = me_ref[0]
    order = [n - 1] + [m for m in range(1, n - 1)] + [0]
    copies = []
    for m in order:
        place = lax.div(jnp.bitwise_xor(me, m) * width, LANES) * LANES
        copy = pltpu.make_async_copy(
            pop_ref.at[:, :, pl.ds(pl.multiple_of(place, LANES), LANES)], tiles.at[m], sems.at[m]
        )
        copy.start()
        copies.append(copy)
    for m, copy in zip(order, copies):
        dest = jnp.bitwise_xor(me, m) * width
        place = lax.div(dest, LANES) * LANES
        turn = place - dest
        total = None
        for z in range(8):
            level = solid_ref[pl.ds(z * 8, 8), pl.ds(pl.multiple_of(place, LANES), LANES)]
            total = level if total is None else total + level
        total = total.astype(F32)
        blocks[m][Q * 8] = total if width % LANES == 0 else roll(total, turn, 1)
        copy.wait()

        def row(r, carry, m=m, turn=turn):
            f = [tiles[m, k, pl.ds(r, 8, stride=8), :] for k in range(Q)]
            out = collide(f)
            for k in range(Q):
                blocks[m][k * 8 + r] = out[k] if width % LANES == 0 else roll(out[k], turn, 1)
            return carry

        lax.fori_loop(0, 8, row, 0)


def edge_kernel(n, width, me_ref, cells_ref, *refs):
    blocks, out = refs[:n], refs[n]
    me = me_ref[0]
    lane = lane_iota()
    for e in range(n + 2):
        for k in range(Q + 2):
            if k < Q + 1 or e in (0, n + 1):
                out[e, k] = jnp.zeros((8, LANES), F32)
    sub = lax.broadcasted_iota(jnp.int32, (8, LANES), 0)
    cells = jnp.zeros((8, LANES), F32)
    for p in range(8):
        cells = jnp.where(sub == p, cells_ref[0, p].astype(F32), cells)
    for e in range(1, n + 1):
        out[e, Q + 1] = cells
    for m in range(n):
        d = jnp.bitwise_xor(me, m)

        def plane(k, carry, m=m, d=d):
            left = jnp.zeros((8, LANES), F32)
            right = jnp.zeros((8, LANES), F32)
            for r in range(8):
                if carry is None:
                    v = jnp.broadcast_to(blocks[m][Q * 8, pl.ds(r, 1), :], (8, LANES))
                else:
                    v = blocks[m][k * 8 + r]
                at = r * 2 * HALO
                left = jnp.where((lane >= at) & (lane < at + HALO), roll(v, at - (width - HALO), 1), left)
                right = jnp.where(
                    (lane >= at + HALO) & (lane < at + 2 * HALO), roll(v, at + HALO, 1), right
                )
            out[d + 2, k] += left
            out[d, k] += right
            return carry

        lax.fori_loop(0, Q, plane, 0)
        plane(Q, None)


def flow_kernel(n, width, me_ref, *refs):
    split = width + 2 * HALO > LANES
    blocks, edges = refs[:n], refs[n : 2 * n]
    fields, picks = refs[2 * n : 3 * n], refs[3 * n : 4 * n]
    state_a, state_b, high_a, high_b, mean_a, mean_b, column = refs[4 * n :]
    rows = 8 * n
    me = me_ref[0]
    lane = lane_iota()
    limits = level_limits()
    group = 4 * HALO
    tail = 3 * HALO

    def place_a(r, v, e):
        a = jnp.where(lane < HALO, roll(e, -(r * 2 * HALO), 1), roll(v, HALO, 1))
        if not split:
            behind = roll(e, width - r * 2 * HALO, 1)
            a = jnp.where(lane < width + HALO, a, behind)
        return a

    def place_b(r, b, g, v, e):
        at = g * group
        b = jnp.where((lane >= at) & (lane < at + tail), roll(v, at - (width - tail), 1), b)
        e = roll(e, at + tail - r * 2 * HALO - HALO, 1)
        return jnp.where((lane >= at + tail) & (lane < at + group), e, b)

    for r in range(8):

        def plane(k, carry, r=r):
            b = jnp.zeros((8, LANES), F32)
            for m in range(n):
                g = jnp.bitwise_xor(me, m)
                v, e = blocks[m][k * 8 + r], edges[m][k]
                state_a[0, k, g * 8 + r] = place_a(r, v, e)
                if split:
                    b = place_b(r, b, g, v, e)
            if split:
                state_b[0, k, r + 1] = b
            return carry

        lax.fori_loop(0, Q, plane, 0)
        b = jnp.zeros((8, LANES), F32)
        for m in range(n):
            g = jnp.bitwise_xor(me, m)
            v = jnp.broadcast_to(blocks[m][Q * 8, pl.ds(r, 1), :], (8, LANES))
            e = edges[m][Q]
            a = place_a(r, v, e)
            for cy in (-1, 0, 1):
                high_a[cy + 1, g * 8 + r] = roll(a, cy, 1)
            if split:
                b = place_b(r, b, g, v, e)
        if split:
            for cy in (-1, 0, 1):
                high_b[cy + 1, r + 1] = roll(b, cy, 1)

    def wrap(ref, lead):
        ref[(*lead, 0)] = roll(ref[(*lead, 8)], group, 1)
        ref[(*lead, 9)] = roll(ref[(*lead, 1)], -group, 1)

    def wrap_state(slot):
        for k in range(Q):
            if VELOCITIES[k][0] > 0:
                state_b[slot, k, 0] = roll(state_b[slot, k, 8], group, 1)
            elif VELOCITIES[k][0] < 0:
                state_b[slot, k, 9] = roll(state_b[slot, k, 1], -group, 1)

    if split:
        for c in range(3):
            wrap(high_b, (c,))
        wrap_state(0)

    def read_a(slot, x):
        before = lax.rem(x + rows - 1, rows)
        after = lax.rem(x + 1, rows)
        at = {1: before, 0: x, -1: after}
        return pulled(
            lambda k, cx: state_a[slot, k, at[cx]],
            lambda cy, cx: high_a[cy + 1, at[cx]],
            limits,
        )

    def read_b(slot, r):
        return pulled(
            lambda k, cx: state_b[slot, k, r - cx],
            lambda cy, cx: high_b[cy + 1, r - cx],
            limits,
        )

    def step(s, carry):
        slot = lax.rem(s, 2)
        then = 1 - slot

        def row_a(x, c):
            for k, v in enumerate(collide(read_a(slot, x))):
                state_a[then, k, x] = v
            return c

        lax.fori_loop(0, rows, row_a, 0)
        if split:

            def row_b(r, c):
                for k, v in enumerate(collide(read_b(slot, r))):
                    state_b[then, k, r] = v
                return c

            lax.fori_loop(1, 9, row_b, 0)
            wrap_state(then)
        return carry

    lax.fori_loop(0, STEPS - 1, step, 0)
    last = (STEPS - 1) % 2

    def last_a(x, c):
        for q, v in enumerate(moments(read_a(last, x))):
            mean_a[q, x] = v
        return c

    lax.fori_loop(0, rows, last_a, 0)
    if split:

        def last_b(r, c):
            for q, v in enumerate(moments(read_b(last, r))):
                mean_b[q, r - 1] = v
            return c

        lax.fori_loop(1, 9, last_b, 0)

    sub = lax.broadcasted_iota(jnp.int32, (8, LANES), 0)
    ids = jnp.where(lane < width, sub * (n * width) + me * width + lane, -1).astype(F32)
    for m in range(n):
        g = jnp.bitwise_xor(me, m)
        for q in range(4):

            def row(r, c, q=q, m=m, g=g):
                v = roll(mean_a[q, g * 8 + r], -HALO, 1)
                if split:
                    whole = LANES - 2 * HALO
                    b = roll(mean_b[q, r], whole - (g * group + HALO), 1)
                    v = jnp.where(lane < whole, v, b)
                fields[m][q, pl.ds(r, 8, stride=8), :] = v
                column[q, pl.ds(r, 1), :] = jnp.sum(v, axis=0, keepdims=True) * (1.0 / 8.0)
                return c

            lax.fori_loop(0, 8, row, 0)
        result = jnp.zeros((8, LANES), F32)
        for q in range(4):
            col = column[q]
            found = jnp.zeros((8, LANES), F32)
            for p in range(8):
                cell = jnp.broadcast_to(edges[m][Q + 1, pl.ds(p, 1), :], (8, LANES))
                hit = jnp.sum(jnp.where(ids == cell, col, 0.0), axis=0, keepdims=True)
                found = jnp.where(sub == p, jnp.broadcast_to(hit, (8, LANES)), found)
            value = jnp.sum(found, axis=1, keepdims=True)
            result = jnp.where(lane == q, value, result)
        picks[m][...] = result


def listen_kernel(n, count_ref, owner_ref, *refs):
    picks, weights, out, signal = refs[:n], refs[n], refs[n + 1], refs[n + 2]
    listeners, bins = signal.shape
    tiles, block = out.shape[:2]
    sub = lax.broadcasted_iota(jnp.int32, (8, LANES), 0)
    lane = lane_iota()
    total = picks[0][...]
    for m in range(1, n):
        total = total + picks[m][...]
    total = total - jnp.where(lane == 0, 1.0, 0.0)
    total = jnp.where(sub < count_ref[0], total, 0.0)
    total = total.astype(jnp.bfloat16).astype(F32)
    factors = [
        jnp.broadcast_to(total[p : p + 1, q : q + 1], (16, LANES)) for p in range(8) for q in range(4)
    ]

    def rows(i, c):
        at = pl.ds(pl.multiple_of(i * 16, 16), 16)
        for b in range(0, bins, LANES):
            acc = None
            for k in range(32):
                term = factors[k] * weights[k, at, pl.ds(b, LANES)].astype(F32)
                acc = term if acc is None else acc + term
            signal[at, pl.ds(b, LANES)] = acc
        return c

    lax.fori_loop(0, listeners // 16, rows, 0)

    def move(t, c):
        out[t] = signal[pl.ds(pl.multiple_of(owner_ref[t] * block, block), block), :]
        return c

    lax.fori_loop(0, tiles, move, 0)


def join_kernel(n, width, me_ref, *refs):
    parts, out = refs[:n], refs[n]
    me = me_ref[0]
    lane = lane_iota()
    if width == LANES:
        for m in range(n):
            place = pl.multiple_of(jnp.bitwise_xor(me, m) * width, LANES)
            out[:, :, pl.ds(place, LANES)] = parts[m][...]
        return
    for m in range(0, n, 2):
        first = jnp.bitwise_xor(me, m)
        even = lax.rem(first, 2) == 0
        place = pl.multiple_of(lax.div(first, 2) * LANES, LANES)
        for q in range(4):
            for z in range(8):
                at = pl.ds(z * 8, 8)
                x, y = parts[m][q, at, :], parts[m + 1][q, at, :]
                low, upper = jnp.where(even, x, y), jnp.where(even, y, x)
                out[q, at, pl.ds(place, LANES)] = jnp.where(lane < width, low, roll(upper, width, 1))


def shape(*dims):
    return jax.ShapeDtypeStruct(dims, F32)


def params():
    return pltpu.CompilerParams(vmem_limit_bytes=50 * 1024 * 1024)


def on_device(populations, solid, panel_cells, panel_counts, owner, retarded):
    n = lax.axis_size("gx")
    ny = lax.axis_size("gy")
    span = populations.shape[3]
    width = span // n
    me = lax.axis_index("gx").astype(jnp.int32).reshape(1)
    swap = [[(i, i ^ m) for i in range(n)] for m in range(n)]
    rows = 8 * n

    def exchange(parts):
        return [parts[0]] + [lax.ppermute(parts[m], "gx", swap[m]) for m in range(1, n)]

    blocks = pl.pallas_call(
        functools.partial(pack_kernel, n, width),
        out_shape=[shape(Q * 8 + 1, 8, LANES)] * n,
        in_specs=[SMEM, ANY, VMEM],
        out_specs=[VMEM] * n,
        scratch_shapes=[pltpu.VMEM((n, Q, 64, LANES), F32), pltpu.SemaphoreType.DMA((n,))],
        compiler_params=params(),
        name="pack",
    )(me, populations.reshape(Q, 64, span), solid.reshape(64, span))
    strips = pl.pallas_call(
        functools.partial(edge_kernel, n, width),
        out_shape=shape(n + 2, Q + 2, 8, LANES),
        in_specs=[SMEM, SMEM] + [VMEM] * n,
        out_specs=VMEM,
        compiler_params=params(),
        name="edges",
    )(me, panel_cells, *blocks)
    up = [(j, (j + 1) % ny) for j in range(ny)]
    down = [(j, i) for i, j in up]
    before = lax.ppermute(strips[n + 1], "gy", up)
    after = lax.ppermute(strips[0], "gy", down)
    received = exchange(blocks)
    edges = []
    for m in range(n):
        dest = jnp.bitwise_xor(me[0], m)
        own = lax.dynamic_index_in_dim(strips, dest + 1, 0, keepdims=False)
        own = own + jnp.where(dest == 0, before, 0.0) + jnp.where(dest == n - 1, after, 0.0)
        edges.append(own)
    edges = exchange(edges)

    results = pl.pallas_call(
        functools.partial(flow_kernel, n, width),
        out_shape=[shape(4, 64, LANES)] * n + [shape(8, LANES)] * n,
        in_specs=[SMEM] + [VMEM] * (2 * n),
        out_specs=[VMEM] * (2 * n),
        scratch_shapes=[
            pltpu.VMEM((2, Q, rows, 8, LANES), F32),
            pltpu.VMEM((2, Q, 10, 8, LANES), F32),
            pltpu.VMEM((3, rows, 8, LANES), F32),
            pltpu.VMEM((3, 10, 8, LANES), F32),
            pltpu.VMEM((4, rows, 8, LANES), F32),
            pltpu.VMEM((4, 8, 8, LANES), F32),
            pltpu.VMEM((4, 8, LANES), F32),
        ],
        compiler_params=params(),
        name="flow",
    )(me, *received, *edges)
    picks = exchange(results[n:])
    parts = exchange(results[:n])

    listeners, bins = retarded.shape[3:]
    tiles = n * ny
    partial_signal = pl.pallas_call(
        functools.partial(listen_kernel, n),
        out_shape=shape(tiles, listeners // tiles, bins),
        in_specs=[SMEM, SMEM] + [VMEM] * (n + 1),
        out_specs=VMEM,
        scratch_shapes=[pltpu.VMEM((listeners, bins), F32)],
        compiler_params=params(),
        name="listen",
    )(panel_counts, owner, *picks, retarded.reshape(32, listeners, bins))
    gathered = lax.all_to_all(partial_signal, ("gx", "gy"), 0, 0, tiled=True)
    owned_signal = jnp.sum(gathered, axis=0)

    fields = pl.pallas_call(
        functools.partial(join_kernel, n, width),
        out_shape=shape(4, 64, span),
        in_specs=[SMEM] + [VMEM] * n,
        out_specs=VMEM,
        compiler_params=params(),
        name="join",
    )(me, *parts)
    return fields.reshape(4, 8, 8, span), owned_signal


def solution(mesh):
    in_specs = (
        P(None, None, "gx", "gy"),
        P(None, "gx", "gy"),
        P(("gx", "gy"), None),
        P(("gx", "gy")),
        P(),
        P(("gx", "gy"), None, None, None, None),
    )
    out_specs = (P(None, None, "gx", "gy"), P(("gx", "gy"), None))
    return jax.shard_map(
        on_device, mesh=mesh, in_specs=in_specs, out_specs=out_specs, check_vma=False
    )
```

time: 569 us -> 134 us (0.24); the launches traced: 563 us -> 134 us
  waiting for transfers between devices: 212 us -> 27.5 us
  other arithmetic: 148 us -> 0.69 us
  local copies, waits for them, and re-layouts: 118 us -> 1.57 us
  Pallas kernels: 0 us -> 77.2 us
  starting transfers between devices: 62.9 us -> 25.4 us
  between operations: 17.6 us -> 1.37 us
    reduce_scatter x1 -> x0, waiting for transfers between devices: 133 us -> none  [on_device(): lax.psum_scatter(stacked, ('gx', 'gy'), scatter_dimension=0, tiled=True)]
    unnamed x144 -> x0, other arithmetic: 97.2 us -> none
    pallas_call x0 -> x5, Pallas kernels: none -> 77.2 us  [the longest x1 60.5 us: on_device(): pl.pallas_call(functools.partial(flow_kernel, n, width), out_shape=[shape...]
    slice x43 -> x0, local copies, waits for them, and re-layouts: 58.1 us -> none  [the longest x16 24.3 us: extended(): initial = lax.slice_in_dim(shard, 0, width, axis=dim)]
    ppermute x36 -> x14, waiting for transfers between devices: 78.8 us -> 27.5 us  [the longest x12 25.3 us: exchange(): lax.ppermute(parts[m], 'gx', swap[m])]
    ppermute x16 -> x0, local copies, waits for them, and re-layouts: 45.2 us -> none  [the longest x8 22.7 us: extended(): after = lax.ppermute(initial, axis, down)]
    ppermute x36 -> x14, starting transfers between devices: 62.8 us -> 21.5 us  [the longest x12 17.9 us: exchange(): lax.ppermute(parts[m], 'gx', swap[m])]
    slice x17 -> x0, other arithmetic: 20.8 us -> none  [the longest x12 12.7 us: shift_vertical(): return jnp.concatenate([border, field[:-1]], axis=0)]
  transfers between devices with their start and end apart: 37 -> 15, of which waited for: 17 -> 8; matrix products, arithmetic and copies ran while one was open for 12% -> 0% of each run, Pallas kernels for 0% -> 6%
where the time goes in v1:
time: 134 us
  Pallas kernels  77.2 us (58%)
  waiting for transfers between devices  27.5 us (21%)
  starting transfers between devices  25.4 us (19%)
  local copies, waits for them, and re-layouts  1.57 us (1%)
  between operations  1.37 us (1%)
    pallas_call x1, Pallas kernels, on_device(): pl.pallas_call(functools.partial(flow_kernel, n, width), out_shape=[shape...  60.5 us
    ppermute x12, waiting for transfers between devices, exchange(): lax.ppermute(parts[m], 'gx', swap[m])  25.3 us
    ppermute x12, starting transfers between devices, exchange(): lax.ppermute(parts[m], 'gx', swap[m])  17.9 us
    pallas_call x1, Pallas kernels, on_device(): pl.pallas_call(functools.partial(edge_kernel, n, width), out_shape=shape(...  7.45 us
    pallas_call x1, Pallas kernels, on_device(): pl.pallas_call(functools.partial(listen_kernel, n), out_shape=shape(tiles...  4.4 us
    pallas_call x1, Pallas kernels, on_device(): pl.pallas_call(functools.partial(pack_kernel, n, width), out_shape=[shape...  4.05 us
    all_to_all x1, starting transfers between devices, on_device(): gathered = lax.all_to_all(partial_signal, ('gx', 'gy'), 0, 0, tiled=True)  3.97 us
    ppermute x1, starting transfers between devices, on_device(): after = lax.ppermute(strips[0], 'gy', down)  3.53 us
  transfers between devices with their start and end apart: 15, of which 8 were waited for; matrix products, arithmetic and copies ran while one was open for 0% of the time, Pallas kernels for 6%

profile of v1, /device:TPU:0, one launch (start us, length us, event | category | flops | bytes accessed | tf_op | source)
XLA Modules:
  0.0 133.8 jit_solution(17350433662048638133)
XLA Ops:
  0.6 0.0 copy-start
  0.6 0.9 copy-done
  1.5 4.1 %pack.1 = (f32[153,8,128]{2,1,0:T(8,128)S(1)}, f32[153,8,128]{2,1,0:T(8,128)}, f32[153,8,128]{2,1,0:T(8,128)}, f32[153,8,128]{2,1,0:T(8,128)}) custom-call(s32[1]{0:T(128)} %bitcast.me_ref, f32[19,64,512]{2,1,0:T(8,128)} %bitcast.27, s32[64,512]{1,0:T(8,128)S(1)} %bitcast.25), custom_call_target="tpu_custom_call" | custom-call | tf_op jit(solution)/shard_map/pack/pallas_call | solution.py:433
  5.6 0.0 copy-start.1
  5.6 3.0 %collective-permute-start = (f32[153,8,128]{2,1,0:T(8,128)}, f32[153,8,128]{2,1,0:T(8,128)S(1)}, u32[]{:S(2)}, u32[]{:S(2)}) collective-permute-start(f32[153,8,128]{2,1,0:T(8,128)} %get-tuple-element.15.refs_1_), channel_id=1, source_target_pairs={{0,8},{8,0},{16,24},{24,16},{1,9},{9,1},{17,25},{25,17},{2,10},{10... | collective-permute-start | bytes 1880072 | tf_op jit(solution)/shard_map/ppermute | solution.py:431
  8.6 1.5 %collective-permute-start.1 = (f32[153,8,128]{2,1,0:T(8,128)}, f32[153,8,128]{2,1,0:T(8,128)S(1)}, u32[]{:S(2)}, u32[]{:S(2)}) collective-permute-start(f32[153,8,128]{2,1,0:T(8,128)} %get-tuple-element.16.refs_2_), channel_id=1, source_target_pairs={{0,16},{8,24},{16,0},{24,8},{1,17},{9,25},{17,1},{25,9},{2,18},{10... | collective-permute-start | bytes 1880072 | tf_op jit(solution)/shard_map/ppermute | solution.py:431
  10.1 0.0 collective-permute-start.2
  10.2 0.0 copy-start.2
  10.2 0.7 copy-done.2
  10.8 7.5 %edges.1 = f32[6,21,8,128]{3,2,1,0:T(8,128)S(1)} custom-call(s32[1]{0:T(128)} %bitcast.me_ref, s32[1,8]{1,0:T(1,128)S(1)} %copy-done.2, f32[153,8,128]{2,1,0:T(8,128)S(1)} %get-tuple-element.14.refs_0_, f32[153,8,128]{2,1,0:T(8,128)} %get-tuple-element.15.refs_1_, f32[153,8,128]{2,1,0:T(8,128)} %get-tuple-element.16.refs_2_, ...), custom_call_target="tpu_custom_call" | custom-call | tf_op jit(solution)/shard_map/edges/pallas_call | solution.py:442
  18.3 0.1 collective-permute-start.3
  18.4 3.5 %collective-permute-start.4 = (f32[21,8,128]{2,1,0:T(8,128)S(1)}, f32[21,8,128]{2,1,0:T(8,128)S(1)}, u32[]{:S(2)}, u32[]{:S(2)}) collective-permute-start(f32[21,8,128]{2,1,0:T(8,128)S(1)} %get-tuple-element.31), channel_id=1, source_target_pairs={{1,0},{2,1},{3,2},{4,3},{5,4},{6,5},{7,6},{0,7},{9,8},{10,9},{11,1... | collective-permute-start | bytes 258056 | tf_op jit(solution)/shard_map/ppermute | solution.py:453
  21.9 2.2 %collective-permute-done.3 = f32[21,8,128]{2,1,0:T(8,128)S(1)} collective-permute-done((f32[21,8,128]{2,1,0:T(8,128)S(1)}, f32[21,8,128]{2,1,0:T(8,128)S(1)}, u32[]{:S(2)}, u32[]{:S(2)}) %collective-permute-start.3) | collective-permute-done | bytes 86048 | tf_op jit(solution)/shard_map/ppermute | solution.py:452
  24.1 0.0 collective-permute-done.4
  24.1 0.1 fusion
  24.2 2.1 %collective-permute-start.5 = (f32[21,8,128]{2,1,0:T(8,128)S(1)}, f32[21,8,128]{2,1,0:T(8,128)S(1)}, u32[]{:S(2)}, u32[]{:S(2)}) collective-permute-start(f32[21,8,128]{2,1,0:T(8,128)S(1)} %get-tuple-element.28), channel_id=1, source_target_pairs={{0,8},{8,0},{16,24},{24,16},{1,9},{9,1},{17,25},{25,17},{2,10},{10... | collective-permute-start | bytes 258056 | tf_op jit(solution)/shard_map/ppermute | solution.py:431
  26.2 1.5 %collective-permute-start.6 = (f32[21,8,128]{2,1,0:T(8,128)S(1)}, f32[21,8,128]{2,1,0:T(8,128)S(1)}, u32[]{:S(2)}, u32[]{:S(2)}) collective-permute-start(f32[21,8,128]{2,1,0:T(8,128)S(1)} %get-tuple-element.27), channel_id=1, source_target_pairs={{0,16},{8,24},{16,0},{24,8},{1,17},{9,25},{17,1},{25,9},{2,18},{10... | collective-permute-start | bytes 258056 | tf_op jit(solution)/shard_map/ppermute | solution.py:431
  27.7 10.5 %collective-permute-done.5.refs_5_ = f32[21,8,128]{2,1,0:T(8,128)S(1)} collective-permute-done((f32[21,8,128]{2,1,0:T(8,128)S(1)}, f32[21,8,128]{2,1,0:T(8,128)S(1)}, u32[]{:S(2)}, u32[]{:S(2)}) %collective-permute-start.5) | collective-permute-done | bytes 86048 | tf_op jit(solution)/shard_map/ppermute | solution.py:431
  38.3 2.7 %collective-permute-start.7 = (f32[21,8,128]{2,1,0:T(8,128)S(1)}, f32[21,8,128]{2,1,0:T(8,128)S(1)}, u32[]{:S(2)}, u32[]{:S(2)}) collective-permute-start(f32[21,8,128]{2,1,0:T(8,128)S(1)} %get-tuple-element.26), channel_id=1, source_target_pairs={{0,24},{8,16},{16,8},{24,0},{1,25},{9,17},{17,9},{25,1},{2,26},{10... | collective-permute-start | bytes 258056 | tf_op jit(solution)/shard_map/ppermute | solution.py:431
  41.0 0.0 collective-permute-done.6.refs_6_
  41.0 2.7 %collective-permute-done.7.refs_7_ = f32[21,8,128]{2,1,0:T(8,128)S(1)} collective-permute-done((f32[21,8,128]{2,1,0:T(8,128)S(1)}, f32[21,8,128]{2,1,0:T(8,128)S(1)}, u32[]{:S(2)}, u32[]{:S(2)}) %collective-permute-start.7) | collective-permute-done | bytes 86048 | tf_op jit(solution)/shard_map/ppermute | solution.py:431
  43.6 0.0 collective-permute-done.refs_1_
  43.7 0.0 collective-permute-done.1.refs_2_
  43.7 0.0 collective-permute-done.2.refs_3_
  43.7 60.5 %flow.1 = (f32[4,64,128]{2,1,0:T(8,128)S(1)}, f32[4,64,128]{2,1,0:T(8,128)S(1)}, f32[4,64,128]{2,1,0:T(8,128)S(1)}, f32[4,64,128]{2,1,0:T(8,128)S(1)}, f32[8,128...) custom-call(s32[1]{0:T(128)} %bitcast.me_ref, ...), custom_call_target="tpu_custom_call" | custom-call | tf_op jit(solution)/shard_map/flow/pallas_call | solution.py:463
  104.1 1.8 %collective-permute-start.11 = (f32[8,128]{1,0:T(8,128)S(1)}, f32[8,128]{1,0:T(8,128)S(1)}, u32[]{:S(2)}, u32[]{:S(2)}) collective-permute-start(f32[8,128]{1,0:T(8,128)S(1)} %get-tuple-element.23), channel_id=1, source_target_pairs={{0,8},{8,0},{16,24},{24,16},{1,9},{9,1},{17,25},{25,17},{2,10},{10... | collective-permute-start | bytes 12296 | tf_op jit(solution)/shard_map/ppermute | solution.py:431
  105.9 1.5 %collective-permute-start.12 = (f32[8,128]{1,0:T(8,128)S(1)}, f32[8,128]{1,0:T(8,128)S(1)}, u32[]{:S(2)}, u32[]{:S(2)}) collective-permute-start(f32[8,128]{1,0:T(8,128)S(1)} %get-tuple-element.24), channel_id=1, source_target_pairs={{0,16},{8,24},{16,0},{24,8},{1,17},{9,25},{17,1},{25,9},{2,18},{10... | collective-permute-start | bytes 12296 | tf_op jit(solution)/shard_map/ppermute | solution.py:431
  107.4 0.2 collective-permute-start.13
  108.3 0.0 collective-permute-done.11.refs_1_
  108.3 1.2 collective-permute-done.12.refs_2_
  109.5 2.4 %collective-permute-done.13.refs_3_ = f32[8,128]{1,0:T(8,128)S(1)} collective-permute-done((f32[8,128]{1,0:T(8,128)S(1)}, f32[8,128]{1,0:T(8,128)S(1)}, u32[]{:S(2)}, u32[]{:S(2)}) %collective-permute-start.13) | collective-permute-done | bytes 4128 | tf_op jit(solution)/shard_map/ppermute | solution.py:431
  111.9 0.0 copy-done.1
  111.9 4.4 %listen.1 = f32[32,8,256]{2,1,0:T(8,128)} custom-call(s32[1]{0:T(128)S(6)} %copy.8.count_ref, s32[32]{0:T(128)S(1)} %copy-done.1, f32[8,128]{1,0:T(8,128)S(1)} %get-tuple-element.22.refs_0_, f32[8,128]{1,0:T(8,128)S(1)} %collective-permute-done.11.refs_1_, f32[8,128]{1,0:T(8,128)S(1)} %collective-permute-done.12.refs_2_, ...), custom_call_target="tpu_custom_call" | custom-call | tf_op jit(solution)/shard_map/listen/pallas_call | solution.py:485
  116.3 4.0 %all-to-all-start = ((f32[32,8,256]{2,1,0:T(8,128)}), f32[32,8,256]{2,1,0:T(8,128)S(1)}, u32[]{:S(2)}, u32[]{:S(2)}) async-start(f32[32,8,256]{2,1,0:T(8,128)} %listen.1), calls=%async_computation | async-start | bytes 524288 | tf_op jit(solution)/shard_map/all_to_all | solution.py:494
  120.3 2.7 %collective-permute-start.10 = (f32[4,64,128]{2,1,0:T(8,128)S(1)}, f32[4,64,128]{2,1,0:T(8,128)S(1)}, u32[]{:S(2)}, u32[]{:S(2)}) collective-permute-start(f32[4,64,128]{2,1,0:T(8,128)S(1)} %get-tuple-element.21), channel_id=1, source_target_pairs={{0,24},{8,16},{16,8},{24,0},{1,25},{9,17},{17,9},{25,1},{2,26},{10... | collective-permute-start | bytes 393224 | tf_op jit(solution)/shard_map/ppermute | solution.py:431
  123.0 0.6 collective-permute-start.8
  123.6 0.3 collective-permute-start.9
  123.9 5.7 %collective-permute-done.10.refs_3_ = f32[4,64,128]{2,1,0:T(8,128)S(1)} collective-permute-done((f32[4,64,128]{2,1,0:T(8,128)S(1)}, f32[4,64,128]{2,1,0:T(8,128)S(1)}, u32[]{:S(2)}, u32[]{:S(2)}) %collective-permute-start.10) | collective-permute-done | bytes 131104 | tf_op jit(solution)/shard_map/ppermute | solution.py:431
  129.6 2.4 %collective-permute-done.8.refs_1_ = f32[4,64,128]{2,1,0:T(8,128)S(1)} collective-permute-done((f32[4,64,128]{2,1,0:T(8,128)S(1)}, f32[4,64,128]{2,1,0:T(8,128)S(1)}, u32[]{:S(2)}, u32[]{:S(2)}) %collective-permute-start.8) | collective-permute-done | bytes 131104 | tf_op jit(solution)/shard_map/ppermute | solution.py:431
  132.0 0.3 collective-permute-done.9.refs_2_
  132.3 0.9 join.1
  133.1 0.0 all-to-all-done
  133.1 0.6 reduce_sum.9
  (1 shorter events, 0.0 us)
Async XLA Ops:
  0.6 0.9 copy-start
  5.6 106.3 %copy-start.1 = (s32[32]{0:T(128)S(1)}, s32[32]{0:T(128)}, u32[]{:S(2)}) copy-start(s32[32]{0:T(128)} %owner_ref.1) | copy-start | bytes 388
  5.6 38.0 %collective-permute-start = (f32[153,8,128]{2,1,0:T(8,128)}, f32[153,8,128]{2,1,0:T(8,128)S(1)}, u32[]{:S(2)}, u32[]{:S(2)}) collective-permute-start(f32[153,8,128]{2,1,0:T(8,128)} %get-tuple-element.15.refs_1_), channel_id=1, source_target_pairs={{0,8},{8,0},{16,24},{24,16},{1,9},{9,1},{17,25},{25,17},{2,10},{10... | collective-permute-start | bytes 1880072 | tf_op jit(solution)/shard_map/ppermute | solution.py:431
  8.6 35.0 %collective-permute-start.1 = (f32[153,8,128]{2,1,0:T(8,128)}, f32[153,8,128]{2,1,0:T(8,128)S(1)}, u32[]{:S(2)}, u32[]{:S(2)}) collective-permute-start(f32[153,8,128]{2,1,0:T(8,128)} %get-tuple-element.16.refs_2_), channel_id=1, source_target_pairs={{0,16},{8,24},{16,0},{24,8},{1,17},{9,25},{17,1},{25,9},{2,18},{10... | collective-permute-start | bytes 1880072 | tf_op jit(solution)/shard_map/ppermute | solution.py:431
  10.1 33.5 %collective-permute-start.2 = (f32[153,8,128]{2,1,0:T(8,128)}, f32[153,8,128]{2,1,0:T(8,128)S(1)}, u32[]{:S(2)}, u32[]{:S(2)}) collective-permute-start(f32[153,8,128]{2,1,0:T(8,128)} %get-tuple-element.17.refs_3_), channel_id=1, source_target_pairs={{0,24},{8,16},{16,8},{24,0},{1,25},{9,17},{17,9},{25,1},{2,26},{10... | collective-permute-start | bytes 1880072 | tf_op jit(solution)/shard_map/ppermute | solution.py:431
  10.2 0.7 copy-start.2
  18.3 5.8 %collective-permute-start.3 = (f32[21,8,128]{2,1,0:T(8,128)S(1)}, f32[21,8,128]{2,1,0:T(8,128)S(1)}, u32[]{:S(2)}, u32[]{:S(2)}) collective-permute-start(f32[21,8,128]{2,1,0:T(8,128)S(1)} %get-tuple-element.30), channel_id=1, source_target_pairs={{0,1},{1,2},{2,3},{3,4},{4,5},{5,6},{6,7},{7,0},{8,9},{9,10},{10,1... | collective-permute-start | bytes 258056 | tf_op jit(solution)/shard_map/ppermute | solution.py:452
  18.4 5.7 %collective-permute-start.4 = (f32[21,8,128]{2,1,0:T(8,128)S(1)}, f32[21,8,128]{2,1,0:T(8,128)S(1)}, u32[]{:S(2)}, u32[]{:S(2)}) collective-permute-start(f32[21,8,128]{2,1,0:T(8,128)S(1)} %get-tuple-element.31), channel_id=1, source_target_pairs={{1,0},{2,1},{3,2},{4,3},{5,4},{6,5},{7,6},{0,7},{9,8},{10,9},{11,1... | collective-permute-start | bytes 258056 | tf_op jit(solution)/shard_map/ppermute | solution.py:453
  24.2 14.1 %collective-permute-start.5 = (f32[21,8,128]{2,1,0:T(8,128)S(1)}, f32[21,8,128]{2,1,0:T(8,128)S(1)}, u32[]{:S(2)}, u32[]{:S(2)}) collective-permute-start(f32[21,8,128]{2,1,0:T(8,128)S(1)} %get-tuple-element.28), channel_id=1, source_target_pairs={{0,8},{8,0},{16,24},{24,16},{1,9},{9,1},{17,25},{25,17},{2,10},{10... | collective-permute-start | bytes 258056 | tf_op jit(solution)/shard_map/ppermute | solution.py:431
  26.2 14.7 %collective-permute-start.6 = (f32[21,8,128]{2,1,0:T(8,128)S(1)}, f32[21,8,128]{2,1,0:T(8,128)S(1)}, u32[]{:S(2)}, u32[]{:S(2)}) collective-permute-start(f32[21,8,128]{2,1,0:T(8,128)S(1)} %get-tuple-element.27), channel_id=1, source_target_pairs={{0,16},{8,24},{16,0},{24,8},{1,17},{9,25},{17,1},{25,9},{2,18},{10... | collective-permute-start | bytes 258056 | tf_op jit(solution)/shard_map/ppermute | solution.py:431
  38.3 5.4 %collective-permute-start.7 = (f32[21,8,128]{2,1,0:T(8,128)S(1)}, f32[21,8,128]{2,1,0:T(8,128)S(1)}, u32[]{:S(2)}, u32[]{:S(2)}) collective-permute-start(f32[21,8,128]{2,1,0:T(8,128)S(1)} %get-tuple-element.26), channel_id=1, source_target_pairs={{0,24},{8,16},{16,8},{24,0},{1,25},{9,17},{17,9},{25,1},{2,26},{10... | collective-permute-start | bytes 258056 | tf_op jit(solution)/shard_map/ppermute | solution.py:431
  104.1 4.2 %collective-permute-start.11 = (f32[8,128]{1,0:T(8,128)S(1)}, f32[8,128]{1,0:T(8,128)S(1)}, u32[]{:S(2)}, u32[]{:S(2)}) collective-permute-start(f32[8,128]{1,0:T(8,128)S(1)} %get-tuple-element.23), channel_id=1, source_target_pairs={{0,8},{8,0},{16,24},{24,16},{1,9},{9,1},{17,25},{25,17},{2,10},{10... | collective-permute-start | bytes 12296 | tf_op jit(solution)/shard_map/ppermute | solution.py:431
  105.9 3.6 %collective-permute-start.12 = (f32[8,128]{1,0:T(8,128)S(1)}, f32[8,128]{1,0:T(8,128)S(1)}, u32[]{:S(2)}, u32[]{:S(2)}) collective-permute-start(f32[8,128]{1,0:T(8,128)S(1)} %get-tuple-element.24), channel_id=1, source_target_pairs={{0,16},{8,24},{16,0},{24,8},{1,17},{9,25},{17,1},{25,9},{2,18},{10... | collective-permute-start | bytes 12296 | tf_op jit(solution)/shard_map/ppermute | solution.py:431
  107.4 4.5 %collective-permute-start.13 = (f32[8,128]{1,0:T(8,128)S(1)}, f32[8,128]{1,0:T(8,128)S(1)}, u32[]{:S(2)}, u32[]{:S(2)}) collective-permute-start(f32[8,128]{1,0:T(8,128)S(1)} %get-tuple-element.25), channel_id=1, source_target_pairs={{0,24},{8,16},{16,8},{24,0},{1,25},{9,17},{17,9},{25,1},{2,26},{10... | collective-permute-start | bytes 12296 | tf_op jit(solution)/shard_map/ppermute | solution.py:431
  116.3 16.8 %all-to-all-start = ((f32[32,8,256]{2,1,0:T(8,128)}), f32[32,8,256]{2,1,0:T(8,128)S(1)}, u32[]{:S(2)}, u32[]{:S(2)}) async-start(f32[32,8,256]{2,1,0:T(8,128)} %listen.1), calls=%async_computation | async-start | bytes 524288 | tf_op jit(solution)/shard_map/all_to_all | solution.py:494
  120.3 9.3 %collective-permute-start.10 = (f32[4,64,128]{2,1,0:T(8,128)S(1)}, f32[4,64,128]{2,1,0:T(8,128)S(1)}, u32[]{:S(2)}, u32[]{:S(2)}) collective-permute-start(f32[4,64,128]{2,1,0:T(8,128)S(1)} %get-tuple-element.21), channel_id=1, source_target_pairs={{0,24},{8,16},{16,8},{24,0},{1,25},{9,17},{17,9},{25,1},{2,26},{10... | collective-permute-start | bytes 393224 | tf_op jit(solution)/shard_map/ppermute | solution.py:431
  123.0 9.0 %collective-permute-start.8 = (f32[4,64,128]{2,1,0:T(8,128)S(1)}, f32[4,64,128]{2,1,0:T(8,128)S(1)}, u32[]{:S(2)}, u32[]{:S(2)}) collective-permute-start(f32[4,64,128]{2,1,0:T(8,128)S(1)} %get-tuple-element.19), channel_id=1, source_target_pairs={{0,8},{8,0},{16,24},{24,16},{1,9},{9,1},{17,25},{25,17},{2,10},{10... | collective-permute-start | bytes 393224 | tf_op jit(solution)/shard_map/ppermute | solution.py:431
  123.6 8.7 %collective-permute-start.9 = (f32[4,64,128]{2,1,0:T(8,128)S(1)}, f32[4,64,128]{2,1,0:T(8,128)S(1)}, u32[]{:S(2)}, u32[]{:S(2)}) collective-permute-start(f32[4,64,128]{2,1,0:T(8,128)S(1)} %get-tuple-element.20), channel_id=1, source_target_pairs={{0,16},{8,24},{16,0},{24,8},{1,17},{9,25},{17,1},{25,9},{2,18},{10... | collective-permute-start | bytes 393224 | tf_op jit(solution)/shard_map/ppermute | solution.py:431

commit v2 on v1

v2 whole, which is shorter than its diff:
```python
import functools

import jax
import jax.numpy as jnp
from jax import lax
from jax.experimental import pallas as pl
from jax.experimental.pallas import tpu as pltpu
from jax.sharding import PartitionSpec as P

STEPS = 8
HALO = STEPS
LANES = 128
RELAX = 1.6
UNROLL = 4

VELOCITIES = (
    (0, 0, 0),
    (1, 0, 0),
    (-1, 0, 0),
    (0, 1, 0),
    (0, -1, 0),
    (0, 0, 1),
    (0, 0, -1),
    (1, 1, 0),
    (-1, -1, 0),
    (1, -1, 0),
    (-1, 1, 0),
    (1, 0, 1),
    (-1, 0, -1),
    (1, 0, -1),
    (-1, 0, 1),
    (0, 1, 1),
    (0, -1, -1),
    (0, 1, -1),
    (0, -1, 1),
)
Q = len(VELOCITIES)
VMEM = pl.BlockSpec(memory_space=pltpu.VMEM)
SMEM = pl.BlockSpec(memory_space=pltpu.SMEM)
ANY = pl.BlockSpec(memory_space=pl.ANY)
F32 = jnp.float32


def opposite(member):
    if member == 0:
        return 0
    return member + 1 if member % 2 == 1 else member - 1


def moments(f):
    plus = [f[k] + f[k + 1] for k in range(1, Q, 2)]
    minus = [f[k] - f[k + 1] for k in range(1, Q, 2)]
    density = (
        (f[0] + (plus[0] + plus[1]))
        + ((plus[2] + plus[3]) + (plus[4] + plus[5]))
        + ((plus[6] + plus[7]) + plus[8])
    )
    m1, m3, m5, m7, m9, m11, m13, m15, m17 = minus
    jx = (m1 + (m7 + m9)) + (m11 + m13)
    jy = (m3 + (m7 - m9)) + (m15 + m17)
    jz = (m5 + (m11 - m13)) + (m15 - m17)
    return density, jx, jy, jz


def collide(f):
    density, jx, jy, jz = moments(f)
    guess = pl.reciprocal(density, approx=True)
    inv = guess * (2.0 - density * guess)
    inv = inv * (2.0 - density * inv)
    square = jx * jx + jy * jy + jz * jz
    base = RELAX * density - (1.5 * RELAX) * (square * inv)
    keep = 1.0 - RELAX
    out = [None] * Q
    out[0] = keep * f[0] + (1.0 / 3.0) * base
    for weight, members in ((1.0 / 18.0, range(1, 7, 2)), (1.0 / 36.0, range(7, Q, 2))):
        odd_scale = 3.0 * RELAX * weight
        ox, oy, oz = odd_scale * jx, odd_scale * jy, odd_scale * jz
        even_scale = (4.5 * RELAX * weight / (odd_scale * odd_scale)) * inv
        even_base = weight * base
        for k in members:
            cx, cy, cz = VELOCITIES[k]
            odd = None
            for c, o in ((cx, ox), (cy, oy), (cz, oz)):
                if c > 0:
                    odd = o if odd is None else odd + o
                elif c < 0:
                    odd = odd - o
            even = even_base + (odd * odd) * even_scale
            out[k] = keep * f[k] + (even + odd)
            out[k + 1] = keep * f[k + 1] + (even - odd)
    return out


def roll(value, shift, axis):
    size = value.shape[axis]
    if isinstance(shift, int):
        shift = shift % size
        return value if shift == 0 else pltpu.roll(value, shift, axis)
    return pltpu.roll(value, lax.rem(shift + 4 * size, size), axis)


def lane_iota():
    return lax.broadcasted_iota(jnp.int32, (8, LANES), 1)


def level_limits():
    z = lax.broadcasted_iota(jnp.int32, (8, LANES), 0)
    up = z - 1
    down = jnp.where(z == 7, -1, z + 1)
    return {0: z.astype(F32), 1: up.astype(F32), -1: down.astype(F32)}


def pulled(here_at, load, height, limits):
    here = [here_at(k) for k in range(Q)]
    f = [here[0]] + [None] * (Q - 1)
    for cx in (-1, 0, 1):
        for cy in (-1, 0, 1):
            members = [k for k in range(1, Q) if VELOCITIES[k][0] == cx and VELOCITIES[k][1] == cy]
            if not members:
                continue
            high = height(cy, cx)
            for k in members:
                cz = VELOCITIES[k][2]
                source = here[k] if cx == 0 and cy == 0 else load(k, cx)
                f[k] = jnp.where(limits[cz] < high, here[opposite(k)], roll(source, cz, 0))
    return f

SHIFTED = tuple(k for k in range(Q) if VELOCITIES[k][1] != 0)


def pack_kernel(n, width, members, me_ref, pop_ref, solid_ref, *refs):
    count = len(members)
    blocks, (tiles, sems) = refs[:count], refs[count:]
    me = me_ref[0]
    aligned = width % LANES == 0
    copies = []
    for at, m in enumerate(members):
        place = lax.div(jnp.bitwise_xor(me, m) * width, LANES) * LANES
        copy = pltpu.make_async_copy(
            pop_ref.at[:, :, pl.ds(pl.multiple_of(place, LANES), LANES)], tiles.at[at], sems.at[at]
        )
        copy.start()
        copies.append(copy)
    for at, m in enumerate(members):
        dest = jnp.bitwise_xor(me, m) * width
        place = lax.div(dest, LANES) * LANES
        turn = HALO if aligned else place - dest + HALO
        total = None
        for z in range(8):
            level = solid_ref[pl.ds(z * 8, 8), pl.ds(pl.multiple_of(place, LANES), LANES)]
            total = level if total is None else total + level
        blocks[at][Q * 8] = roll(total.astype(F32), turn, 1)
        copies[at].wait()

        def row(r, carry, at=at, turn=turn):
            f = [tiles[at, k, pl.ds(r, 8, stride=8), :] for k in range(Q)]
            out = collide(f)
            for k in range(Q):
                blocks[at][k * 8 + r] = roll(out[k], turn, 1)
            return carry

        lax.fori_loop(0, 8, row, 0, unroll=4)


def edge_kernel(n, width, me_ref, cells_ref, *refs):
    blocks, out, ends = refs[:n], refs[n], refs[n + 1]
    me = me_ref[0]
    lane = lane_iota()
    pair = 2 * HALO
    first = lax.rem(lane, pair) < HALO
    sub = lax.broadcasted_iota(jnp.int32, (8, LANES), 0)
    for m in range(n):
        d = jnp.bitwise_xor(me, m)

        def gather(values):
            c = None
            for r, v in enumerate(values):
                if width != LANES:
                    v = jnp.where(lane < HALO, roll(v, -width, 1), v)
                v = roll(v, r * pair, 1)
                c = v if c is None else jnp.where(lane >= r * pair, v, c)
            return c

        def plane(k, carry, m=m, d=d):
            ends[d + 1, k] = gather([blocks[m][k * 8 + r] for r in range(8)])
            return carry

        lax.fori_loop(0, Q - 1, plane, 0, unroll=3)
        plane(Q - 1, 0)
        heights = [jnp.broadcast_to(blocks[m][Q * 8, pl.ds(r, 1), :], (8, LANES)) for r in range(8)]
        ends[d + 1, Q] = gather(heights)
    zero = jnp.zeros((8, LANES), F32)
    cells = zero
    for p in range(8):
        cells = jnp.where(sub == p, cells_ref[0, p].astype(F32), cells)
    for e in range(n + 2):
        for k in range(Q + 1):
            left = ends[e - 1, k] if e >= 2 else zero
            right = ends[e + 1, k] if e < n else zero
            out[e, k] = jnp.where(first, left, right)
        out[e, Q + 1] = cells if 1 <= e <= n else zero


def spread_kernel(n, me_ref, *refs):
    edges, out = refs[:n], refs[n]
    me = me_ref[0]
    for m in range(n):
        g = jnp.bitwise_xor(me, m)

        def plane(k, carry, m=m, g=g):
            e = edges[m][k]
            for r in range(8):
                out[k, g * 8 + r] = roll(e, -(r * 2 * HALO), 1)
            return carry

        lax.fori_loop(0, Q + 1, plane, 0, unroll=2)


def flow_kernel(n, width, me_ref, *refs):
    split = width + 2 * HALO > LANES
    blocks, edges, spread = refs[:n], refs[n : 2 * n], refs[2 * n]
    refs = refs[2 * n + 1 :]
    fields, picks = refs[:n], refs[n : 2 * n]
    scratch = refs[2 * n :]
    plain_a, turned_a, plain_b, turned_b = scratch[0:2], scratch[2:4], scratch[4:6], scratch[6:8]
    high_a, high_b, mean_a, mean_b, column = scratch[8:]
    rows = 8 * n
    me = me_ref[0]
    lane = lane_iota()
    sub = lax.broadcasted_iota(jnp.int32, (8, LANES), 0)
    limits = level_limits()
    group = 4 * HALO
    slot_of = {k: at for at, k in enumerate(SHIFTED)}

    def place_a(v, s):
        if split:
            return jnp.where(lane < HALO, s, v)
        behind = roll(s, width, 1)
        return jnp.where(lane < HALO, s, jnp.where(lane < width + HALO, v, behind))

    def place_b(values, strips):
        b = None
        for m in range(n):
            g = jnp.bitwise_xor(me, m)
            joined = jnp.where((lane >= HALO) & (lane < 2 * HALO), strips[m], values[m])
            joined = roll(joined, g * group - (LANES - 2 * HALO), 1)
            b = joined if b is None else jnp.where((lane >= g * group) & (lane < (g + 1) * group), joined, b)
        return b

    def fill(k, r, turn):
        values = [blocks[m][k * 8 + r] for m in range(n)]
        strips = [spread[k, jnp.bitwise_xor(me, m) * 8 + r] for m in range(n)]
        for m in range(n):
            x = jnp.bitwise_xor(me, m) * 8 + r
            a = place_a(values[m], strips[m])
            plain_a[0][k, x] = a
            if turn is not None:
                turned_a[0][turn[0], x] = roll(a, turn[1], 1)
        if split:
            b = place_b(values, strips)
            plain_b[0][k, r + 1] = b
            if turn is not None:
                turned_b[0][turn[0], r + 1] = roll(b, turn[1], 1)

    for k in range(Q):
        cy = VELOCITIES[k][1]
        turn = None if cy == 0 else (slot_of[k], cy)

        def fill_row(r, c, k=k, turn=turn):
            fill(k, r, turn)
            return c

        lax.fori_loop(0, 8, fill_row, 0, unroll=4)
    for r in range(8):
        values = [jnp.broadcast_to(blocks[m][Q * 8, pl.ds(r, 1), :], (8, LANES)) for m in range(n)]
        strips = [spread[Q, jnp.bitwise_xor(me, m) * 8 + r] for m in range(n)]
        for m in range(n):
            a = place_a(values[m], strips[m])
            for cy in (-1, 0, 1):
                high_a[cy + 1, jnp.bitwise_xor(me, m) * 8 + r] = roll(a, cy, 1)
        if split:
            b = place_b(values, strips)
            for cy in (-1, 0, 1):
                high_b[cy + 1, r + 1] = roll(b, cy, 1)

    def wrap(slot):
        for k in range(Q):
            cx, cy, _ = VELOCITIES[k]
            if cx == 0:
                continue
            ref, at = (plain_b[slot], k) if cy == 0 else (turned_b[slot], slot_of[k])
            if cx > 0:
                ref[at, 0] = roll(ref[at, 8], group, 1)
            else:
                ref[at, 9] = roll(ref[at, 1], -group, 1)

    if split:
        for c in range(3):
            high_b[c, 0] = roll(high_b[c, 8], group, 1)
            high_b[c, 9] = roll(high_b[c, 1], -group, 1)
        wrap(0)

    def load_from(plain, turned, at):
        def load(k, cx):
            if VELOCITIES[k][1] == 0:
                return plain[k, at[cx]]
            return turned[slot_of[k], at[cx]]

        return load

    def read(plain, turned, high, at):
        return pulled(
            lambda k: plain[k, at[0]],
            load_from(plain, turned, at),
            lambda cy, cx: high[cy + 1, at[cx]],
            limits,
        )

    def around_a(x):
        return {1: lax.rem(x + rows - 1, rows), 0: x, -1: lax.rem(x + 1, rows)}

    def around_b(r):
        return {1: r - 1, 0: r, -1: r + 1}

    def store(plain, turned, x, out):
        for k in range(Q):
            plain[k, x] = out[k]
        for at, k in enumerate(SHIFTED):
            turned[at, x] = roll(out[k], VELOCITIES[k][1], 1)

    def step(slot):
        then = 1 - slot

        def row_a(x, c):
            out = collide(read(plain_a[slot], turned_a[slot], high_a, around_a(x)))
            store(plain_a[then], turned_a[then], x, out)
            return c

        lax.fori_loop(0, rows, row_a, 0, unroll=UNROLL)
        if split:

            def row_b(r, c):
                out = collide(read(plain_b[slot], turned_b[slot], high_b, around_b(r)))
                store(plain_b[then], turned_b[then], r, out)
                return c

            lax.fori_loop(1, 9, row_b, 0, unroll=UNROLL)
            wrap(then)

    def twice(s, c):
        step(0)
        step(1)
        return c

    lax.fori_loop(0, (STEPS - 1) // 2, twice, 0)
    if (STEPS - 1) % 2:
        step(0)
    last = (STEPS - 1) % 2

    def last_a(x, c):
        f = read(plain_a[last], turned_a[last], high_a, around_a(x))
        for q, v in enumerate(moments(f)):
            mean_a[q, x] = roll(v, -HALO, 1)
        return c

    lax.fori_loop(0, rows, last_a, 0, unroll=UNROLL)
    if split:

        def last_b(r, c):
            f = read(plain_b[last], turned_b[last], high_b, around_b(r))
            for q, v in enumerate(moments(f)):
                mean_b[q, r - 1] = v
            return c

        lax.fori_loop(1, 9, last_b, 0, unroll=UNROLL)

    ids = jnp.where(lane < width, sub * (n * width) + me * width + lane, -1).astype(F32)
    whole = LANES - 2 * HALO
    for m in range(n):
        g = jnp.bitwise_xor(me, m)
        for q in range(4):
            for r in range(8):
                v = mean_a[q, g * 8 + r]
                if split:
                    v = jnp.where(lane < whole, v, roll(mean_b[q, r], whole - (g * group + HALO), 1))
                fields[m][q, pl.ds(r, 8, stride=8), :] = v
                column[m, q, pl.ds(r, 1), :] = jnp.sum(v, axis=0, keepdims=True) * (1.0 / 8.0)
    for m in range(n):
        found = [None] * 4
        for p in range(8):
            hit = ids == jnp.broadcast_to(edges[m][Q + 1, pl.ds(p, 1), :], (8, LANES))
            for q in range(4):
                value = jnp.sum(jnp.where(hit, column[m, q], 0.0), axis=0, keepdims=True)
                value = jnp.broadcast_to(value, (8, LANES))
                found[q] = value if p == 0 else jnp.where(sub == p, value, found[q])
        result = jnp.zeros((8, LANES), F32)
        for q in range(4):
            result = jnp.where(lane == q, jnp.sum(found[q], axis=1, keepdims=True), result)
        picks[m][...] = result


def flow_scratch(n):
    rows = 8 * n
    few = len(SHIFTED)
    sizes = (
        [(Q, rows, 8, LANES)] * 2
        + [(few, rows, 8, LANES)] * 2
        + [(Q, 10, 8, LANES)] * 2
        + [(few, 10, 8, LANES)] * 2
        + [(3, rows, 8, LANES), (3, 10, 8, LANES), (4, rows, 8, LANES), (4, 8, 8, LANES), (n, 4, 8, LANES)]
    )
    return [pltpu.VMEM(size, F32) for size in sizes]


def listen_kernel(n, count_ref, owner_ref, *refs):
    picks, weights, out, signal = refs[:n], refs[n], refs[n + 1], refs[n + 2]
    listeners, bins = signal.shape
    tiles, block = out.shape[:2]
    sub = lax.broadcasted_iota(jnp.int32, (8, LANES), 0)
    lane = lane_iota()
    total = picks[0][...]
    for m in range(1, n):
        total = total + picks[m][...]
    total = total - jnp.where(lane == 0, 1.0, 0.0)
    total = jnp.where(sub < count_ref[0], total, 0.0)
    total = total.astype(jnp.bfloat16).astype(F32)
    factors = [
        jnp.broadcast_to(total[p : p + 1, q : q + 1], (16, LANES)) for p in range(8) for q in range(4)
    ]

    def rows(i, c):
        at = pl.ds(pl.multiple_of(i * 16, 16), 16)
        for b in range(0, bins, LANES):
            sums = []
            for start in range(0, 32, 8):
                acc = None
                for k in range(start, start + 8):
                    term = factors[k] * weights[k, at, pl.ds(b, LANES)].astype(F32)
                    acc = term if acc is None else acc + term
                sums.append(acc)
            signal[at, pl.ds(b, LANES)] = (sums[0] + sums[1]) + (sums[2] + sums[3])
        return c

    lax.fori_loop(0, listeners // 16, rows, 0)

    def move(t, c):
        out[t] = signal[pl.ds(pl.multiple_of(owner_ref[t] * block, block), block), :]
        return c

    lax.fori_loop(0, tiles, move, 0, unroll=4)


def join_kernel(n, width, me_ref, *refs):
    parts, out = refs[:n], refs[n]
    me = me_ref[0]
    lane = lane_iota()
    if width == LANES:
        for m in range(n):
            place = pl.multiple_of(jnp.bitwise_xor(me, m) * width, LANES)
            out[:, :, pl.ds(place, LANES)] = parts[m][...]
        return
    for m in range(0, n, 2):
        first = jnp.bitwise_xor(me, m)
        even = lax.rem(first, 2) == 0
        place = pl.multiple_of(lax.div(first, 2) * LANES, LANES)
        for q in range(4):
            for z in range(8):
                at = pl.ds(z * 8, 8)
                x, y = parts[m][q, at, :], parts[m + 1][q, at, :]
                low, upper = jnp.where(even, x, y), jnp.where(even, y, x)
                out[q, at, pl.ds(place, LANES)] = jnp.where(lane < width, low, roll(upper, width, 1))


def shape(*dims):
    return jax.ShapeDtypeStruct(dims, F32)


def params():
    return pltpu.CompilerParams(vmem_limit_bytes=50 * 1024 * 1024)


def on_device(populations, solid, panel_cells, panel_counts, owner, retarded):
    n = lax.axis_size("gx")
    ny = lax.axis_size("gy")
    span = populations.shape[3]
    width = span // n
    me = lax.axis_index("gx").astype(jnp.int32).reshape(1)
    swap = [[(i, i ^ m) for i in range(n)] for m in range(n)]
    rows = 8 * n

    def exchange(parts):
        return [parts[0]] + [lax.ppermute(parts[m], "gx", swap[m]) for m in range(1, n)]

    def pack(members, name):
        return pl.pallas_call(
            functools.partial(pack_kernel, n, width, members),
            out_shape=[shape(Q * 8 + 1, 8, LANES)] * len(members),
            in_specs=[SMEM, ANY, VMEM],
            out_specs=[VMEM] * len(members),
            scratch_shapes=[
                pltpu.VMEM((len(members), Q, 64, LANES), F32),
                pltpu.SemaphoreType.DMA((len(members),)),
            ],
            compiler_params=params(),
            name=name,
        )(me, populations.reshape(Q, 64, span), solid.reshape(64, span))

    sent = pack(tuple(range(1, n)), "pack")
    blocks = list(pack((0,), "pack_own")) + list(sent)
    strips = pl.pallas_call(
        functools.partial(edge_kernel, n, width),
        out_shape=shape(n + 2, Q + 2, 8, LANES),
        in_specs=[SMEM, SMEM] + [VMEM] * n,
        out_specs=VMEM,
        scratch_shapes=[pltpu.VMEM((n + 1, Q + 1, 8, LANES), F32)],
        compiler_params=params(),
        name="edges",
    )(me, panel_cells, *blocks)
    up = [(j, (j + 1) % ny) for j in range(ny)]
    down = [(j, i) for i, j in up]
    before = lax.ppermute(strips[n + 1], "gy", up)
    after = lax.ppermute(strips[0], "gy", down)
    received = exchange(blocks)
    edges = []
    for m in range(n):
        dest = jnp.bitwise_xor(me[0], m)
        own = lax.dynamic_index_in_dim(strips, dest + 1, 0, keepdims=False)
        own = own + jnp.where(dest == 0, before, 0.0) + jnp.where(dest == n - 1, after, 0.0)
        edges.append(own)
    edges = exchange(edges)

    spread = pl.pallas_call(
        functools.partial(spread_kernel, n),
        out_shape=shape(Q + 1, rows, 8, LANES),
        in_specs=[SMEM] + [VMEM] * n,
        out_specs=VMEM,
        compiler_params=params(),
        name="spread",
    )(me, *edges)
    results = pl.pallas_call(
        functools.partial(flow_kernel, n, width),
        out_shape=[shape(4, 64, LANES)] * n + [shape(8, LANES)] * n,
        in_specs=[SMEM] + [VMEM] * (2 * n + 1),
        out_specs=[VMEM] * (2 * n),
        scratch_shapes=flow_scratch(n),
        compiler_params=params(),
        name="flow",
    )(me, *received, *edges, spread)
    picks = exchange(results[n:])
    parts = exchange(results[:n])

    listeners, bins = retarded.shape[3:]
    tiles = n * ny
    partial_signal = pl.pallas_call(
        functools.partial(listen_kernel, n),
        out_shape=shape(tiles, listeners // tiles, bins),
        in_specs=[SMEM, SMEM] + [VMEM] * (n + 1),
        out_specs=VMEM,
        scratch_shapes=[pltpu.VMEM((listeners, bins), F32)],
        compiler_params=params(),
        name="listen",
    )(panel_counts, owner, *picks, retarded.reshape(32, listeners, bins))
    gathered = lax.all_to_all(partial_signal, ("gx", "gy"), 0, 0, tiled=True)
    owned_signal = jnp.sum(gathered, axis=0)

    fields = pl.pallas_call(
        functools.partial(join_kernel, n, width),
        out_shape=shape(4, 64, span),
        in_specs=[SMEM] + [VMEM] * n,
        out_specs=VMEM,
        compiler_params=params(),
        name="join",
    )(me, *parts)
    return fields.reshape(4, 8, 8, span), owned_signal


def solution(mesh):
    in_specs = (
        P(None, None, "gx", "gy"),
        P(None, "gx", "gy"),
        P(("gx", "gy"), None),
        P(("gx", "gy")),
        P(),
        P(("gx", "gy"), None, None, None, None),
    )
    out_specs = (P(None, None, "gx", "gy"), P(("gx", "gy"), None))
    return jax.shard_map(
        on_device, mesh=mesh, in_specs=in_specs, out_specs=out_specs, check_vma=False
    )
```

time: 134 us -> 103 us (0.77)
  Pallas kernels: 77.2 us -> 41.3 us
  waiting for transfers between devices: 27.5 us -> 32.8 us
    pallas_call x1, Pallas kernels: 60.5 us -> 25.1 us  [on_device(): pl.pallas_call(functools.partial(flow_kernel, n, width), out_shape=[shape...]
    pallas_call x1, Pallas kernels: 7.45 us -> 3.74 us  [on_device(): pl.pallas_call(functools.partial(edge_kernel, n, width), out_shape=shape(...]
    pallas_call x1 -> x3, Pallas kernels: 4.05 us -> 7.41 us  [the longest x2 4.15 us: pack(): pl.pallas_call(functools.partial(pack_kernel, n, width, members), out_sha...]
    ppermute x1, waiting for transfers between devices: 0.01 us -> 2.1 us  [on_device(): after = lax.ppermute(strips[0], 'gy', down)]
    ppermute x12, waiting for transfers between devices: 25.3 us -> 27.1 us  [exchange(): lax.ppermute(parts[m], 'gx', swap[m])]
    ppermute x1, waiting for transfers between devices: 2.2 us -> 3.61 us  [on_device(): before = lax.ppermute(strips[n + 1], 'gy', up)]
  transfers between devices with their start and end apart: 15 -> 15, of which waited for: 8 -> 9; matrix products, arithmetic and copies ran while one was open for 0% -> 0% of each run, Pallas kernels for 6% -> 8%
where the time goes in v2:
time: 103 us
  Pallas kernels  41.3 us (40%)
  waiting for transfers between devices  32.8 us (32%)
  starting transfers between devices  24.1 us (23%)
  local copies, waits for them, and re-layouts  2.57 us (2%)
  between operations  1.41 us (1%)
    ppermute x12, waiting for transfers between devices, exchange(): lax.ppermute(parts[m], 'gx', swap[m])  27.1 us
    pallas_call x1, Pallas kernels, on_device(): pl.pallas_call(functools.partial(flow_kernel, n, width), out_shape=[shape...  25.1 us
    ppermute x12, starting transfers between devices, exchange(): lax.ppermute(parts[m], 'gx', swap[m])  17.4 us
    pallas_call x2, Pallas kernels, pack(): pl.pallas_call(functools.partial(pack_kernel, n, width, members), out_sha...  4.15 us
    pallas_call x1, Pallas kernels, on_device(): pl.pallas_call(functools.partial(listen_kernel, n), out_shape=shape(tiles...  4.13 us
    all_to_all x1, starting transfers between devices, on_device(): gathered = lax.all_to_all(partial_signal, ('gx', 'gy'), 0, 0, tiled=True)  3.97 us
    pallas_call x1, Pallas kernels, on_device(): pl.pallas_call(functools.partial(edge_kernel, n, width), out_shape=shape(...  3.74 us
    ppermute x1, waiting for transfers between devices, on_device(): before = lax.ppermute(strips[n + 1], 'gy', up)  3.61 us
  transfers between devices with their start and end apart: 15, of which 9 were waited for; matrix products, arithmetic and copies ran while one was open for 0% of the time, Pallas kernels for 8%

profile of v2, /device:TPU:0, one launch (start us, length us, event | category | flops | bytes accessed | tf_op | source)
XLA Modules:
  0.0 102.8 jit_solution(15049541060962201620)
XLA Ops:
  0.6 0.0 copy-start.1
  0.6 0.0 copy-start.2
  0.7 1.0 %copy-done.2 = s32[8,8,512]{2,1,0:T(8,128)S(1)} copy-done((s32[8,8,512]{2,1,0:T(8,128)S(1)}, s32[8,8,512]{2,1,0:T(8,128)}, u32[]{:S(2)}) %copy-start.2) | copy-done | bytes 131096
  1.7 0.0 copy-start.4
  1.7 3.5 %pack.1 = (f32[153,8,128]{2,1,0:T(8,128)}, f32[153,8,128]{2,1,0:T(8,128)}, f32[153,8,128]{2,1,0:T(8,128)}) custom-call(s32[1]{0:T(128)} %bitcast.me_ref, f32[19,64,512]{2,1,0:T(8,128)} %bitcast.25, s32[64,512]{1,0:T(8,128)S(1)} %bitcast.27), custom_call_target="tpu_custom_call" | custom-call | tf_op jit(solution)/shard_map/pack/pallas_call | solution.py:495
  5.3 3.0 %collective-permute-start = (f32[153,8,128]{2,1,0:T(8,128)}, f32[153,8,128]{2,1,0:T(8,128)}, u32[]{:S(2)}, u32[]{:S(2)}) collective-permute-start(f32[153,8,128]{2,1,0:T(8,128)} %get-tuple-element.13.refs_1_), channel_id=1, source_target_pairs={{0,8},{8,0},{16,24},{24,16},{1,9},{9,1},{17,25},{25,17},{2,10},{10... | collective-permute-start | bytes 1880072 | tf_op jit(solution)/shard_map/ppermute | solution.py:492
  8.3 1.5 %collective-permute-start.1 = (f32[153,8,128]{2,1,0:T(8,128)}, f32[153,8,128]{2,1,0:T(8,128)}, u32[]{:S(2)}, u32[]{:S(2)}) collective-permute-start(f32[153,8,128]{2,1,0:T(8,128)} %get-tuple-element.14.refs_2_), channel_id=1, source_target_pairs={{0,16},{8,24},{16,0},{24,8},{1,17},{9,25},{17,1},{25,9},{2,18},{10... | collective-permute-start | bytes 1880072 | tf_op jit(solution)/shard_map/ppermute | solution.py:492
  9.8 0.0 collective-permute-start.2
  9.8 0.0 copy-done.1
  9.8 0.6 pack_own.1.refs_0_
  10.4 0.0 copy-done.4
  10.4 3.7 %edges.1 = f32[6,21,8,128]{3,2,1,0:T(8,128)S(1)} custom-call(s32[1]{0:T(128)} %bitcast.me_ref, s32[1,8]{1,0:T(1,128)S(1)} %copy-done.4, f32[153,8,128]{2,1,0:T(8,128)S(1)} %pack_own.1.refs_0_, f32[153,8,128]{2,1,0:T(8,128)} %get-tuple-element.13.refs_1_, f32[153,8,128]{2,1,0:T(8,128)} %get-tuple-element.14.refs_2_, f32[153,8,128]{2,1,0:T(8,128)} %get-tuple-element.15.refs_3_), custom_call_target="tpu_custom_call" | custom-call | tf_op jit(solution)/shard_map/edges/pallas_call | solution.py:510
  14.2 2.7 %collective-permute-start.4 = (f32[21,8,128]{2,1,0:T(8,128)S(1)}, f32[21,8,128]{2,1,0:T(8,128)S(1)}, u32[]{:S(2)}, u32[]{:S(2)}) collective-permute-start(f32[21,8,128]{2,1,0:T(8,128)S(1)} %get-tuple-element.29), channel_id=1, source_target_pairs={{1,0},{2,1},{3,2},{4,3},{5,4},{6,5},{7,6},{0,7},{9,8},{10,9},{11,1... | collective-permute-start | bytes 258056 | tf_op jit(solution)/shard_map/ppermute | solution.py:522
  16.9 0.0 collective-permute-start.3
  16.9 2.1 %collective-permute-done.4 = f32[21,8,128]{2,1,0:T(8,128)S(1)} collective-permute-done((f32[21,8,128]{2,1,0:T(8,128)S(1)}, f32[21,8,128]{2,1,0:T(8,128)S(1)}, u32[]{:S(2)}, u32[]{:S(2)}) %collective-permute-start.4) | collective-permute-done | bytes 86048 | tf_op jit(solution)/shard_map/ppermute | solution.py:522
  19.0 3.6 %collective-permute-done.3 = f32[21,8,128]{2,1,0:T(8,128)S(1)} collective-permute-done((f32[21,8,128]{2,1,0:T(8,128)S(1)}, f32[21,8,128]{2,1,0:T(8,128)S(1)}, u32[]{:S(2)}, u32[]{:S(2)}) %collective-permute-start.3) | collective-permute-done | bytes 86048 | tf_op jit(solution)/shard_map/ppermute | solution.py:521
  22.6 0.1 fusion
  22.7 1.6 %collective-permute-start.5 = (f32[21,8,128]{2,1,0:T(8,128)S(1)}, f32[21,8,128]{2,1,0:T(8,128)S(1)}, u32[]{:S(2)}, u32[]{:S(2)}) collective-permute-start(f32[21,8,128]{2,1,0:T(8,128)S(1)} %get-tuple-element.26), channel_id=1, source_target_pairs={{0,8},{8,0},{16,24},{24,16},{1,9},{9,1},{17,25},{25,17},{2,10},{10... | collective-permute-start | bytes 258056 | tf_op jit(solution)/shard_map/ppermute | solution.py:492
  24.2 1.5 %collective-permute-start.6 = (f32[21,8,128]{2,1,0:T(8,128)S(1)}, f32[21,8,128]{2,1,0:T(8,128)S(1)}, u32[]{:S(2)}, u32[]{:S(2)}) collective-permute-start(f32[21,8,128]{2,1,0:T(8,128)S(1)} %get-tuple-element.25), channel_id=1, source_target_pairs={{0,16},{8,24},{16,0},{24,8},{1,17},{9,25},{17,1},{25,9},{2,18},{10... | collective-permute-start | bytes 258056 | tf_op jit(solution)/shard_map/ppermute | solution.py:492
  25.8 12.2 %collective-permute-done.5.refs_1_.refs_5_ = f32[21,8,128]{2,1,0:T(8,128)S(1)} collective-permute-done((f32[21,8,128]{2,1,0:T(8,128)S(1)}, f32[21,8,128]{2,1,0:T(8,128)S(1)}, u32[]{:S(2)}, u32[]{:S(2)}) %collective-permute-start.5) | collective-permute-done | bytes 86048 | tf_op jit(solution)/shard_map/ppermute | solution.py:492
  37.9 2.7 %collective-permute-start.7 = (f32[21,8,128]{2,1,0:T(8,128)S(1)}, f32[21,8,128]{2,1,0:T(8,128)S(1)}, u32[]{:S(2)}, u32[]{:S(2)}) collective-permute-start(f32[21,8,128]{2,1,0:T(8,128)S(1)} %get-tuple-element.24), channel_id=1, source_target_pairs={{0,24},{8,16},{16,8},{24,0},{1,25},{9,17},{17,9},{25,1},{2,26},{10... | collective-permute-start | bytes 258056 | tf_op jit(solution)/shard_map/ppermute | solution.py:492
  40.6 0.0 collective-permute-done.6.refs_2_.refs_6_
  40.6 2.7 %collective-permute-done.7.refs_3_.refs_7_ = f32[21,8,128]{2,1,0:T(8,128)S(1)} collective-permute-done((f32[21,8,128]{2,1,0:T(8,128)S(1)}, f32[21,8,128]{2,1,0:T(8,128)S(1)}, u32[]{:S(2)}, u32[]{:S(2)}) %collective-permute-start.7) | collective-permute-done | bytes 86048 | tf_op jit(solution)/shard_map/ppermute | solution.py:492
  43.3 3.3 %spread.1.refs_8_ = f32[20,32,8,128]{3,2,1,0:T(8,128)S(1)} custom-call(s32[1]{0:T(128)} %bitcast.me_ref, f32[21,8,128]{2,1,0:T(8,128)S(1)} %get-tuple-element.27.refs_0_.refs_4_, f32[21,8,128]{2,1,0:T(8,128)S(1)} %collective-permute-done.5.refs_1_.refs_5_, f32[21,8,128]{2,1,0:T(8,128)S(1)} %collective-permute-done.6.refs_2_.refs_6_, ...), custom_call_target="tpu_custom_call" | custom-call | tf_op jit(solution)/shard_map/spread/pallas_call | solution.py:532
  46.6 0.0 copy-start
  46.6 1.5 %copy-done = f32[20,32,8,128]{3,2,1,0:T(8,128)} copy-done((f32[20,32,8,128]{3,2,1,0:T(8,128)}, f32[20,32,8,128]{3,2,1,0:T(8,128)S(1)}, u32[]{:S(2)}) %copy-start) | copy-done | bytes 2621464
  48.1 0.0 collective-permute-done.refs_1_
  48.1 0.0 collective-permute-done.1.refs_2_
  48.1 0.0 collective-permute-done.2.refs_3_
  48.1 25.1 %flow.1 = (f32[4,64,128]{2,1,0:T(8,128)S(1)}, f32[4,64,128]{2,1,0:T(8,128)S(1)}, f32[4,64,128]{2,1,0:T(8,128)S(1)}, f32[4,64,128]{2,1,0:T(8,128)S(1)}, f32[8,128...) custom-call(s32[1]{0:T(128)} %bitcast.me_ref, ...), custom_call_target="tpu_custom_call" | custom-call | tf_op jit(solution)/shard_map/flow/pallas_call | solution.py:540
  73.2 1.8 %collective-permute-start.11 = (f32[8,128]{1,0:T(8,128)S(1)}, f32[8,128]{1,0:T(8,128)S(1)}, u32[]{:S(2)}, u32[]{:S(2)}) collective-permute-start(f32[8,128]{1,0:T(8,128)S(1)} %get-tuple-element.21), channel_id=1, source_target_pairs={{0,8},{8,0},{16,24},{24,16},{1,9},{9,1},{17,25},{25,17},{2,10},{10... | collective-permute-start | bytes 12296 | tf_op jit(solution)/shard_map/ppermute | solution.py:492
  75.0 1.5 %collective-permute-start.12 = (f32[8,128]{1,0:T(8,128)S(1)}, f32[8,128]{1,0:T(8,128)S(1)}, u32[]{:S(2)}, u32[]{:S(2)}) collective-permute-start(f32[8,128]{1,0:T(8,128)S(1)} %get-tuple-element.22), channel_id=1, source_target_pairs={{0,16},{8,24},{16,0},{24,8},{1,17},{9,25},{17,1},{25,9},{2,18},{10... | collective-permute-start | bytes 12296 | tf_op jit(solution)/shard_map/ppermute | solution.py:492
  76.5 0.2 collective-permute-start.13
  77.4 0.0 collective-permute-done.11.refs_1_
  77.4 1.2 %collective-permute-done.12.refs_2_ = f32[8,128]{1,0:T(8,128)S(1)} collective-permute-done((f32[8,128]{1,0:T(8,128)S(1)}, f32[8,128]{1,0:T(8,128)S(1)}, u32[]{:S(2)}, u32[]{:S(2)}) %collective-permute-start.12) | collective-permute-done | bytes 4128 | tf_op jit(solution)/shard_map/ppermute | solution.py:492
  78.6 2.4 %collective-permute-done.13.refs_3_ = f32[8,128]{1,0:T(8,128)S(1)} collective-permute-done((f32[8,128]{1,0:T(8,128)S(1)}, f32[8,128]{1,0:T(8,128)S(1)}, u32[]{:S(2)}, u32[]{:S(2)}) %collective-permute-start.13) | collective-permute-done | bytes 4128 | tf_op jit(solution)/shard_map/ppermute | solution.py:492
  81.0 0.0 copy-done.3
  81.0 4.1 %listen.1 = f32[32,8,256]{2,1,0:T(8,128)} custom-call(s32[1]{0:T(128)S(6)} %copy.8.count_ref, s32[32]{0:T(128)S(1)} %copy-done.3, f32[8,128]{1,0:T(8,128)S(1)} %get-tuple-element.20.refs_0_, f32[8,128]{1,0:T(8,128)S(1)} %collective-permute-done.11.refs_1_, f32[8,128]{1,0:T(8,128)S(1)} %collective-permute-done.12.refs_2_, ...), custom_call_target="tpu_custom_call" | custom-call | tf_op jit(solution)/shard_map/listen/pallas_call | solution.py:554
  85.1 4.0 %all-to-all-start = ((f32[32,8,256]{2,1,0:T(8,128)}), f32[32,8,256]{2,1,0:T(8,128)S(1)}, u32[]{:S(2)}, u32[]{:S(2)}) async-start(f32[32,8,256]{2,1,0:T(8,128)} %listen.1), calls=%async_computation | async-start | bytes 524288 | tf_op jit(solution)/shard_map/all_to_all | solution.py:563
  89.1 1.8 %collective-permute-start.8 = (f32[4,64,128]{2,1,0:T(8,128)S(1)}, f32[4,64,128]{2,1,0:T(8,128)S(1)}, u32[]{:S(2)}, u32[]{:S(2)}) collective-permute-start(f32[4,64,128]{2,1,0:T(8,128)S(1)} %get-tuple-element.17), channel_id=1, source_target_pairs={{0,8},{8,0},{16,24},{24,16},{1,9},{9,1},{17,25},{25,17},{2,10},{10... | collective-permute-start | bytes 393224 | tf_op jit(solution)/shard_map/ppermute | solution.py:492
  90.9 1.5 %collective-permute-start.9 = (f32[4,64,128]{2,1,0:T(8,128)S(1)}, f32[4,64,128]{2,1,0:T(8,128)S(1)}, u32[]{:S(2)}, u32[]{:S(2)}) collective-permute-start(f32[4,64,128]{2,1,0:T(8,128)S(1)} %get-tuple-element.18), channel_id=1, source_target_pairs={{0,16},{8,24},{16,0},{24,8},{1,17},{9,25},{17,1},{25,9},{2,18},{10... | collective-permute-start | bytes 393224 | tf_op jit(solution)/shard_map/ppermute | solution.py:492
  92.4 0.3 collective-permute-start.10
  92.7 4.7 %collective-permute-done.8.refs_1_ = f32[4,64,128]{2,1,0:T(8,128)S(1)} collective-permute-done((f32[4,64,128]{2,1,0:T(8,128)S(1)}, f32[4,64,128]{2,1,0:T(8,128)S(1)}, u32[]{:S(2)}, u32[]{:S(2)}) %collective-permute-start.8) | collective-permute-done | bytes 131104 | tf_op jit(solution)/shard_map/ppermute | solution.py:492
  97.4 1.4 %collective-permute-done.9.refs_2_ = f32[4,64,128]{2,1,0:T(8,128)S(1)} collective-permute-done((f32[4,64,128]{2,1,0:T(8,128)S(1)}, f32[4,64,128]{2,1,0:T(8,128)S(1)}, u32[]{:S(2)}, u32[]{:S(2)}) %collective-permute-start.9) | collective-permute-done | bytes 131104 | tf_op jit(solution)/shard_map/ppermute | solution.py:492
  98.8 2.5 %collective-permute-done.10.refs_3_ = f32[4,64,128]{2,1,0:T(8,128)S(1)} collective-permute-done((f32[4,64,128]{2,1,0:T(8,128)S(1)}, f32[4,64,128]{2,1,0:T(8,128)S(1)}, u32[]{:S(2)}, u32[]{:S(2)}) %collective-permute-start.10) | collective-permute-done | bytes 131104 | tf_op jit(solution)/shard_map/ppermute | solution.py:492
  101.3 0.9 join.1
  102.2 0.0 all-to-all-done
  102.2 0.6 reduce_sum.9
  (2 shorter events, 0.0 us)
Async XLA Ops:
  0.6 9.2 %copy-start.1 = (f32[19,8,8,512]{3,2,1,0:T(8,128)S(1)}, f32[19,8,8,512]{3,2,1,0:T(8,128)}, u32[]{:S(2)}) copy-start(f32[19,8,8,512]{3,2,1,0:T(8,128)} %param.6) | copy-start | bytes 7471108
  0.6 1.1 %copy-start.2 = (s32[8,8,512]{2,1,0:T(8,128)S(1)}, s32[8,8,512]{2,1,0:T(8,128)}, u32[]{:S(2)}) copy-start(s32[8,8,512]{2,1,0:T(8,128)} %param.7) | copy-start | bytes 393220
  1.7 8.7 %copy-start.4 = (s32[1,8]{1,0:T(1,128)S(1)}, s32[1,8]{1,0:T(1,128)}, u32[]{:S(2)}) copy-start(s32[1,8]{1,0:T(1,128)} %cells_ref.1) | copy-start | bytes 100
  5.3 42.8 %collective-permute-start = (f32[153,8,128]{2,1,0:T(8,128)}, f32[153,8,128]{2,1,0:T(8,128)}, u32[]{:S(2)}, u32[]{:S(2)}) collective-permute-start(f32[153,8,128]{2,1,0:T(8,128)} %get-tuple-element.13.refs_1_), channel_id=1, source_target_pairs={{0,8},{8,0},{16,24},{24,16},{1,9},{9,1},{17,25},{25,17},{2,10},{10... | collective-permute-start | bytes 1880072 | tf_op jit(solution)/shard_map/ppermute | solution.py:492
  8.3 39.8 %collective-permute-start.1 = (f32[153,8,128]{2,1,0:T(8,128)}, f32[153,8,128]{2,1,0:T(8,128)}, u32[]{:S(2)}, u32[]{:S(2)}) collective-permute-start(f32[153,8,128]{2,1,0:T(8,128)} %get-tuple-element.14.refs_2_), channel_id=1, source_target_pairs={{0,16},{8,24},{16,0},{24,8},{1,17},{9,25},{17,1},{25,9},{2,18},{10... | collective-permute-start | bytes 1880072 | tf_op jit(solution)/shard_map/ppermute | solution.py:492
  9.8 38.3 %collective-permute-start.2 = (f32[153,8,128]{2,1,0:T(8,128)}, f32[153,8,128]{2,1,0:T(8,128)}, u32[]{:S(2)}, u32[]{:S(2)}) collective-permute-start(f32[153,8,128]{2,1,0:T(8,128)} %get-tuple-element.15.refs_3_), channel_id=1, source_target_pairs={{0,24},{8,16},{16,8},{24,0},{1,25},{9,17},{17,9},{25,1},{2,26},{10... | collective-permute-start | bytes 1880072 | tf_op jit(solution)/shard_map/ppermute | solution.py:492
  14.2 4.8 %collective-permute-start.4 = (f32[21,8,128]{2,1,0:T(8,128)S(1)}, f32[21,8,128]{2,1,0:T(8,128)S(1)}, u32[]{:S(2)}, u32[]{:S(2)}) collective-permute-start(f32[21,8,128]{2,1,0:T(8,128)S(1)} %get-tuple-element.29), channel_id=1, source_target_pairs={{1,0},{2,1},{3,2},{4,3},{5,4},{6,5},{7,6},{0,7},{9,8},{10,9},{11,1... | collective-permute-start | bytes 258056 | tf_op jit(solution)/shard_map/ppermute | solution.py:522
  16.9 5.7 %collective-permute-start.3 = (f32[21,8,128]{2,1,0:T(8,128)S(1)}, f32[21,8,128]{2,1,0:T(8,128)S(1)}, u32[]{:S(2)}, u32[]{:S(2)}) collective-permute-start(f32[21,8,128]{2,1,0:T(8,128)S(1)} %get-tuple-element.28), channel_id=1, source_target_pairs={{0,1},{1,2},{2,3},{3,4},{4,5},{5,6},{6,7},{7,0},{8,9},{9,10},{10,1... | collective-permute-start | bytes 258056 | tf_op jit(solution)/shard_map/ppermute | solution.py:521
  22.7 15.2 %collective-permute-start.5 = (f32[21,8,128]{2,1,0:T(8,128)S(1)}, f32[21,8,128]{2,1,0:T(8,128)S(1)}, u32[]{:S(2)}, u32[]{:S(2)}) collective-permute-start(f32[21,8,128]{2,1,0:T(8,128)S(1)} %get-tuple-element.26), channel_id=1, source_target_pairs={{0,8},{8,0},{16,24},{24,16},{1,9},{9,1},{17,25},{25,17},{2,10},{10... | collective-permute-start | bytes 258056 | tf_op jit(solution)/shard_map/ppermute | solution.py:492
  24.2 16.4 %collective-permute-start.6 = (f32[21,8,128]{2,1,0:T(8,128)S(1)}, f32[21,8,128]{2,1,0:T(8,128)S(1)}, u32[]{:S(2)}, u32[]{:S(2)}) collective-permute-start(f32[21,8,128]{2,1,0:T(8,128)S(1)} %get-tuple-element.25), channel_id=1, source_target_pairs={{0,16},{8,24},{16,0},{24,8},{1,17},{9,25},{17,1},{25,9},{2,18},{10... | collective-permute-start | bytes 258056 | tf_op jit(solution)/shard_map/ppermute | solution.py:492
  37.9 5.4 %collective-permute-start.7 = (f32[21,8,128]{2,1,0:T(8,128)S(1)}, f32[21,8,128]{2,1,0:T(8,128)S(1)}, u32[]{:S(2)}, u32[]{:S(2)}) collective-permute-start(f32[21,8,128]{2,1,0:T(8,128)S(1)} %get-tuple-element.24), channel_id=1, source_target_pairs={{0,24},{8,16},{16,8},{24,0},{1,25},{9,17},{17,9},{25,1},{2,26},{10... | collective-permute-start | bytes 258056 | tf_op jit(solution)/shard_map/ppermute | solution.py:492
  46.6 1.5 %copy-start = (f32[20,32,8,128]{3,2,1,0:T(8,128)}, f32[20,32,8,128]{3,2,1,0:T(8,128)S(1)}, u32[]{:S(2)}) copy-start(f32[20,32,8,128]{3,2,1,0:T(8,128)S(1)} %spread.1.refs_8_) | copy-start | bytes 7864324
  48.1 32.9 %copy-start.3 = (s32[32]{0:T(128)S(1)}, s32[32]{0:T(128)}, u32[]{:S(2)}) copy-start(s32[32]{0:T(128)} %owner_ref.1) | copy-start | bytes 388
  73.2 4.2 %collective-permute-start.11 = (f32[8,128]{1,0:T(8,128)S(1)}, f32[8,128]{1,0:T(8,128)S(1)}, u32[]{:S(2)}, u32[]{:S(2)}) collective-permute-start(f32[8,128]{1,0:T(8,128)S(1)} %get-tuple-element.21), channel_id=1, source_target_pairs={{0,8},{8,0},{16,24},{24,16},{1,9},{9,1},{17,25},{25,17},{2,10},{10... | collective-permute-start | bytes 12296 | tf_op jit(solution)/shard_map/ppermute | solution.py:492
  75.0 3.6 %collective-permute-start.12 = (f32[8,128]{1,0:T(8,128)S(1)}, f32[8,128]{1,0:T(8,128)S(1)}, u32[]{:S(2)}, u32[]{:S(2)}) collective-permute-start(f32[8,128]{1,0:T(8,128)S(1)} %get-tuple-element.22), channel_id=1, source_target_pairs={{0,16},{8,24},{16,0},{24,8},{1,17},{9,25},{17,1},{25,9},{2,18},{10... | collective-permute-start | bytes 12296 | tf_op jit(solution)/shard_map/ppermute | solution.py:492
  76.5 4.5 %collective-permute-start.13 = (f32[8,128]{1,0:T(8,128)S(1)}, f32[8,128]{1,0:T(8,128)S(1)}, u32[]{:S(2)}, u32[]{:S(2)}) collective-permute-start(f32[8,128]{1,0:T(8,128)S(1)} %get-tuple-element.23), channel_id=1, source_target_pairs={{0,24},{8,16},{16,8},{24,0},{1,25},{9,17},{17,9},{25,1},{2,26},{10... | collective-permute-start | bytes 12296 | tf_op jit(solution)/shard_map/ppermute | solution.py:492
  85.1 17.0 %all-to-all-start = ((f32[32,8,256]{2,1,0:T(8,128)}), f32[32,8,256]{2,1,0:T(8,128)S(1)}, u32[]{:S(2)}, u32[]{:S(2)}) async-start(f32[32,8,256]{2,1,0:T(8,128)} %listen.1), calls=%async_computation | async-start | bytes 524288 | tf_op jit(solution)/shard_map/all_to_all | solution.py:563
  89.1 8.3 %collective-permute-start.8 = (f32[4,64,128]{2,1,0:T(8,128)S(1)}, f32[4,64,128]{2,1,0:T(8,128)S(1)}, u32[]{:S(2)}, u32[]{:S(2)}) collective-permute-start(f32[4,64,128]{2,1,0:T(8,128)S(1)} %get-tuple-element.17), channel_id=1, source_target_pairs={{0,8},{8,0},{16,24},{24,16},{1,9},{9,1},{17,25},{25,17},{2,10},{10... | collective-permute-start | bytes 393224 | tf_op jit(solution)/shard_map/ppermute | solution.py:492
  90.9 7.8 %collective-permute-start.9 = (f32[4,64,128]{2,1,0:T(8,128)S(1)}, f32[4,64,128]{2,1,0:T(8,128)S(1)}, u32[]{:S(2)}, u32[]{:S(2)}) collective-permute-start(f32[4,64,128]{2,1,0:T(8,128)S(1)} %get-tuple-element.18), channel_id=1, source_target_pairs={{0,16},{8,24},{16,0},{24,8},{1,17},{9,25},{17,1},{25,9},{2,18},{10... | collective-permute-start | bytes 393224 | tf_op jit(solution)/shard_map/ppermute | solution.py:492
  92.4 8.9 %collective-permute-start.10 = (f32[4,64,128]{2,1,0:T(8,128)S(1)}, f32[4,64,128]{2,1,0:T(8,128)S(1)}, u32[]{:S(2)}, u32[]{:S(2)}) collective-permute-start(f32[4,64,128]{2,1,0:T(8,128)S(1)} %get-tuple-element.19), channel_id=1, source_target_pairs={{0,24},{8,16},{16,8},{24,0},{1,25},{9,17},{17,9},{25,1},{2,26},{10... | collective-permute-start | bytes 393224 | tf_op jit(solution)/shard_map/ppermute | solution.py:492

commit v3 on v2

v3 whole, which is shorter than its diff:
```python
import functools
import math

import jax
import jax.numpy as jnp
from jax import lax
from jax.experimental import pallas as pl
from jax.experimental.pallas import tpu as pltpu
from jax.sharding import PartitionSpec as P

STEPS = 8
HALO = STEPS
LANES = 128
RELAX = 1.6
UNROLL = 4

VELOCITIES = (
    (0, 0, 0),
    (1, 0, 0),
    (-1, 0, 0),
    (0, 1, 0),
    (0, -1, 0),
    (0, 0, 1),
    (0, 0, -1),
    (1, 1, 0),
    (-1, -1, 0),
    (1, -1, 0),
    (-1, 1, 0),
    (1, 0, 1),
    (-1, 0, -1),
    (1, 0, -1),
    (-1, 0, 1),
    (0, 1, 1),
    (0, -1, -1),
    (0, 1, -1),
    (0, -1, 1),
)
Q = len(VELOCITIES)
VMEM = pl.BlockSpec(memory_space=pltpu.VMEM)
SMEM = pl.BlockSpec(memory_space=pltpu.SMEM)
HBM = pl.BlockSpec(memory_space=pltpu.HBM)
F32 = jnp.float32


def opposite(member):
    if member == 0:
        return 0
    return member + 1 if member % 2 == 1 else member - 1


def moments(f):
    plus = [f[k] + f[k + 1] for k in range(1, Q, 2)]
    minus = [f[k] - f[k + 1] for k in range(1, Q, 2)]
    density = (
        (f[0] + (plus[0] + plus[1]))
        + ((plus[2] + plus[3]) + (plus[4] + plus[5]))
        + ((plus[6] + plus[7]) + plus[8])
    )
    m1, m3, m5, m7, m9, m11, m13, m15, m17 = minus
    jx = (m1 + (m7 + m9)) + (m11 + m13)
    jy = (m3 + (m7 - m9)) + (m15 + m17)
    jz = (m5 + (m11 - m13)) + (m15 - m17)
    return density, jx, jy, jz


def collide(f):
    density, jx, jy, jz = moments(f)
    guess = pl.reciprocal(density, approx=True)
    inv = guess * (2.0 - density * guess)
    inv = inv * (2.0 - density * inv)
    square = jx * jx + jy * jy + jz * jz
    base = RELAX * density - (1.5 * RELAX) * (square * inv)
    keep = 1.0 - RELAX
    out = [None] * Q
    out[0] = keep * f[0] + (1.0 / 3.0) * base
    for weight, members in ((1.0 / 18.0, range(1, 7, 2)), (1.0 / 36.0, range(7, Q, 2))):
        odd_scale = 3.0 * RELAX * weight
        ox, oy, oz = odd_scale * jx, odd_scale * jy, odd_scale * jz
        even_scale = (4.5 * RELAX * weight / (odd_scale * odd_scale)) * inv
        even_base = weight * base
        for k in members:
            cx, cy, cz = VELOCITIES[k]
            odd = None
            for c, o in ((cx, ox), (cy, oy), (cz, oz)):
                if c > 0:
                    odd = o if odd is None else odd + o
                elif c < 0:
                    odd = odd - o
            even = even_base + (odd * odd) * even_scale
            out[k] = keep * f[k] + (even + odd)
            out[k + 1] = keep * f[k + 1] + (even - odd)
    return out


def roll(value, shift, axis):
    size = value.shape[axis]
    if isinstance(shift, int):
        shift = shift % size
        return value if shift == 0 else pltpu.roll(value, shift, axis)
    return pltpu.roll(value, lax.rem(shift + 8 * size, size), axis)


def lane_iota():
    return lax.broadcasted_iota(jnp.int32, (8, LANES), 1)


def level_limits():
    z = lax.broadcasted_iota(jnp.int32, (8, LANES), 0)
    up = z - 1
    down = jnp.where(z == 7, -1, z + 1)
    return {0: z.astype(F32), 1: up.astype(F32), -1: down.astype(F32)}


def pulled(here_at, load, height, limits):
    here = [here_at(k) for k in range(Q)]
    f = [here[0]] + [None] * (Q - 1)
    for cx in (-1, 0, 1):
        for cy in (-1, 0, 1):
            members = [k for k in range(1, Q) if VELOCITIES[k][0] == cx and VELOCITIES[k][1] == cy]
            if not members:
                continue
            high = height(cy, cx)
            for k in members:
                cz = VELOCITIES[k][2]
                source = here[k] if cx == 0 and cy == 0 else load(k, cx)
                f[k] = jnp.where(limits[cz] < high, here[opposite(k)], roll(source, cz, 0))
    return f

SHIFTED = tuple(k for k in range(Q) if VELOCITIES[k][1] != 0)


def pack_kernel(n, width, order, me_ref, pop_ref, wall_ref, *refs):
    blocks, (tiles, solid_ref, sems, wall_sem) = refs[:n], refs[n:]
    me = me_ref[0]
    copies = {}
    for m in order:
        place = lax.div(jnp.bitwise_xor(me, m) * width, LANES) * LANES
        copies[m] = pltpu.make_async_copy(
            pop_ref.at[:, :, pl.ds(pl.multiple_of(place, LANES), LANES)], tiles.at[m], sems.at[m]
        )
        copies[m].start()
    walls = pltpu.make_async_copy(wall_ref, solid_ref, wall_sem)
    walls.start()
    for m in order:
        dest = jnp.bitwise_xor(me, m) * width
        turn = 0 if width % LANES == 0 else lax.div(dest, LANES) * LANES - dest
        copies[m].wait()

        def row(r, carry, m=m, turn=turn):
            out = collide([tiles[m, k, pl.ds(r, 8, stride=8), :] for k in range(Q)])
            for k in range(Q):
                blocks[m][k * 8 + r] = roll(out[k], turn, 1)
            return carry

        lax.fori_loop(0, 8, row, 0, unroll=4)
    walls.wait()
    for m in order:
        dest = jnp.bitwise_xor(me, m) * width
        place = lax.div(dest, LANES) * LANES
        total = None
        for z in range(8):
            level = solid_ref[pl.ds(z * 8, 8), pl.ds(pl.multiple_of(place, LANES), LANES)]
            total = level if total is None else total + level
        blocks[m][Q * 8] = roll(total.astype(F32), 0 if width % LANES == 0 else place - dest, 1)


def plane_rows(block, k, last):
    if last:
        return [jnp.broadcast_to(block[Q * 8, pl.ds(r, 1), :], (8, LANES)) for r in range(8)]
    return [block[k * 8 + r] for r in range(8)]


def ends_joined(v, width, count):
    if width == LANES:
        return v
    return jnp.where(lane_iota() >= LANES - count, roll(v, LANES - width, 1), v)


def edge_kernel(n, width, me_ref, cells_ref, *refs):
    blocks, (out, ends) = refs[:n], refs[n:]
    me = me_ref[0]
    lane = lane_iota()
    pair = 2 * HALO
    first = lax.rem(lane, pair) < HALO
    sub = lax.broadcasted_iota(jnp.int32, (8, LANES), 0)
    for m in range(n):
        d = jnp.bitwise_xor(me, m)

        def plane(k, carry, last=False, m=m, d=d):
            c = None
            for r, v in enumerate(plane_rows(blocks[m], k, last)):
                v = roll(ends_joined(v, width, HALO), r * pair + HALO, 1)
                c = v if c is None else jnp.where(lane >= r * pair, v, c)
            ends[d + 1, k] = c
            return carry

        lax.fori_loop(0, Q - 1, plane, 0, unroll=3)
        plane(Q - 1, 0)
        plane(Q, 0, last=True)
    zero = jnp.zeros((8, LANES), F32)
    cells = zero
    for p in range(8):
        cells = jnp.where(sub == p, cells_ref[0, p].astype(F32), cells)
    for e in range(n + 2):
        for k in range(Q + 1):
            left = ends[e - 1, k] if e >= 2 else zero
            right = ends[e + 1, k] if e < n else zero
            out[e, k] = jnp.where(first, left, right)
        out[e, Q + 1] = cells if 1 <= e <= n else zero


def passing(plain, turned, high, at):
    def load(k, cx):
        if VELOCITIES[k][1] == 0:
            return plain[(k, *at[cx])]
        return turned[(SHIFTED.index(k), *at[cx])]

    return pulled(
        lambda k: plain[(k, *at[0])],
        load,
        lambda cy, cx: high[(cy + 1, *at[cx])],
        level_limits(),
    )


def put(plain, turned, at, out):
    for k in range(Q):
        plain[(k, *at)] = out[k]
    for slot, k in enumerate(SHIFTED):
        turned[(slot, *at)] = roll(out[k], VELOCITIES[k][1], 1)


def run_steps(step):
    def twice(s, c):
        step(0)
        step(1)
        return c

    lax.fori_loop(0, (STEPS - 1) // 2, twice, 0)
    if (STEPS - 1) % 2:
        step(0)
    return (STEPS - 1) % 2


def flow_kernel(n, me_ref, *refs):
    blocks, means = refs[:n], refs[n]
    scratch = refs[n + 1 :]
    plain, turned, high = scratch[0:2], scratch[2:4], scratch[4]
    rows = 8 * n
    me = me_ref[0]
    for m in range(n):
        start = jnp.bitwise_xor(me, m) * 8
        for r, v in enumerate(plane_rows(blocks[m], Q, True)):
            for cy in (-1, 0, 1):
                high[cy + 1, start + r] = roll(v, cy, 1)

        def fill(r, c, m=m, start=start):
            put(plain[0], turned[0], (start + r,), [blocks[m][k * 8 + r] for k in range(Q)])
            return c

        lax.fori_loop(0, 8, fill, 0, unroll=4)

    def around(x):
        return {1: (lax.rem(x + rows - 1, rows),), 0: (x,), -1: (lax.rem(x + 1, rows),)}

    def step(slot):
        def row(x, c):
            out = collide(passing(plain[slot], turned[slot], high, around(x)))
            put(plain[1 - slot], turned[1 - slot], (x,), out)
            return c

        lax.fori_loop(0, rows, row, 0, unroll=UNROLL)

    last = run_steps(step)

    def final(x, c):
        for q, v in enumerate(moments(passing(plain[last], turned[last], high, around(x)))):
            means[q, x] = v
        return c

    lax.fori_loop(0, rows, final, 0, unroll=UNROLL)


def seam_kernel(n, width, me_ref, *refs):
    blocks, edges, middle = refs[:n], refs[n : 2 * n], refs[2 * n]
    refs = refs[2 * n + 1 :]
    fields, picks = refs[:n], refs[n]
    plain, turned = refs[n + 1 : n + 3], refs[n + 3 : n + 5]
    high, means, column = refs[n + 5 :]
    depth = 2 * n
    group = 4 * HALO
    me = me_ref[0]
    lane = lane_iota()
    sub = lax.broadcasted_iota(jnp.int32, (8, LANES), 0)
    within = lax.rem(lane, group)
    at_left = (within >= HALO) & (within < 2 * HALO)
    at_right = (within >= 2 * HALO) & (within < 3 * HALO)
    whole = n == 4

    def home(m):
        x = jnp.bitwise_xor(me, m) * 8
        return lax.div(x, depth), lax.rem(x, depth)

    def fill(k, carry, last=False):
        rows_of = [plane_rows(blocks[m], k, last) for m in range(n)]
        strips = [edges[m][k] for m in range(n)]
        for r in range(8):
            left = right = None
            for m in range(n):
                at, base = home(m)
                v = roll(ends_joined(rows_of[m][r], width, 2 * HALO), at * group + 2 * HALO, 1)
                e = roll(strips[m], at * group + HALO - r * 2 * HALO, 1)
                a, b = jnp.where(at_left, e, v), jnp.where(at_right, e, v)
                if not whole:
                    row = base + r + 1
                    ref = high if last else plain[0]
                    lead = 1 if last else k
                    left, right = ref[lead, 0, row], ref[lead, 1, row]
                mine = (lane >= at * group) & (lane < (at + 1) * group)
                left = a if left is None else jnp.where(mine, a, left)
                right = b if right is None else jnp.where(mine, b, right)
                if not whole:
                    ref[lead, 0, row] = left
                    ref[lead, 1, row] = right
            if whole:
                ref = high if last else plain[0]
                lead = 1 if last else k
                ref[lead, 0, r + 1] = left
                ref[lead, 1, r + 1] = right
        return carry

    lax.fori_loop(0, Q - 1, fill, 0, unroll=1 if not whole else 2)
    fill(Q - 1, 0)
    fill(Q, 0, last=True)
    for side in range(2):
        for r in range(1, depth + 1):
            for cy in (-1, 1):
                high[cy + 1, side, r] = roll(high[1, side, r], cy, 1)
        for c in range(3):
            high[c, side, 0] = roll(high[c, side, depth], group, 1)
            high[c, side, depth + 1] = roll(high[c, side, 1], -group, 1)
        for slot, k in enumerate(SHIFTED):
            for r in range(1, depth + 1):
                turned[0][slot, side, r] = roll(plain[0][k, side, r], VELOCITIES[k][1], 1)

    def wrap(slot):
        for k in range(Q):
            cx, cy, _ = VELOCITIES[k]
            if cx == 0:
                continue
            ref, at = (plain[slot], k) if cy == 0 else (turned[slot], SHIFTED.index(k))
            for side in range(2):
                if cx > 0:
                    ref[at, side, 0] = roll(ref[at, side, depth], group, 1)
                else:
                    ref[at, side, depth + 1] = roll(ref[at, side, 1], -group, 1)

    wrap(0)

    def around(side, r):
        return {1: (side, r - 1), 0: (side, r), -1: (side, r + 1)}

    def step(slot):
        def row(r, c):
            for side in range(2):
                out = collide(passing(plain[slot], turned[slot], high, around(side, r)))
                put(plain[1 - slot], turned[1 - slot], (side, r), out)
            return c

        lax.fori_loop(1, depth + 1, row, 0, unroll=UNROLL // 2)
        wrap(1 - slot)

    last = run_steps(step)

    def final(r, c):
        both = [moments(passing(plain[last], turned[last], high, around(side, r))) for side in range(2)]
        for q in range(4):
            means[q, r - 1] = jnp.where(at_left, both[1][q], both[0][q])
        return c

    lax.fori_loop(1, depth + 1, final, 0, unroll=UNROLL // 2)

    ids = jnp.where(lane < width, sub * (n * width) + me * width + lane, -1).astype(F32)
    for m in range(n):
        g = jnp.bitwise_xor(me, m)
        at, base = home(m)
        for q in range(4):
            for r in range(8):
                ends = roll(means[q, base + r], -(at * group + 2 * HALO), 1)
                v = jnp.where(lane < HALO, ends, middle[q, g * 8 + r])
                after = ends if width == LANES else roll(ends, width, 1)
                v = jnp.where(lane >= width - HALO, after, v)
                fields[m][q, pl.ds(r, 8, stride=8), :] = v
                column[m, q, pl.ds(r, 1), :] = jnp.sum(v, axis=0, keepdims=True) * (1.0 / 8.0)
    for m in range(n):
        g = jnp.bitwise_xor(me, m)
        cells = edges[m][Q + 1]
        found = [None] * 4
        for p in range(8):
            hit = ids == jnp.broadcast_to(cells[p : p + 1, :], (8, LANES))
            for q in range(4):
                value = jnp.sum(jnp.where(hit, column[m, q], 0.0), axis=0, keepdims=True)
                value = jnp.broadcast_to(value, (8, LANES))
                found[q] = value if p == 0 else jnp.where(sub == p, value, found[q])
        result = jnp.zeros((8, LANES), F32)
        for q in range(4):
            result = jnp.where(lane == q, jnp.sum(found[q], axis=1, keepdims=True), result)
        picks[g] = result


def vectors(*sizes):
    return [pltpu.VMEM((*size, 8, LANES), F32) for size in sizes]


def held(scratch):
    return 4 * sum(math.prod(piece.shape) for piece in scratch)


def listen_kernel(count_ref, owner_ref, picks, weights, out, signal):
    listeners, bins = signal.shape
    tiles, block = out.shape[:2]
    sub = lax.broadcasted_iota(jnp.int32, (8, LANES), 0)
    lane = lane_iota()
    total = picks[0]
    for m in range(1, picks.shape[0]):
        total = total + picks[m]
    total = total - jnp.where(lane == 0, 1.0, 0.0)
    total = jnp.where(sub < count_ref[0], total, 0.0)
    total = total.astype(jnp.bfloat16).astype(F32)
    factors = [
        jnp.broadcast_to(total[p : p + 1, q : q + 1], (16, LANES)) for p in range(8) for q in range(4)
    ]

    def rows(i, c):
        at = pl.ds(pl.multiple_of(i * 16, 16), 16)
        for b in range(0, bins, LANES):
            sums = []
            for start in range(0, 32, 8):
                acc = None
                for k in range(start, start + 8):
                    term = factors[k] * weights[k, at, pl.ds(b, LANES)].astype(F32)
                    acc = term if acc is None else acc + term
                sums.append(acc)
            signal[at, pl.ds(b, LANES)] = (sums[0] + sums[1]) + (sums[2] + sums[3])
        return c

    lax.fori_loop(0, listeners // 16, rows, 0)

    def move(t, c):
        out[t] = signal[pl.ds(pl.multiple_of(owner_ref[t] * block, block), block), :]
        return c

    lax.fori_loop(0, tiles, move, 0, unroll=4)


def join_kernel(n, width, me_ref, *refs):
    parts, out = refs[:n], refs[n]
    me = me_ref[0]
    lane = lane_iota()
    if width == LANES:
        for m in range(n):
            place = pl.multiple_of(jnp.bitwise_xor(me, m) * width, LANES)
            out[:, :, pl.ds(place, LANES)] = parts[m][...]
        return
    for m in range(0, n, 2):
        first = jnp.bitwise_xor(me, m)
        even = lax.rem(first, 2) == 0
        place = pl.multiple_of(lax.div(first, 2) * LANES, LANES)
        for q in range(4):
            for z in range(8):
                at = pl.ds(z * 8, 8)
                x, y = parts[m][q, at, :], parts[m + 1][q, at, :]
                low, upper = jnp.where(even, x, y), jnp.where(even, y, x)
                out[q, at, pl.ds(place, LANES)] = jnp.where(lane < width, low, roll(upper, width, 1))


def shape(*dims):
    return jax.ShapeDtypeStruct(dims, F32)


def call(kernel, name, arguments, specs, out_shape, scratch=(), extra=0, grant=0, work=0):
    outs = out_shape if isinstance(out_shape, list) else [out_shape]
    held = [a for a, spec in zip(arguments, specs) if spec is VMEM] + outs
    size = sum(a.size * a.dtype.itemsize for a in held) + extra
    return pl.pallas_call(
        kernel,
        out_shape=out_shape,
        in_specs=specs,
        out_specs=[VMEM] * len(outs) if isinstance(out_shape, list) else VMEM,
        scratch_shapes=list(scratch),
        compiler_params=pltpu.CompilerParams(
            vmem_limit_bytes=max(grant, size + size // 8 + 2 * 1024 * 1024)
        ),
        cost_estimate=pl.CostEstimate(flops=0, bytes_accessed=work, transcendentals=0) if work else None,
        name=name,
    )(*arguments)


def on_device(populations, solid, panel_cells, panel_counts, owner, retarded):
    n = lax.axis_size("gx")
    ny = lax.axis_size("gy")
    span = populations.shape[3]
    width = span // n
    me = lax.axis_index("gx").astype(jnp.int32).reshape(1)
    swap = [[(i, i ^ m) for i in range(n)] for m in range(n)]
    rows = 8 * n

    def exchange(parts):
        return [parts[0]] + [lax.ppermute(parts[m], "gx", swap[m]) for m in range(1, n)]

    order = [n - 1] + list(range(1, n - 1)) + [0]
    blocks = call(
        functools.partial(pack_kernel, n, width, order),
        "pack",
        [me, populations.reshape(Q, 64, span), solid.reshape(64, span)],
        [SMEM, HBM, HBM],
        [shape(Q * 8 + 1, 8, LANES)] * n,
        [
            pltpu.VMEM((n, Q, 64, LANES), F32),
            pltpu.VMEM((64, span), jnp.int32),
            pltpu.SemaphoreType.DMA((n,)),
            pltpu.SemaphoreType.DMA,
        ],
        extra=4 * (n * Q + 4) * 64 * LANES,
        grant=60 * 1024 * 1024,
    )
    received = exchange(blocks)
    strips = call(
        functools.partial(edge_kernel, n, width),
        "edges",
        [me, panel_cells, *blocks],
        [SMEM, SMEM] + [VMEM] * n,
        shape(n + 2, Q + 2, 8, LANES),
        vectors((n + 1, Q + 1)),
        extra=4 * (n + 1) * (Q + 1) * 8 * LANES,
    )
    up = [(j, (j + 1) % ny) for j in range(ny)]
    down = [(j, i) for i, j in up]
    before = lax.ppermute(strips[n + 1], "gy", up)
    after = lax.ppermute(strips[0], "gy", down)
    edges = []
    for m in range(n):
        dest = jnp.bitwise_xor(me[0], m)
        own = lax.dynamic_index_in_dim(strips, dest + 1, 0, keepdims=False)
        edges.append(own + jnp.where(dest == 0, before, 0.0) + jnp.where(dest == n - 1, after, 0.0))
    edges = exchange(edges)
    few, depth = len(SHIFTED), 2 * n
    scratch = vectors((Q, rows), (Q, rows), (few, rows), (few, rows), (3, rows))
    middle = call(
        functools.partial(flow_kernel, n),
        "flow",
        [me, *received],
        [SMEM] + [VMEM] * n,
        shape(4, rows, 8, LANES),
        scratch,
        extra=held(scratch),
        work=STEPS * rows * 73 * 4 * 8 * LANES,
    )
    lines = (2, depth + 2)
    scratch = vectors((Q, *lines), (Q, *lines), (few, *lines), (few, *lines), (3, *lines), (4, depth), (n, 4))
    *parts, picks = call(
        functools.partial(seam_kernel, n, width),
        "seam",
        [me, *received, *edges, middle],
        [SMEM] + [VMEM] * (2 * n + 1),
        [shape(4, 64, LANES)] * n + [shape(n, 8, LANES)],
        scratch,
        extra=held(scratch),
        work=STEPS * 16 * 73 * 4 * 8 * LANES,
    )
    weights = retarded.reshape(32, *retarded.shape[3:])
    picks = lax.all_to_all(picks, "gx", 0, 0, tiled=True)
    parts = exchange(parts)

    listeners, bins = retarded.shape[3:]
    tiles = n * ny
    partial_signal = call(
        listen_kernel,
        "listen",
        [panel_counts, owner, picks, weights],
        [SMEM, SMEM, VMEM, VMEM],
        shape(tiles, listeners // tiles, bins),
        [pltpu.VMEM((listeners, bins), F32)],
        extra=4 * listeners * bins,
    )
    gathered = lax.all_to_all(partial_signal, ("gx", "gy"), 0, 0, tiled=True)
    owned_signal = jnp.sum(gathered, axis=0)

    fields = call(
        functools.partial(join_kernel, n, width),
        "join",
        [me, *parts],
        [SMEM] + [VMEM] * n,
        shape(4, 64, span),
    )
    return fields.reshape(4, 8, 8, span), owned_signal


def solution(mesh):
    in_specs = (
        P(None, None, "gx", "gy"),
        P(None, "gx", "gy"),
        P(("gx", "gy"), None),
        P(("gx", "gy")),
        P(),
        P(("gx", "gy"), None, None, None, None),
    )
    out_specs = (P(None, None, "gx", "gy"), P(("gx", "gy"), None))
    return jax.shard_map(
        on_device, mesh=mesh, in_specs=in_specs, out_specs=out_specs, check_vma=False
    )
```

time: 103 us -> 94.7 us (0.919)
  Pallas kernels: 41.3 us -> 35 us
  waiting for transfers between devices: 32.8 us -> 27 us
  local copies, waits for them, and re-layouts: 2.57 us -> 7.17 us
  starting transfers between devices: 24.1 us -> 22.9 us
    ppermute x12 -> x9, waiting for transfers between devices: 27.1 us -> 20.7 us  [exchange(): lax.ppermute(parts[m], 'gx', swap[m])]
    pallas_call x7 -> x6, Pallas kernels: 41.3 us -> 35 us  [call(): pl.pallas_call(kernel, out_shape=out_shape, in_specs=specs, out_specs=[VM...]
    ppermute x12 -> x9, starting transfers between devices: 17.4 us -> 11.7 us  [exchange(): lax.ppermute(parts[m], 'gx', swap[m])]
    unnamed x10 -> x16, local copies, waits for them, and re-layouts: 2.55 us -> 7.16 us
    all_to_all x0 -> x1, waiting for transfers between devices: none -> 4.06 us  [on_device(): picks = lax.all_to_all(picks, 'gx', 0, 0, tiled=True)]
    all_to_all x0 -> x1, starting transfers between devices: none -> 3.61 us  [on_device(): picks = lax.all_to_all(picks, 'gx', 0, 0, tiled=True)]
    ppermute x1, waiting for transfers between devices: 2.1 us -> 0.01 us  [on_device(): after = lax.ppermute(strips[0], 'gy', down)]
    ppermute x1, waiting for transfers between devices: 3.61 us -> 2.2 us  [on_device(): before = lax.ppermute(strips[n + 1], 'gy', up)]
  transfers between devices with their start and end apart: 15 -> 13, of which waited for: 9 -> 6; matrix products, arithmetic and copies ran while one was open for 0% -> 0% of each run, Pallas kernels for 8% -> 19%
where the time goes in v3:
time: 94.7 us; the launch traced here: 94.2 us
  Pallas kernels  35 us (37%)
  waiting for transfers between devices  27 us (29%)
  starting transfers between devices  22.9 us (24%)
  local copies, waits for them, and re-layouts  7.17 us (8%)
  between operations  1.39 us (1%)
    pallas_call x6, Pallas kernels, call(): pl.pallas_call(kernel, out_shape=out_shape, in_specs=specs, out_specs=[VM...  35 us
    ppermute x9, waiting for transfers between devices, exchange(): lax.ppermute(parts[m], 'gx', swap[m])  20.7 us
    ppermute x9, starting transfers between devices, exchange(): lax.ppermute(parts[m], 'gx', swap[m])  11.7 us
    unnamed x16, local copies, waits for them, and re-layouts  7.16 us
    all_to_all x1, waiting for transfers between devices, on_device(): picks = lax.all_to_all(picks, 'gx', 0, 0, tiled=True)  4.06 us
    all_to_all x1, starting transfers between devices, on_device(): gathered = lax.all_to_all(partial_signal, ('gx', 'gy'), 0, 0, tiled=True)  4.01 us
    all_to_all x1, starting transfers between devices, on_device(): picks = lax.all_to_all(picks, 'gx', 0, 0, tiled=True)  3.61 us
    ppermute x1, starting transfers between devices, on_device(): after = lax.ppermute(strips[0], 'gy', down)  3.53 us
  transfers between devices with their start and end apart: 13, of which 6 were waited for; matrix products, arithmetic and copies ran while one was open for 0% of the time, Pallas kernels for 19%

profile of v3, /device:TPU:0, one launch (start us, length us, event | category | flops | bytes accessed | tf_op | source)
XLA Modules:
  0.0 94.2 jit_solution(4266749491996006661)
XLA Ops:
  0.6 3.8 %pack.1 = (f32[153,8,128]{2,1,0:T(8,128)}, f32[153,8,128]{2,1,0:T(8,128)}, f32[153,8,128]{2,1,0:T(8,128)}, f32[153,8,128]{2,1,0:T(8,128)}) custom-call(s32[1]{0:T(128)} %bitcast.me_ref, f32[19,64,512]{2,1,0:T(8,128)} %bitcast.26, s32[64,512]{1,0:T(8,128)} %bitcast.28), custom_call_target="tpu_custom_call" | custom-call | tf_op jit(solution)/shard_map/pack/pallas_call | solution.py:485
  4.5 3.0 %collective-permute-start = (f32[153,8,128]{2,1,0:T(8,128)}, f32[153,8,128]{2,1,0:T(8,128)S(1)}, u32[]{:S(2)}, u32[]{:S(2)}) collective-permute-start(f32[153,8,128]{2,1,0:T(8,128)} %get-tuple-element.12.refs_1_), channel_id=1, source_target_pairs={{0,8},{8,0},{16,24},{24,16},{1,9},{9,1},{17,25},{25,17},{2,10},{10... | collective-permute-start | bytes 1880072 | tf_op jit(solution)/shard_map/ppermute | solution.py:509
  7.5 1.5 %collective-permute-start.1 = (f32[153,8,128]{2,1,0:T(8,128)}, f32[153,8,128]{2,1,0:T(8,128)S(1)}, u32[]{:S(2)}, u32[]{:S(2)}) collective-permute-start(f32[153,8,128]{2,1,0:T(8,128)} %get-tuple-element.13.refs_2_), channel_id=1, source_target_pairs={{0,16},{8,24},{16,0},{24,8},{1,17},{9,25},{17,1},{25,9},{2,18},{10... | collective-permute-start | bytes 1880072 | tf_op jit(solution)/shard_map/ppermute | solution.py:509
  9.0 0.0 collective-permute-start.2
  9.0 0.0 copy-start
  9.0 1.1 %copy-done = f32[153,8,128]{2,1,0:T(8,128)S(1)} copy-done((f32[153,8,128]{2,1,0:T(8,128)S(1)}, f32[153,8,128]{2,1,0:T(8,128)}, u32[]{:S(2)}) %copy-start) | copy-done | bytes 626712
  10.1 0.0 copy-start.3
  10.1 1.1 %copy-done.3 = f32[153,8,128]{2,1,0:T(8,128)S(1)} copy-done((f32[153,8,128]{2,1,0:T(8,128)S(1)}, f32[153,8,128]{2,1,0:T(8,128)}, u32[]{:S(2)}) %copy-start.3) | copy-done | bytes 626712
  11.2 0.0 copy-start.4
  11.2 1.1 %copy-done.4 = f32[153,8,128]{2,1,0:T(8,128)S(1)} copy-done((f32[153,8,128]{2,1,0:T(8,128)S(1)}, f32[153,8,128]{2,1,0:T(8,128)}, u32[]{:S(2)}) %copy-start.4) | copy-done | bytes 626712
  12.2 0.0 copy-start.5
  12.2 1.1 %copy-done.5 = f32[153,8,128]{2,1,0:T(8,128)S(1)} copy-done((f32[153,8,128]{2,1,0:T(8,128)S(1)}, f32[153,8,128]{2,1,0:T(8,128)}, u32[]{:S(2)}) %copy-start.5) | copy-done | bytes 626712
  13.3 0.0 copy-start.7
  13.3 0.7 copy-done.7
  14.0 2.9 %edges.1 = f32[6,21,8,128]{3,2,1,0:T(8,128)S(1)} custom-call(s32[1]{0:T(128)} %bitcast.me_ref, s32[1,8]{1,0:T(1,128)S(1)} %copy-done.7, f32[153,8,128]{2,1,0:T(8,128)S(1)} %copy-done, f32[153,8,128]{2,1,0:T(8,128)S(1)} %copy-done.5, f32[153,8,128]{2,1,0:T(8,128)S(1)} %copy-done.4, f32[153,8,128]{2,1,0:T(8,128)S(1)} %copy-done.3), custom_call_target="tpu_custom_call" | custom-call | tf_op jit(solution)/shard_map/edges/pallas_call | solution.py:485
  16.9 0.0 copy-start.6
  16.9 0.1 collective-permute-start.3
  17.0 3.5 %collective-permute-start.4 = (f32[21,8,128]{2,1,0:T(8,128)S(1)}, f32[21,8,128]{2,1,0:T(8,128)S(1)}, u32[]{:S(2)}, u32[]{:S(2)}) collective-permute-start(f32[21,8,128]{2,1,0:T(8,128)S(1)} %get-tuple-element.25), channel_id=1, source_target_pairs={{1,0},{2,1},{3,2},{4,3},{5,4},{6,5},{7,6},{0,7},{9,8},{10,9},{11,1... | collective-permute-start | bytes 258056 | tf_op jit(solution)/shard_map/ppermute | solution.py:540
  20.5 2.2 %collective-permute-done.3 = f32[21,8,128]{2,1,0:T(8,128)S(1)} collective-permute-done((f32[21,8,128]{2,1,0:T(8,128)S(1)}, f32[21,8,128]{2,1,0:T(8,128)S(1)}, u32[]{:S(2)}, u32[]{:S(2)}) %collective-permute-start.3) | collective-permute-done | bytes 86048 | tf_op jit(solution)/shard_map/ppermute | solution.py:539
  22.7 0.0 collective-permute-done.4
  22.7 0.1 fusion
  22.8 2.1 %collective-permute-start.5 = (f32[21,8,128]{2,1,0:T(8,128)S(1)}, f32[21,8,128]{2,1,0:T(8,128)S(1)}, u32[]{:S(2)}, u32[]{:S(2)}) collective-permute-start(f32[21,8,128]{2,1,0:T(8,128)S(1)} %get-tuple-element.22), channel_id=1, source_target_pairs={{0,8},{8,0},{16,24},{24,16},{1,9},{9,1},{17,25},{25,17},{2,10},{10... | collective-permute-start | bytes 258056 | tf_op jit(solution)/shard_map/ppermute | solution.py:509
  24.8 1.5 %collective-permute-start.6 = (f32[21,8,128]{2,1,0:T(8,128)S(1)}, f32[21,8,128]{2,1,0:T(8,128)S(1)}, u32[]{:S(2)}, u32[]{:S(2)}) collective-permute-start(f32[21,8,128]{2,1,0:T(8,128)S(1)} %get-tuple-element.21), channel_id=1, source_target_pairs={{0,16},{8,24},{16,0},{24,8},{1,17},{9,25},{17,1},{25,9},{2,18},{10... | collective-permute-start | bytes 258056 | tf_op jit(solution)/shard_map/ppermute | solution.py:509
  26.3 0.0 collective-permute-done.refs_1_
  26.3 0.0 collective-permute-start.7
  26.4 12.3 %collective-permute-done.1.refs_2_ = f32[153,8,128]{2,1,0:T(8,128)S(1)} collective-permute-done((f32[153,8,128]{2,1,0:T(8,128)}, f32[153,8,128]{2,1,0:T(8,128)S(1)}, u32[]{:S(2)}, u32[]{:S(2)}) %collective-permute-start.1) | collective-permute-done | bytes 626720 | tf_op jit(solution)/shard_map/ppermute | solution.py:509
  38.6 0.0 collective-permute-done.2.refs_3_
  38.6 0.0 copy-done.1
  38.6 14.1 %flow.1.refs_8_ = f32[4,32,8,128]{3,2,1,0:T(8,128)S(1)} custom-call(s32[1]{0:T(128)} %bitcast.me_ref, f32[153,8,128]{2,1,0:T(8,128)S(1)} %copy-done.1, f32[153,8,128]{2,1,0:T(8,128)S(1)} %collective-permute-done.refs_1_, f32[153,8,128]{2,1,0:T(8,128)S(1)} %collective-permute-done.1.refs_2_, f32[153,8,128]{2,1,0:T(8,128)S(1)} %collective-permute-done.2.refs_3_), custom_call_target="tpu_custom_call" | custom-call | bytes 76546048 | tf_op jit(solution)/shard_map/flow/pallas_call | solution.py:485
  52.8 0.0 collective-permute-done.5.refs_5_
  52.8 0.0 collective-permute-done.6.refs_6_
  52.8 0.0 collective-permute-done.7.refs_7_
  52.8 10.8 %seam.1 = (f32[4,64,128]{2,1,0:T(8,128)S(1)}, f32[4,64,128]{2,1,0:T(8,128)S(1)}, f32[4,64,128]{2,1,0:T(8,128)S(1)}, f32[4,64,128]{2,1,0:T(8,128)S(1)}, f32[4,8,128]{2,1,0:T(8,128)}) custom-call(s32[1]{0:T(128)} %bitcast.me_ref, f32[153,8,128]{2,1,0:T(8,128)S(1)} %copy-done.1, f32[153,8,128]{2,1,0:T(8,128)S(1)} %collective-permute-done.refs_1_, ...), custom_call_target="tpu_custom_call" | custom-call | bytes 38273024 | tf_op jit(solution)/shard_map/seam/pallas_call | solution.py:485
  63.7 3.6 %all-to-all-start = ((f32[4,8,128]{2,1,0:T(8,128)}), f32[4,8,128]{2,1,0:T(8,128)S(1)}, u32[]{:S(2)}, u32[]{:S(2)}) async-start(f32[4,8,128]{2,1,0:T(8,128)} %get-tuple-element.19), calls=%async_computation | async-start | bytes 32768 | tf_op jit(solution)/shard_map/all_to_all | solution.py:572
  67.9 4.1 %all-to-all-done.picks = f32[4,8,128]{2,1,0:T(8,128)S(1)} async-done(((f32[4,8,128]{2,1,0:T(8,128)}), f32[4,8,128]{2,1,0:T(8,128)S(1)}, u32[]{:S(2)}, u32[]{:S(2)}) %all-to-all-start) | async-done | bytes 16416 | tf_op jit(solution)/shard_map/all_to_all | solution.py:572
  72.0 0.0 copy-done.6
  72.0 2.2 %copy-done.2 = bf16[1,8,4,256,256]{4,3,2,1,0:T(8,128)(2,1)S(1)} copy-done((bf16[1,8,4,256,256]{4,3,2,1,0:T(8,128)(2,1)S(1)}, bf16[1,8,4,256,256]{4,3,2,1,0:T(8,128)(2,1)}, u32[]{:S(2)}) %copy-start.2) | copy-done | bytes 4194328
  74.2 2.5 %listen.1 = f32[32,8,256]{2,1,0:T(8,128)} custom-call(s32[1]{0:T(128)S(6)} %copy.8.count_ref, s32[32]{0:T(128)S(1)} %copy-done.6, f32[4,8,128]{2,1,0:T(8,128)S(1)} %all-to-all-done.picks, bf16[32,256,256]{2,1,0:T(8,128)(2,1)S(1)} %bitcast.25), custom_call_target="tpu_custom_call" | custom-call | tf_op jit(solution)/shard_map/listen/pallas_call | solution.py:485
  76.7 4.0 %all-to-all-start.1 = ((f32[32,8,256]{2,1,0:T(8,128)}), f32[32,8,256]{2,1,0:T(8,128)S(1)}, u32[]{:S(2)}, u32[]{:S(2)}) async-start(f32[32,8,256]{2,1,0:T(8,128)} %listen.1), calls=%async_computation.1 | async-start | bytes 524288 | tf_op jit(solution)/shard_map/all_to_all | solution.py:586
  80.7 2.7 %collective-permute-start.10 = (f32[4,64,128]{2,1,0:T(8,128)S(1)}, f32[4,64,128]{2,1,0:T(8,128)S(1)}, u32[]{:S(2)}, u32[]{:S(2)}) collective-permute-start(f32[4,64,128]{2,1,0:T(8,128)S(1)} %get-tuple-element.18), channel_id=1, source_target_pairs={{0,24},{8,16},{16,8},{24,0},{1,25},{9,17},{17,9},{25,1},{2,26},{10... | collective-permute-start | bytes 393224 | tf_op jit(solution)/shard_map/ppermute | solution.py:509
  83.4 0.6 collective-permute-start.8
  84.0 0.3 collective-permute-start.9
  84.2 5.7 %collective-permute-done.10.refs_3_ = f32[4,64,128]{2,1,0:T(8,128)S(1)} collective-permute-done((f32[4,64,128]{2,1,0:T(8,128)S(1)}, f32[4,64,128]{2,1,0:T(8,128)S(1)}, u32[]{:S(2)}, u32[]{:S(2)}) %collective-permute-start.10) | collective-permute-done | bytes 131104 | tf_op jit(solution)/shard_map/ppermute | solution.py:509
  90.0 2.4 %collective-permute-done.8.refs_1_ = f32[4,64,128]{2,1,0:T(8,128)S(1)} collective-permute-done((f32[4,64,128]{2,1,0:T(8,128)S(1)}, f32[4,64,128]{2,1,0:T(8,128)S(1)}, u32[]{:S(2)}, u32[]{:S(2)}) %collective-permute-start.8) | collective-permute-done | bytes 131104 | tf_op jit(solution)/shard_map/ppermute | solution.py:509
  92.4 0.3 collective-permute-done.9.refs_2_
  92.7 0.9 join.1
  93.5 0.0 all-to-all-done.1
  93.5 0.6 reduce_sum.9
  (3 shorter events, 0.0 us)
Async XLA Ops:
  4.5 21.9 %collective-permute-start = (f32[153,8,128]{2,1,0:T(8,128)}, f32[153,8,128]{2,1,0:T(8,128)S(1)}, u32[]{:S(2)}, u32[]{:S(2)}) collective-permute-start(f32[153,8,128]{2,1,0:T(8,128)} %get-tuple-element.12.refs_1_), channel_id=1, source_target_pairs={{0,8},{8,0},{16,24},{24,16},{1,9},{9,1},{17,25},{25,17},{2,10},{10... | collective-permute-start | bytes 1880072 | tf_op jit(solution)/shard_map/ppermute | solution.py:509
  7.5 31.2 %collective-permute-start.1 = (f32[153,8,128]{2,1,0:T(8,128)}, f32[153,8,128]{2,1,0:T(8,128)S(1)}, u32[]{:S(2)}, u32[]{:S(2)}) collective-permute-start(f32[153,8,128]{2,1,0:T(8,128)} %get-tuple-element.13.refs_2_), channel_id=1, source_target_pairs={{0,16},{8,24},{16,0},{24,8},{1,17},{9,25},{17,1},{25,9},{2,18},{10... | collective-permute-start | bytes 1880072 | tf_op jit(solution)/shard_map/ppermute | solution.py:509
  9.0 29.6 %collective-permute-start.2 = (f32[153,8,128]{2,1,0:T(8,128)}, f32[153,8,128]{2,1,0:T(8,128)S(1)}, u32[]{:S(2)}, u32[]{:S(2)}) collective-permute-start(f32[153,8,128]{2,1,0:T(8,128)} %get-tuple-element.14.refs_3_), channel_id=1, source_target_pairs={{0,24},{8,16},{16,8},{24,0},{1,25},{9,17},{17,9},{25,1},{2,26},{10... | collective-permute-start | bytes 1880072 | tf_op jit(solution)/shard_map/ppermute | solution.py:509
  9.0 1.1 %copy-start = (f32[153,8,128]{2,1,0:T(8,128)S(1)}, f32[153,8,128]{2,1,0:T(8,128)}, u32[]{:S(2)}) copy-start(f32[153,8,128]{2,1,0:T(8,128)} %get-tuple-element.11.refs_0_) | copy-start | bytes 1880068
  10.1 1.1 %copy-start.3 = (f32[153,8,128]{2,1,0:T(8,128)S(1)}, f32[153,8,128]{2,1,0:T(8,128)}, u32[]{:S(2)}) copy-start(f32[153,8,128]{2,1,0:T(8,128)} %get-tuple-element.14.refs_3_) | copy-start | bytes 1880068
  11.2 1.1 %copy-start.4 = (f32[153,8,128]{2,1,0:T(8,128)S(1)}, f32[153,8,128]{2,1,0:T(8,128)}, u32[]{:S(2)}) copy-start(f32[153,8,128]{2,1,0:T(8,128)} %get-tuple-element.13.refs_2_) | copy-start | bytes 1880068
  12.2 1.1 %copy-start.5 = (f32[153,8,128]{2,1,0:T(8,128)S(1)}, f32[153,8,128]{2,1,0:T(8,128)}, u32[]{:S(2)}) copy-start(f32[153,8,128]{2,1,0:T(8,128)} %get-tuple-element.12.refs_1_) | copy-start | bytes 1880068
  13.3 0.7 copy-start.7
  14.0 24.7 %copy-start.1 = (f32[153,8,128]{2,1,0:T(8,128)S(1)}, f32[153,8,128]{2,1,0:T(8,128)}, u32[]{:S(2)}) copy-start(f32[153,8,128]{2,1,0:T(8,128)} %get-tuple-element.11.refs_0_) | copy-start | bytes 1880068
  16.9 55.1 %copy-start.6 = (s32[32]{0:T(128)S(1)}, s32[32]{0:T(128)}, u32[]{:S(2)}) copy-start(s32[32]{0:T(128)} %owner_ref.1) | copy-start | bytes 388
  16.9 5.8 %collective-permute-start.3 = (f32[21,8,128]{2,1,0:T(8,128)S(1)}, f32[21,8,128]{2,1,0:T(8,128)S(1)}, u32[]{:S(2)}, u32[]{:S(2)}) collective-permute-start(f32[21,8,128]{2,1,0:T(8,128)S(1)} %get-tuple-element.24), channel_id=1, source_target_pairs={{0,1},{1,2},{2,3},{3,4},{4,5},{5,6},{6,7},{7,0},{8,9},{9,10},{10,1... | collective-permute-start | bytes 258056 | tf_op jit(solution)/shard_map/ppermute | solution.py:539
  17.0 5.7 %collective-permute-start.4 = (f32[21,8,128]{2,1,0:T(8,128)S(1)}, f32[21,8,128]{2,1,0:T(8,128)S(1)}, u32[]{:S(2)}, u32[]{:S(2)}) collective-permute-start(f32[21,8,128]{2,1,0:T(8,128)S(1)} %get-tuple-element.25), channel_id=1, source_target_pairs={{1,0},{2,1},{3,2},{4,3},{5,4},{6,5},{7,6},{0,7},{9,8},{10,9},{11,1... | collective-permute-start | bytes 258056 | tf_op jit(solution)/shard_map/ppermute | solution.py:540
  22.8 30.0 %collective-permute-start.5 = (f32[21,8,128]{2,1,0:T(8,128)S(1)}, f32[21,8,128]{2,1,0:T(8,128)S(1)}, u32[]{:S(2)}, u32[]{:S(2)}) collective-permute-start(f32[21,8,128]{2,1,0:T(8,128)S(1)} %get-tuple-element.22), channel_id=1, source_target_pairs={{0,8},{8,0},{16,24},{24,16},{1,9},{9,1},{17,25},{25,17},{2,10},{10... | collective-permute-start | bytes 258056 | tf_op jit(solution)/shard_map/ppermute | solution.py:509
  24.8 28.0 %collective-permute-start.6 = (f32[21,8,128]{2,1,0:T(8,128)S(1)}, f32[21,8,128]{2,1,0:T(8,128)S(1)}, u32[]{:S(2)}, u32[]{:S(2)}) collective-permute-start(f32[21,8,128]{2,1,0:T(8,128)S(1)} %get-tuple-element.21), channel_id=1, source_target_pairs={{0,16},{8,24},{16,0},{24,8},{1,17},{9,25},{17,1},{25,9},{2,18},{10... | collective-permute-start | bytes 258056 | tf_op jit(solution)/shard_map/ppermute | solution.py:509
  26.3 26.5 %collective-permute-start.7 = (f32[21,8,128]{2,1,0:T(8,128)S(1)}, f32[21,8,128]{2,1,0:T(8,128)S(1)}, u32[]{:S(2)}, u32[]{:S(2)}) collective-permute-start(f32[21,8,128]{2,1,0:T(8,128)S(1)} %get-tuple-element.20), channel_id=1, source_target_pairs={{0,24},{8,16},{16,8},{24,0},{1,25},{9,17},{17,9},{25,1},{2,26},{10... | collective-permute-start | bytes 258056 | tf_op jit(solution)/shard_map/ppermute | solution.py:509
  63.7 8.3 %all-to-all-start = ((f32[4,8,128]{2,1,0:T(8,128)}), f32[4,8,128]{2,1,0:T(8,128)S(1)}, u32[]{:S(2)}, u32[]{:S(2)}) async-start(f32[4,8,128]{2,1,0:T(8,128)} %get-tuple-element.19), calls=%async_computation | async-start | bytes 32768 | tf_op jit(solution)/shard_map/all_to_all | solution.py:572
  72.0 2.2 %copy-start.2 = (bf16[1,8,4,256,256]{4,3,2,1,0:T(8,128)(2,1)S(1)}, bf16[1,8,4,256,256]{4,3,2,1,0:T(8,128)(2,1)}, u32[]{:S(2)}) copy-start(bf16[1,8,4,256,256]{4,3,2,1,0:T(8,128)(2,1)} %param.11) | copy-start | bytes 12582916
  76.7 16.9 %all-to-all-start.1 = ((f32[32,8,256]{2,1,0:T(8,128)}), f32[32,8,256]{2,1,0:T(8,128)S(1)}, u32[]{:S(2)}, u32[]{:S(2)}) async-start(f32[32,8,256]{2,1,0:T(8,128)} %listen.1), calls=%async_computation.1 | async-start | bytes 524288 | tf_op jit(solution)/shard_map/all_to_all | solution.py:586
  80.7 9.3 %collective-permute-start.10 = (f32[4,64,128]{2,1,0:T(8,128)S(1)}, f32[4,64,128]{2,1,0:T(8,128)S(1)}, u32[]{:S(2)}, u32[]{:S(2)}) collective-permute-start(f32[4,64,128]{2,1,0:T(8,128)S(1)} %get-tuple-element.18), channel_id=1, source_target_pairs={{0,24},{8,16},{16,8},{24,0},{1,25},{9,17},{17,9},{25,1},{2,26},{10... | collective-permute-start | bytes 393224 | tf_op jit(solution)/shard_map/ppermute | solution.py:509
  83.4 9.0 %collective-permute-start.8 = (f32[4,64,128]{2,1,0:T(8,128)S(1)}, f32[4,64,128]{2,1,0:T(8,128)S(1)}, u32[]{:S(2)}, u32[]{:S(2)}) collective-permute-start(f32[4,64,128]{2,1,0:T(8,128)S(1)} %get-tuple-element.16), channel_id=1, source_target_pairs={{0,8},{8,0},{16,24},{24,16},{1,9},{9,1},{17,25},{25,17},{2,10},{10... | collective-permute-start | bytes 393224 | tf_op jit(solution)/shard_map/ppermute | solution.py:509
  84.0 8.7 %collective-permute-start.9 = (f32[4,64,128]{2,1,0:T(8,128)S(1)}, f32[4,64,128]{2,1,0:T(8,128)S(1)}, u32[]{:S(2)}, u32[]{:S(2)}) collective-permute-start(f32[4,64,128]{2,1,0:T(8,128)S(1)} %get-tuple-element.17), channel_id=1, source_target_pairs={{0,16},{8,24},{16,0},{24,8},{1,17},{9,25},{17,1},{25,9},{2,18},{10... | collective-permute-start | bytes 393224 | tf_op jit(solution)/shard_map/ppermute | solution.py:509

commit v4 on v3

--- a/solution.py
+++ b/solution.py
@@ -12,7 +12,7 @@
 HALO = STEPS
 LANES = 128
 RELAX = 1.6
-UNROLL = 4
+UNROLL = 16
 
 VELOCITIES = (
     (0, 0, 0),
@@ -303,13 +303,20 @@
 
     def fill(k, carry, last=False):
         rows_of = [plane_rows(blocks[m], k, last) for m in range(n)]
-        strips = [edges[m][k] for m in range(n)]
+        strips = [roll(edges[m][k], home(m)[0] * group, 1) for m in range(n)]
         for r in range(8):
             left = right = None
+            begin = r * 2 * HALO
+            beside = None
+            for m in range(n):
+                first = begin + home(m)[0] * group
+                offset = jnp.bitwise_and(lane - first, LANES - 1)
+                beside = strips[m] if beside is None else jnp.where(offset < 2 * HALO, strips[m], beside)
+            beside = roll(beside, HALO - begin, 1)
             for m in range(n):
                 at, base = home(m)
                 v = roll(ends_joined(rows_of[m][r], width, 2 * HALO), at * group + 2 * HALO, 1)
-                e = roll(strips[m], at * group + HALO - r * 2 * HALO, 1)
+                e = beside if whole else roll(edges[m][k], at * group + HALO - begin, 1)
                 a, b = jnp.where(at_left, e, v), jnp.where(at_right, e, v)
                 if not whole:
                     row = base + r + 1
@@ -444,7 +451,7 @@
             signal[at, pl.ds(b, LANES)] = (sums[0] + sums[1]) + (sums[2] + sums[3])
         return c
 
-    lax.fori_loop(0, listeners // 16, rows, 0)
+    lax.fori_loop(0, listeners // 16, rows, 0, unroll=2)
 
     def move(t, c):
         out[t] = signal[pl.ds(pl.multiple_of(owner_ref[t] * block, block), block), :]

time: 94.7 us -> 87.4 us (0.923)
  Pallas kernels: 35 us -> 27.7 us
    pallas_call x6, Pallas kernels: 35 us -> 27.7 us  [call(): pl.pallas_call(kernel, out_shape=out_shape, in_specs=specs, out_specs=[VM...]
  transfers between devices with their start and end apart: 13 -> 13, of which waited for: 6 -> 6; matrix products, arithmetic and copies ran while one was open for 0% -> 0% of each run, Pallas kernels for 19% -> 16%
where the time goes in v4:
time: 87.4 us; the launch traced here: 86.9 us
  Pallas kernels  27.7 us (32%)
  waiting for transfers between devices  27 us (31%)
  starting transfers between devices  22.9 us (26%)
  local copies, waits for them, and re-layouts  7.17 us (8%)
  between operations  1.39 us (2%)
    pallas_call x6, Pallas kernels, call(): pl.pallas_call(kernel, out_shape=out_shape, in_specs=specs, out_specs=[VM...  27.7 us
    ppermute x9, waiting for transfers between devices, exchange(): lax.ppermute(parts[m], 'gx', swap[m])  20.7 us
    ppermute x9, starting transfers between devices, exchange(): lax.ppermute(parts[m], 'gx', swap[m])  11.7 us
    unnamed x16, local copies, waits for them, and re-layouts  7.16 us
    all_to_all x1, waiting for transfers between devices, on_device(): picks = lax.all_to_all(picks, 'gx', 0, 0, tiled=True)  4.06 us
    all_to_all x1, starting transfers between devices, on_device(): gathered = lax.all_to_all(partial_signal, ('gx', 'gy'), 0, 0, tiled=True)  4.01 us
    all_to_all x1, starting transfers between devices, on_device(): picks = lax.all_to_all(picks, 'gx', 0, 0, tiled=True)  3.61 us
    ppermute x1, starting transfers between devices, on_device(): after = lax.ppermute(strips[0], 'gy', down)  3.53 us
  transfers between devices with their start and end apart: 13, of which 6 were waited for; matrix products, arithmetic and copies ran while one was open for 0% of the time, Pallas kernels for 16%

profile of v4, /device:TPU:0, one launch (start us, length us, event | category | flops | bytes accessed | tf_op | source)
XLA Modules:
  0.0 86.9 jit_solution(15440076042359207762)
XLA Ops:
  0.6 3.8 %pack.1 = (f32[153,8,128]{2,1,0:T(8,128)}, f32[153,8,128]{2,1,0:T(8,128)}, f32[153,8,128]{2,1,0:T(8,128)}, f32[153,8,128]{2,1,0:T(8,128)}) custom-call(s32[1]{0:T(128)} %bitcast.me_ref, f32[19,64,512]{2,1,0:T(8,128)} %bitcast.26, s32[64,512]{1,0:T(8,128)} %bitcast.28), custom_call_target="tpu_custom_call" | custom-call | tf_op jit(solution)/shard_map/pack/pallas_call | solution.py:492
  4.5 3.0 %collective-permute-start = (f32[153,8,128]{2,1,0:T(8,128)}, f32[153,8,128]{2,1,0:T(8,128)S(1)}, u32[]{:S(2)}, u32[]{:S(2)}) collective-permute-start(f32[153,8,128]{2,1,0:T(8,128)} %get-tuple-element.12.refs_1_), channel_id=1, source_target_pairs={{0,8},{8,0},{16,24},{24,16},{1,9},{9,1},{17,25},{25,17},{2,10},{10... | collective-permute-start | bytes 1880072 | tf_op jit(solution)/shard_map/ppermute | solution.py:516
  7.5 1.5 %collective-permute-start.1 = (f32[153,8,128]{2,1,0:T(8,128)}, f32[153,8,128]{2,1,0:T(8,128)S(1)}, u32[]{:S(2)}, u32[]{:S(2)}) collective-permute-start(f32[153,8,128]{2,1,0:T(8,128)} %get-tuple-element.13.refs_2_), channel_id=1, source_target_pairs={{0,16},{8,24},{16,0},{24,8},{1,17},{9,25},{17,1},{25,9},{2,18},{10... | collective-permute-start | bytes 1880072 | tf_op jit(solution)/shard_map/ppermute | solution.py:516
  9.0 0.0 collective-permute-start.2
  9.0 0.0 copy-start
  9.0 1.1 %copy-done = f32[153,8,128]{2,1,0:T(8,128)S(1)} copy-done((f32[153,8,128]{2,1,0:T(8,128)S(1)}, f32[153,8,128]{2,1,0:T(8,128)}, u32[]{:S(2)}) %copy-start) | copy-done | bytes 626712
  10.1 0.0 copy-start.3
  10.1 1.1 %copy-done.3 = f32[153,8,128]{2,1,0:T(8,128)S(1)} copy-done((f32[153,8,128]{2,1,0:T(8,128)S(1)}, f32[153,8,128]{2,1,0:T(8,128)}, u32[]{:S(2)}) %copy-start.3) | copy-done | bytes 626712
  11.2 0.0 copy-start.4
  11.2 1.1 %copy-done.4 = f32[153,8,128]{2,1,0:T(8,128)S(1)} copy-done((f32[153,8,128]{2,1,0:T(8,128)S(1)}, f32[153,8,128]{2,1,0:T(8,128)}, u32[]{:S(2)}) %copy-start.4) | copy-done | bytes 626712
  12.2 0.0 copy-start.5
  12.2 1.1 %copy-done.5 = f32[153,8,128]{2,1,0:T(8,128)S(1)} copy-done((f32[153,8,128]{2,1,0:T(8,128)S(1)}, f32[153,8,128]{2,1,0:T(8,128)}, u32[]{:S(2)}) %copy-start.5) | copy-done | bytes 626712
  13.3 0.0 copy-start.7
  13.3 0.7 copy-done.7
  14.0 2.9 %edges.1 = f32[6,21,8,128]{3,2,1,0:T(8,128)S(1)} custom-call(s32[1]{0:T(128)} %bitcast.me_ref, s32[1,8]{1,0:T(1,128)S(1)} %copy-done.7, f32[153,8,128]{2,1,0:T(8,128)S(1)} %copy-done, f32[153,8,128]{2,1,0:T(8,128)S(1)} %copy-done.5, f32[153,8,128]{2,1,0:T(8,128)S(1)} %copy-done.4, f32[153,8,128]{2,1,0:T(8,128)S(1)} %copy-done.3), custom_call_target="tpu_custom_call" | custom-call | tf_op jit(solution)/shard_map/edges/pallas_call | solution.py:492
  16.9 0.0 copy-start.6
  16.9 0.1 collective-permute-start.3
  17.0 3.5 %collective-permute-start.4 = (f32[21,8,128]{2,1,0:T(8,128)S(1)}, f32[21,8,128]{2,1,0:T(8,128)S(1)}, u32[]{:S(2)}, u32[]{:S(2)}) collective-permute-start(f32[21,8,128]{2,1,0:T(8,128)S(1)} %get-tuple-element.25), channel_id=1, source_target_pairs={{1,0},{2,1},{3,2},{4,3},{5,4},{6,5},{7,6},{0,7},{9,8},{10,9},{11,1... | collective-permute-start | bytes 258056 | tf_op jit(solution)/shard_map/ppermute | solution.py:547
  20.5 2.2 %collective-permute-done.3 = f32[21,8,128]{2,1,0:T(8,128)S(1)} collective-permute-done((f32[21,8,128]{2,1,0:T(8,128)S(1)}, f32[21,8,128]{2,1,0:T(8,128)S(1)}, u32[]{:S(2)}, u32[]{:S(2)}) %collective-permute-start.3) | collective-permute-done | bytes 86048 | tf_op jit(solution)/shard_map/ppermute | solution.py:546
  22.7 0.0 collective-permute-done.4
  22.7 0.1 fusion
  22.8 2.1 %collective-permute-start.5 = (f32[21,8,128]{2,1,0:T(8,128)S(1)}, f32[21,8,128]{2,1,0:T(8,128)S(1)}, u32[]{:S(2)}, u32[]{:S(2)}) collective-permute-start(f32[21,8,128]{2,1,0:T(8,128)S(1)} %get-tuple-element.22), channel_id=1, source_target_pairs={{0,8},{8,0},{16,24},{24,16},{1,9},{9,1},{17,25},{25,17},{2,10},{10... | collective-permute-start | bytes 258056 | tf_op jit(solution)/shard_map/ppermute | solution.py:516
  24.8 1.5 %collective-permute-start.6 = (f32[21,8,128]{2,1,0:T(8,128)S(1)}, f32[21,8,128]{2,1,0:T(8,128)S(1)}, u32[]{:S(2)}, u32[]{:S(2)}) collective-permute-start(f32[21,8,128]{2,1,0:T(8,128)S(1)} %get-tuple-element.21), channel_id=1, source_target_pairs={{0,16},{8,24},{16,0},{24,8},{1,17},{9,25},{17,1},{25,9},{2,18},{10... | collective-permute-start | bytes 258056 | tf_op jit(solution)/shard_map/ppermute | solution.py:516
  26.3 0.0 collective-permute-done.refs_1_
  26.3 0.0 collective-permute-start.7
  26.4 12.3 %collective-permute-done.1.refs_2_ = f32[153,8,128]{2,1,0:T(8,128)S(1)} collective-permute-done((f32[153,8,128]{2,1,0:T(8,128)}, f32[153,8,128]{2,1,0:T(8,128)S(1)}, u32[]{:S(2)}, u32[]{:S(2)}) %collective-permute-start.1) | collective-permute-done | bytes 626720 | tf_op jit(solution)/shard_map/ppermute | solution.py:516
  38.6 0.0 collective-permute-done.2.refs_3_
  38.6 0.0 copy-done.1
  38.6 10.2 %flow.1.refs_8_ = f32[4,32,8,128]{3,2,1,0:T(8,128)S(1)} custom-call(s32[1]{0:T(128)} %bitcast.me_ref, f32[153,8,128]{2,1,0:T(8,128)S(1)} %copy-done.1, f32[153,8,128]{2,1,0:T(8,128)S(1)} %collective-permute-done.refs_1_, f32[153,8,128]{2,1,0:T(8,128)S(1)} %collective-permute-done.1.refs_2_, f32[153,8,128]{2,1,0:T(8,128)S(1)} %collective-permute-done.2.refs_3_), custom_call_target="tpu_custom_call" | custom-call | bytes 76546048 | tf_op jit(solution)/shard_map/flow/pallas_call | solution.py:492
  48.9 0.0 collective-permute-done.5.refs_5_
  48.9 0.0 collective-permute-done.6.refs_6_
  48.9 0.0 collective-permute-done.7.refs_7_
  48.9 7.6 %seam.1 = (f32[4,64,128]{2,1,0:T(8,128)S(1)}, f32[4,64,128]{2,1,0:T(8,128)S(1)}, f32[4,64,128]{2,1,0:T(8,128)S(1)}, f32[4,64,128]{2,1,0:T(8,128)S(1)}, f32[4,8,128]{2,1,0:T(8,128)}) custom-call(s32[1]{0:T(128)} %bitcast.me_ref, f32[153,8,128]{2,1,0:T(8,128)S(1)} %copy-done.1, f32[153,8,128]{2,1,0:T(8,128)S(1)} %collective-permute-done.refs_1_, ...), custom_call_target="tpu_custom_call" | custom-call | bytes 38273024 | tf_op jit(solution)/shard_map/seam/pallas_call | solution.py:492
  56.4 3.6 %all-to-all-start = ((f32[4,8,128]{2,1,0:T(8,128)}), f32[4,8,128]{2,1,0:T(8,128)S(1)}, u32[]{:S(2)}, u32[]{:S(2)}) async-start(f32[4,8,128]{2,1,0:T(8,128)} %get-tuple-element.19), calls=%async_computation | async-start | bytes 32768 | tf_op jit(solution)/shard_map/all_to_all | solution.py:579
  60.7 4.1 %all-to-all-done.picks = f32[4,8,128]{2,1,0:T(8,128)S(1)} async-done(((f32[4,8,128]{2,1,0:T(8,128)}), f32[4,8,128]{2,1,0:T(8,128)S(1)}, u32[]{:S(2)}, u32[]{:S(2)}) %all-to-all-start) | async-done | bytes 16416 | tf_op jit(solution)/shard_map/all_to_all | solution.py:579
  64.8 0.0 copy-done.6
  64.8 2.2 %copy-done.2 = bf16[1,8,4,256,256]{4,3,2,1,0:T(8,128)(2,1)S(1)} copy-done((bf16[1,8,4,256,256]{4,3,2,1,0:T(8,128)(2,1)S(1)}, bf16[1,8,4,256,256]{4,3,2,1,0:T(8,128)(2,1)}, u32[]{:S(2)}) %copy-start.2) | copy-done | bytes 4194328
  67.0 2.4 %listen.1 = f32[32,8,256]{2,1,0:T(8,128)} custom-call(s32[1]{0:T(128)S(6)} %copy.8.count_ref, s32[32]{0:T(128)S(1)} %copy-done.6, f32[4,8,128]{2,1,0:T(8,128)S(1)} %all-to-all-done.picks, bf16[32,256,256]{2,1,0:T(8,128)(2,1)S(1)} %bitcast.25), custom_call_target="tpu_custom_call" | custom-call | tf_op jit(solution)/shard_map/listen/pallas_call | solution.py:492
  69.4 4.0 %all-to-all-start.1 = ((f32[32,8,256]{2,1,0:T(8,128)}), f32[32,8,256]{2,1,0:T(8,128)S(1)}, u32[]{:S(2)}, u32[]{:S(2)}) async-start(f32[32,8,256]{2,1,0:T(8,128)} %listen.1), calls=%async_computation.1 | async-start | bytes 524288 | tf_op jit(solution)/shard_map/all_to_all | solution.py:593
  73.4 2.7 %collective-permute-start.10 = (f32[4,64,128]{2,1,0:T(8,128)S(1)}, f32[4,64,128]{2,1,0:T(8,128)S(1)}, u32[]{:S(2)}, u32[]{:S(2)}) collective-permute-start(f32[4,64,128]{2,1,0:T(8,128)S(1)} %get-tuple-element.18), channel_id=1, source_target_pairs={{0,24},{8,16},{16,8},{24,0},{1,25},{9,17},{17,9},{25,1},{2,26},{10... | collective-permute-start | bytes 393224 | tf_op jit(solution)/shard_map/ppermute | solution.py:516
  76.1 0.6 collective-permute-start.8
  76.7 0.3 collective-permute-start.9
  76.9 5.7 %collective-permute-done.10.refs_3_ = f32[4,64,128]{2,1,0:T(8,128)S(1)} collective-permute-done((f32[4,64,128]{2,1,0:T(8,128)S(1)}, f32[4,64,128]{2,1,0:T(8,128)S(1)}, u32[]{:S(2)}, u32[]{:S(2)}) %collective-permute-start.10) | collective-permute-done | bytes 131104 | tf_op jit(solution)/shard_map/ppermute | solution.py:516
  82.6 2.4 %collective-permute-done.8.refs_1_ = f32[4,64,128]{2,1,0:T(8,128)S(1)} collective-permute-done((f32[4,64,128]{2,1,0:T(8,128)S(1)}, f32[4,64,128]{2,1,0:T(8,128)S(1)}, u32[]{:S(2)}, u32[]{:S(2)}) %collective-permute-start.8) | collective-permute-done | bytes 131104 | tf_op jit(solution)/shard_map/ppermute | solution.py:516
  85.1 0.3 collective-permute-done.9.refs_2_
  85.4 0.9 join.1
  86.2 0.0 all-to-all-done.1
  86.2 0.6 reduce_sum.9
  (3 shorter events, 0.0 us)
Async XLA Ops:
  4.5 21.9 %collective-permute-start = (f32[153,8,128]{2,1,0:T(8,128)}, f32[153,8,128]{2,1,0:T(8,128)S(1)}, u32[]{:S(2)}, u32[]{:S(2)}) collective-permute-start(f32[153,8,128]{2,1,0:T(8,128)} %get-tuple-element.12.refs_1_), channel_id=1, source_target_pairs={{0,8},{8,0},{16,24},{24,16},{1,9},{9,1},{17,25},{25,17},{2,10},{10... | collective-permute-start | bytes 1880072 | tf_op jit(solution)/shard_map/ppermute | solution.py:516
  7.5 31.2 %collective-permute-start.1 = (f32[153,8,128]{2,1,0:T(8,128)}, f32[153,8,128]{2,1,0:T(8,128)S(1)}, u32[]{:S(2)}, u32[]{:S(2)}) collective-permute-start(f32[153,8,128]{2,1,0:T(8,128)} %get-tuple-element.13.refs_2_), channel_id=1, source_target_pairs={{0,16},{8,24},{16,0},{24,8},{1,17},{9,25},{17,1},{25,9},{2,18},{10... | collective-permute-start | bytes 1880072 | tf_op jit(solution)/shard_map/ppermute | solution.py:516
  9.0 29.6 %collective-permute-start.2 = (f32[153,8,128]{2,1,0:T(8,128)}, f32[153,8,128]{2,1,0:T(8,128)S(1)}, u32[]{:S(2)}, u32[]{:S(2)}) collective-permute-start(f32[153,8,128]{2,1,0:T(8,128)} %get-tuple-element.14.refs_3_), channel_id=1, source_target_pairs={{0,24},{8,16},{16,8},{24,0},{1,25},{9,17},{17,9},{25,1},{2,26},{10... | collective-permute-start | bytes 1880072 | tf_op jit(solution)/shard_map/ppermute | solution.py:516
  9.0 1.1 %copy-start = (f32[153,8,128]{2,1,0:T(8,128)S(1)}, f32[153,8,128]{2,1,0:T(8,128)}, u32[]{:S(2)}) copy-start(f32[153,8,128]{2,1,0:T(8,128)} %get-tuple-element.11.refs_0_) | copy-start | bytes 1880068
  10.1 1.1 %copy-start.3 = (f32[153,8,128]{2,1,0:T(8,128)S(1)}, f32[153,8,128]{2,1,0:T(8,128)}, u32[]{:S(2)}) copy-start(f32[153,8,128]{2,1,0:T(8,128)} %get-tuple-element.14.refs_3_) | copy-start | bytes 1880068
  11.2 1.1 %copy-start.4 = (f32[153,8,128]{2,1,0:T(8,128)S(1)}, f32[153,8,128]{2,1,0:T(8,128)}, u32[]{:S(2)}) copy-start(f32[153,8,128]{2,1,0:T(8,128)} %get-tuple-element.13.refs_2_) | copy-start | bytes 1880068
  12.2 1.1 %copy-start.5 = (f32[153,8,128]{2,1,0:T(8,128)S(1)}, f32[153,8,128]{2,1,0:T(8,128)}, u32[]{:S(2)}) copy-start(f32[153,8,128]{2,1,0:T(8,128)} %get-tuple-element.12.refs_1_) | copy-start | bytes 1880068
  13.3 0.7 copy-start.7
  14.0 24.7 %copy-start.1 = (f32[153,8,128]{2,1,0:T(8,128)S(1)}, f32[153,8,128]{2,1,0:T(8,128)}, u32[]{:S(2)}) copy-start(f32[153,8,128]{2,1,0:T(8,128)} %get-tuple-element.11.refs_0_) | copy-start | bytes 1880068
  16.9 47.9 %copy-start.6 = (s32[32]{0:T(128)S(1)}, s32[32]{0:T(128)}, u32[]{:S(2)}) copy-start(s32[32]{0:T(128)} %owner_ref.1) | copy-start | bytes 388
  16.9 5.8 %collective-permute-start.3 = (f32[21,8,128]{2,1,0:T(8,128)S(1)}, f32[21,8,128]{2,1,0:T(8,128)S(1)}, u32[]{:S(2)}, u32[]{:S(2)}) collective-permute-start(f32[21,8,128]{2,1,0:T(8,128)S(1)} %get-tuple-element.24), channel_id=1, source_target_pairs={{0,1},{1,2},{2,3},{3,4},{4,5},{5,6},{6,7},{7,0},{8,9},{9,10},{10,1... | collective-permute-start | bytes 258056 | tf_op jit(solution)/shard_map/ppermute | solution.py:546
  17.0 5.7 %collective-permute-start.4 = (f32[21,8,128]{2,1,0:T(8,128)S(1)}, f32[21,8,128]{2,1,0:T(8,128)S(1)}, u32[]{:S(2)}, u32[]{:S(2)}) collective-permute-start(f32[21,8,128]{2,1,0:T(8,128)S(1)} %get-tuple-element.25), channel_id=1, source_target_pairs={{1,0},{2,1},{3,2},{4,3},{5,4},{6,5},{7,6},{0,7},{9,8},{10,9},{11,1... | collective-permute-start | bytes 258056 | tf_op jit(solution)/shard_map/ppermute | solution.py:547
  22.8 26.1 %collective-permute-start.5 = (f32[21,8,128]{2,1,0:T(8,128)S(1)}, f32[21,8,128]{2,1,0:T(8,128)S(1)}, u32[]{:S(2)}, u32[]{:S(2)}) collective-permute-start(f32[21,8,128]{2,1,0:T(8,128)S(1)} %get-tuple-element.22), channel_id=1, source_target_pairs={{0,8},{8,0},{16,24},{24,16},{1,9},{9,1},{17,25},{25,17},{2,10},{10... | collective-permute-start | bytes 258056 | tf_op jit(solution)/shard_map/ppermute | solution.py:516
  24.8 24.0 %collective-permute-start.6 = (f32[21,8,128]{2,1,0:T(8,128)S(1)}, f32[21,8,128]{2,1,0:T(8,128)S(1)}, u32[]{:S(2)}, u32[]{:S(2)}) collective-permute-start(f32[21,8,128]{2,1,0:T(8,128)S(1)} %get-tuple-element.21), channel_id=1, source_target_pairs={{0,16},{8,24},{16,0},{24,8},{1,17},{9,25},{17,1},{25,9},{2,18},{10... | collective-permute-start | bytes 258056 | tf_op jit(solution)/shard_map/ppermute | solution.py:516
  26.3 22.5 %collective-permute-start.7 = (f32[21,8,128]{2,1,0:T(8,128)S(1)}, f32[21,8,128]{2,1,0:T(8,128)S(1)}, u32[]{:S(2)}, u32[]{:S(2)}) collective-permute-start(f32[21,8,128]{2,1,0:T(8,128)S(1)} %get-tuple-element.20), channel_id=1, source_target_pairs={{0,24},{8,16},{16,8},{24,0},{1,25},{9,17},{17,9},{25,1},{2,26},{10... | collective-permute-start | bytes 258056 | tf_op jit(solution)/shard_map/ppermute | solution.py:516
  56.4 8.3 %all-to-all-start = ((f32[4,8,128]{2,1,0:T(8,128)}), f32[4,8,128]{2,1,0:T(8,128)S(1)}, u32[]{:S(2)}, u32[]{:S(2)}) async-start(f32[4,8,128]{2,1,0:T(8,128)} %get-tuple-element.19), calls=%async_computation | async-start | bytes 32768 | tf_op jit(solution)/shard_map/all_to_all | solution.py:579
  64.8 2.2 %copy-start.2 = (bf16[1,8,4,256,256]{4,3,2,1,0:T(8,128)(2,1)S(1)}, bf16[1,8,4,256,256]{4,3,2,1,0:T(8,128)(2,1)}, u32[]{:S(2)}) copy-start(bf16[1,8,4,256,256]{4,3,2,1,0:T(8,128)(2,1)} %param.11) | copy-start | bytes 12582916
  69.4 16.9 %all-to-all-start.1 = ((f32[32,8,256]{2,1,0:T(8,128)}), f32[32,8,256]{2,1,0:T(8,128)S(1)}, u32[]{:S(2)}, u32[]{:S(2)}) async-start(f32[32,8,256]{2,1,0:T(8,128)} %listen.1), calls=%async_computation.1 | async-start | bytes 524288 | tf_op jit(solution)/shard_map/all_to_all | solution.py:593
  73.4 9.3 %collective-permute-start.10 = (f32[4,64,128]{2,1,0:T(8,128)S(1)}, f32[4,64,128]{2,1,0:T(8,128)S(1)}, u32[]{:S(2)}, u32[]{:S(2)}) collective-permute-start(f32[4,64,128]{2,1,0:T(8,128)S(1)} %get-tuple-element.18), channel_id=1, source_target_pairs={{0,24},{8,16},{16,8},{24,0},{1,25},{9,17},{17,9},{25,1},{2,26},{10... | collective-permute-start | bytes 393224 | tf_op jit(solution)/shard_map/ppermute | solution.py:516
  76.1 9.0 %collective-permute-start.8 = (f32[4,64,128]{2,1,0:T(8,128)S(1)}, f32[4,64,128]{2,1,0:T(8,128)S(1)}, u32[]{:S(2)}, u32[]{:S(2)}) collective-permute-start(f32[4,64,128]{2,1,0:T(8,128)S(1)} %get-tuple-element.16), channel_id=1, source_target_pairs={{0,8},{8,0},{16,24},{24,16},{1,9},{9,1},{17,25},{25,17},{2,10},{10... | collective-permute-start | bytes 393224 | tf_op jit(solution)/shard_map/ppermute | solution.py:516
  76.7 8.7 %collective-permute-start.9 = (f32[4,64,128]{2,1,0:T(8,128)S(1)}, f32[4,64,128]{2,1,0:T(8,128)S(1)}, u32[]{:S(2)}, u32[]{:S(2)}) collective-permute-start(f32[4,64,128]{2,1,0:T(8,128)S(1)} %get-tuple-element.17), channel_id=1, source_target_pairs={{0,16},{8,24},{16,0},{24,8},{1,17},{9,25},{17,1},{25,9},{2,18},{10... | collective-permute-start | bytes 393224 | tf_op jit(solution)/shard_map/ppermute | solution.py:516

commit v5 on v4

--- a/solution.py
+++ b/solution.py
@@ -152,7 +152,7 @@
                 blocks[m][k * 8 + r] = roll(out[k], turn, 1)
             return carry
 
-        lax.fori_loop(0, 8, row, 0, unroll=4)
+        lax.fori_loop(0, 8, row, 0, unroll=8)
     walls.wait()
     for m in order:
         dest = jnp.bitwise_xor(me, m) * width
@@ -400,7 +400,6 @@
                 fields[m][q, pl.ds(r, 8, stride=8), :] = v
                 column[m, q, pl.ds(r, 1), :] = jnp.sum(v, axis=0, keepdims=True) * (1.0 / 8.0)
     for m in range(n):
-        g = jnp.bitwise_xor(me, m)
         cells = edges[m][Q + 1]
         found = [None] * 4
         for p in range(8):
@@ -412,7 +411,7 @@
         result = jnp.zeros((8, LANES), F32)
         for q in range(4):
             result = jnp.where(lane == q, jnp.sum(found[q], axis=1, keepdims=True), result)
-        picks[g] = result
+        picks[m] = result
 
 
 def vectors(*sizes):
@@ -428,9 +427,7 @@
     tiles, block = out.shape[:2]
     sub = lax.broadcasted_iota(jnp.int32, (8, LANES), 0)
     lane = lane_iota()
-    total = picks[0]
-    for m in range(1, picks.shape[0]):
-        total = total + picks[m]
+    total = picks[...]
     total = total - jnp.where(lane == 0, 1.0, 0.0)
     total = jnp.where(sub < count_ref[0], total, 0.0)
     total = total.astype(jnp.bfloat16).astype(F32)
@@ -451,7 +448,7 @@
             signal[at, pl.ds(b, LANES)] = (sums[0] + sums[1]) + (sums[2] + sums[3])
         return c
 
-    lax.fori_loop(0, listeners // 16, rows, 0, unroll=2)
+    lax.fori_loop(0, listeners // 16, rows, 0, unroll=8)
 
     def move(t, c):
         out[t] = signal[pl.ds(pl.multiple_of(owner_ref[t] * block, block), block), :]
@@ -576,7 +573,15 @@
         work=STEPS * 16 * 73 * 4 * 8 * LANES,
     )
     weights = retarded.reshape(32, *retarded.shape[3:])
-    picks = lax.all_to_all(picks, "gx", 0, 0, tiled=True)
+    found = {m: picks[m] for m in range(n)}
+    bit = 1
+    while bit < n:
+        moving = [m for m in found if m & bit]
+        moved = lax.ppermute(jnp.stack([found.pop(m) for m in moving]), "gx", swap[bit])
+        for at, m in enumerate(moving):
+            found[m ^ bit] = found[m ^ bit] + moved[at]
+        bit *= 2
+    picks = found[0]
     parts = exchange(parts)
 
     listeners, bins = retarded.shape[3:]

time: 87.4 us -> 85.1 us (0.974)
  local copies, waits for them, and re-layouts: 7.17 us -> 4.99 us
    all_to_all x1 -> x0, waiting for transfers between devices: 4.06 us -> none  [on_device(): picks = lax.all_to_all(picks, 'gx', 0, 0, tiled=True)]
    ppermute x0 -> x2, waiting for transfers between devices: none -> 4.05 us  [on_device(): lax.ppermute(jnp.stack([found.pop(m) for m in moving]), 'gx', swap[bit])]
    all_to_all x1 -> x0, starting transfers between devices: 3.61 us -> none  [on_device(): picks = lax.all_to_all(picks, 'gx', 0, 0, tiled=True)]
    ppermute x0 -> x2, starting transfers between devices: none -> 2.92 us  [on_device(): lax.ppermute(jnp.stack([found.pop(m) for m in moving]), 'gx', swap[bit])]
    unnamed x16, local copies, waits for them, and re-layouts: 7.16 us -> 4.98 us
    all_to_all x1, starting transfers between devices: 4.01 us -> 5.43 us  [on_device(): gathered = lax.all_to_all(partial_signal, ('gx', 'gy'), 0, 0, tiled=True)]
  transfers between devices with their start and end apart: 13 -> 14, of which waited for: 6 -> 7; matrix products, arithmetic and copies ran while one was open for 0% -> 0% of each run, Pallas kernels for 16% -> 16%
where the time goes in v5:
time: 85.1 us; the launch traced here: 84.7 us
  Pallas kernels  27 us (32%)
  waiting for transfers between devices  27 us (32%)
  starting transfers between devices  23.6 us (28%)
  local copies, waits for them, and re-layouts  4.99 us (6%)
  between operations  1.4 us (2%)
    pallas_call x6, Pallas kernels, call(): pl.pallas_call(kernel, out_shape=out_shape, in_specs=specs, out_specs=[VM...  27 us
    ppermute x9, waiting for transfers between devices, exchange(): lax.ppermute(parts[m], 'gx', swap[m])  20.7 us
    ppermute x9, starting transfers between devices, exchange(): lax.ppermute(parts[m], 'gx', swap[m])  11.7 us
    all_to_all x1, starting transfers between devices, on_device(): gathered = lax.all_to_all(partial_signal, ('gx', 'gy'), 0, 0, tiled=True)  5.43 us
    unnamed x16, local copies, waits for them, and re-layouts  4.98 us
    ppermute x2, waiting for transfers between devices, on_device(): lax.ppermute(jnp.stack([found.pop(m) for m in moving]), 'gx', swap[bit])  4.05 us
    ppermute x1, starting transfers between devices, on_device(): after = lax.ppermute(strips[0], 'gy', down)  3.53 us
    ppermute x2, starting transfers between devices, on_device(): lax.ppermute(jnp.stack([found.pop(m) for m in moving]), 'gx', swap[bit])  2.92 us
  transfers between devices with their start and end apart: 14, of which 7 were waited for; matrix products, arithmetic and copies ran while one was open for 0% of the time, Pallas kernels for 16%

profile of v5, /device:TPU:0, one launch (start us, length us, event | category | flops | bytes accessed | tf_op | source)
XLA Modules:
  0.0 84.7 jit_solution(1087086432964096216)
XLA Ops:
  0.6 3.8 %pack.1 = (f32[153,8,128]{2,1,0:T(8,128)}, f32[153,8,128]{2,1,0:T(8,128)}, f32[153,8,128]{2,1,0:T(8,128)}, f32[153,8,128]{2,1,0:T(8,128)}) custom-call(s32[1]{0:T(128)} %bitcast.me_ref, f32[19,64,512]{2,1,0:T(8,128)} %bitcast.28, s32[64,512]{1,0:T(8,128)} %bitcast.30), custom_call_target="tpu_custom_call" | custom-call | tf_op jit(solution)/shard_map/pack/pallas_call | solution.py:489
  4.4 3.0 %collective-permute-start = (f32[153,8,128]{2,1,0:T(8,128)}, f32[153,8,128]{2,1,0:T(8,128)S(1)}, u32[]{:S(2)}, u32[]{:S(2)}) collective-permute-start(f32[153,8,128]{2,1,0:T(8,128)} %get-tuple-element.12.refs_1_), channel_id=1, source_target_pairs={{0,8},{8,0},{16,24},{24,16},{1,9},{9,1},{17,25},{25,17},{2,10},{10... | collective-permute-start | bytes 1880072 | tf_op jit(solution)/shard_map/ppermute | solution.py:513
  7.4 1.5 %collective-permute-start.1 = (f32[153,8,128]{2,1,0:T(8,128)}, f32[153,8,128]{2,1,0:T(8,128)S(1)}, u32[]{:S(2)}, u32[]{:S(2)}) collective-permute-start(f32[153,8,128]{2,1,0:T(8,128)} %get-tuple-element.13.refs_2_), channel_id=1, source_target_pairs={{0,16},{8,24},{16,0},{24,8},{1,17},{9,25},{17,1},{25,9},{2,18},{10... | collective-permute-start | bytes 1880072 | tf_op jit(solution)/shard_map/ppermute | solution.py:513
  8.9 0.0 collective-permute-start.2
  9.0 0.0 copy-start
  9.0 1.1 %copy-done = f32[153,8,128]{2,1,0:T(8,128)S(1)} copy-done((f32[153,8,128]{2,1,0:T(8,128)S(1)}, f32[153,8,128]{2,1,0:T(8,128)}, u32[]{:S(2)}) %copy-start) | copy-done | bytes 626712
  10.0 0.0 copy-start.3
  10.0 1.1 %copy-done.3 = f32[153,8,128]{2,1,0:T(8,128)S(1)} copy-done((f32[153,8,128]{2,1,0:T(8,128)S(1)}, f32[153,8,128]{2,1,0:T(8,128)}, u32[]{:S(2)}) %copy-start.3) | copy-done | bytes 626712
  11.1 0.0 copy-start.4
  11.1 1.1 %copy-done.4 = f32[153,8,128]{2,1,0:T(8,128)S(1)} copy-done((f32[153,8,128]{2,1,0:T(8,128)S(1)}, f32[153,8,128]{2,1,0:T(8,128)}, u32[]{:S(2)}) %copy-start.4) | copy-done | bytes 626712
  12.2 1.1 %copy-done.5 = f32[153,8,128]{2,1,0:T(8,128)S(1)} copy-done((f32[153,8,128]{2,1,0:T(8,128)S(1)}, f32[153,8,128]{2,1,0:T(8,128)}, u32[]{:S(2)}) %copy-start.5) | copy-done | bytes 626712
  13.3 0.7 copy-done.7
  13.9 2.9 %edges.1 = f32[6,21,8,128]{3,2,1,0:T(8,128)S(1)} custom-call(s32[1]{0:T(128)} %bitcast.me_ref, s32[1,8]{1,0:T(1,128)S(1)} %copy-done.7, f32[153,8,128]{2,1,0:T(8,128)S(1)} %copy-done, f32[153,8,128]{2,1,0:T(8,128)S(1)} %copy-done.5, f32[153,8,128]{2,1,0:T(8,128)S(1)} %copy-done.4, f32[153,8,128]{2,1,0:T(8,128)S(1)} %copy-done.3), custom_call_target="tpu_custom_call" | custom-call | tf_op jit(solution)/shard_map/edges/pallas_call | solution.py:489
  16.8 0.0 copy-start.6
  16.8 0.1 collective-permute-start.3
  16.9 3.5 %collective-permute-start.4 = (f32[21,8,128]{2,1,0:T(8,128)S(1)}, f32[21,8,128]{2,1,0:T(8,128)S(1)}, u32[]{:S(2)}, u32[]{:S(2)}) collective-permute-start(f32[21,8,128]{2,1,0:T(8,128)S(1)} %get-tuple-element.25), channel_id=1, source_target_pairs={{1,0},{2,1},{3,2},{4,3},{5,4},{6,5},{7,6},{0,7},{9,8},{10,9},{11,1... | collective-permute-start | bytes 258056 | tf_op jit(solution)/shard_map/ppermute | solution.py:544
  20.4 2.2 %collective-permute-done.3 = f32[21,8,128]{2,1,0:T(8,128)S(1)} collective-permute-done((f32[21,8,128]{2,1,0:T(8,128)S(1)}, f32[21,8,128]{2,1,0:T(8,128)S(1)}, u32[]{:S(2)}, u32[]{:S(2)}) %collective-permute-start.3) | collective-permute-done | bytes 86048 | tf_op jit(solution)/shard_map/ppermute | solution.py:543
  22.6 0.0 collective-permute-done.4
  22.6 0.1 fusion
  22.7 2.1 %collective-permute-start.5 = (f32[21,8,128]{2,1,0:T(8,128)S(1)}, f32[21,8,128]{2,1,0:T(8,128)S(1)}, u32[]{:S(2)}, u32[]{:S(2)}) collective-permute-start(f32[21,8,128]{2,1,0:T(8,128)S(1)} %get-tuple-element.22), channel_id=1, source_target_pairs={{0,8},{8,0},{16,24},{24,16},{1,9},{9,1},{17,25},{25,17},{2,10},{10... | collective-permute-start | bytes 258056 | tf_op jit(solution)/shard_map/ppermute | solution.py:513
  24.8 1.5 %collective-permute-start.6 = (f32[21,8,128]{2,1,0:T(8,128)S(1)}, f32[21,8,128]{2,1,0:T(8,128)S(1)}, u32[]{:S(2)}, u32[]{:S(2)}) collective-permute-start(f32[21,8,128]{2,1,0:T(8,128)S(1)} %get-tuple-element.21), channel_id=1, source_target_pairs={{0,16},{8,24},{16,0},{24,8},{1,17},{9,25},{17,1},{25,9},{2,18},{10... | collective-permute-start | bytes 258056 | tf_op jit(solution)/shard_map/ppermute | solution.py:513
  26.3 0.0 collective-permute-done.refs_1_
  26.3 0.0 collective-permute-start.7
  26.3 12.3 %collective-permute-done.1.refs_2_ = f32[153,8,128]{2,1,0:T(8,128)S(1)} collective-permute-done((f32[153,8,128]{2,1,0:T(8,128)}, f32[153,8,128]{2,1,0:T(8,128)S(1)}, u32[]{:S(2)}, u32[]{:S(2)}) %collective-permute-start.1) | collective-permute-done | bytes 626720 | tf_op jit(solution)/shard_map/ppermute | solution.py:513
  38.6 0.0 collective-permute-done.2.refs_3_
  38.6 0.0 copy-done.1
  38.6 10.2 %flow.1.refs_8_ = f32[4,32,8,128]{3,2,1,0:T(8,128)S(1)} custom-call(s32[1]{0:T(128)} %bitcast.me_ref, f32[153,8,128]{2,1,0:T(8,128)S(1)} %copy-done.1, f32[153,8,128]{2,1,0:T(8,128)S(1)} %collective-permute-done.refs_1_, f32[153,8,128]{2,1,0:T(8,128)S(1)} %collective-permute-done.1.refs_2_, f32[153,8,128]{2,1,0:T(8,128)S(1)} %collective-permute-done.2.refs_3_), custom_call_target="tpu_custom_call" | custom-call | bytes 76546048 | tf_op jit(solution)/shard_map/flow/pallas_call | solution.py:489
  48.8 0.0 collective-permute-done.5.refs_5_
  48.8 0.0 collective-permute-done.6.refs_6_
  48.8 0.0 collective-permute-done.7.refs_7_
  48.8 6.9 %seam.1 = (f32[4,64,128]{2,1,0:T(8,128)S(1)}, f32[4,64,128]{2,1,0:T(8,128)S(1)}, f32[4,64,128]{2,1,0:T(8,128)S(1)}, f32[4,64,128]{2,1,0:T(8,128)S(1)}, f32[4,8,128]{2,1,0:T(8,128)S(1)}) custom-call(s32[1]{0:T(128)} %bitcast.me_ref, f32[153,8,128]{2,1,0:T(8,128)S(1)} %copy-done.1, f32[153,8,128]{2,1,0:T(8,128)S(1)} %collective-permute-done.refs_1_, ...), custom_call_target="tpu_custom_call" | custom-call | bytes 38273024 | tf_op jit(solution)/shard_map/seam/pallas_call | solution.py:489
  55.8 0.6 collective-permute-start.11
  56.3 3.1 %collective-permute-done.11 = f32[2,8,128]{2,1,0:T(8,128)S(1)} collective-permute-done((f32[2,8,128]{2,1,0:T(8,128)S(1)}, f32[2,8,128]{2,1,0:T(8,128)S(1)}, u32[]{:S(2)}, u32[]{:S(2)}) %collective-permute-start.11) | collective-permute-done | bytes 8224 | tf_op jit(solution)/shard_map/ppermute | solution.py:580
  59.5 2.3 %collective-permute-start.12 = (f32[1,8,128]{2,1,0:T(8,128)S(1)}, f32[1,8,128]{2,1,0:T(8,128)S(1)}, u32[]{:S(2)}, u32[]{:S(2)}) collective-permute-start(f32[1,8,128]{2,1,0:T(8,128)S(1)} %slice_add_fusion), channel_id=1, source_target_pairs={{0,16},{8,24},{16,0},{24,8},{1,17},{9,25},{17,1},{25,9},{2,18},{10... | collective-permute-start | bytes 12296 | tf_op jit(solution)/shard_map/ppermute | solution.py:580
  62.5 0.9 %collective-permute-done.12 = f32[1,8,128]{2,1,0:T(8,128)S(1)} collective-permute-done((f32[1,8,128]{2,1,0:T(8,128)S(1)}, f32[1,8,128]{2,1,0:T(8,128)S(1)}, u32[]{:S(2)}, u32[]{:S(2)}) %collective-permute-start.12) | collective-permute-done | bytes 4128 | tf_op jit(solution)/shard_map/ppermute | solution.py:580
  63.4 0.0 copy-done.6
  63.4 0.0 copy-done.2
  63.4 2.3 %listen.1 = f32[32,8,256]{2,1,0:T(8,128)} custom-call(s32[1]{0:T(128)S(6)} %copy.8.count_ref, s32[32]{0:T(128)S(1)} %copy-done.6, f32[8,128]{1,0:T(8,128)S(1)} %fusion.5.picks, bf16[32,256,256]{2,1,0:T(8,128)(2,1)S(1)} %bitcast.27), custom_call_target="tpu_custom_call" | custom-call | tf_op jit(solution)/shard_map/listen/pallas_call | solution.py:489
  65.7 5.4 %all-to-all-start = ((f32[32,8,256]{2,1,0:T(8,128)}), f32[32,8,256]{2,1,0:T(8,128)S(1)}, u32[]{:S(2)}, u32[]{:S(2)}) async-start(f32[32,8,256]{2,1,0:T(8,128)} %listen.1), calls=%async_computation | async-start | bytes 524288 | tf_op jit(solution)/shard_map/all_to_all | solution.py:598
  71.2 2.7 %collective-permute-start.10 = (f32[4,64,128]{2,1,0:T(8,128)S(1)}, f32[4,64,128]{2,1,0:T(8,128)S(1)}, u32[]{:S(2)}, u32[]{:S(2)}) collective-permute-start(f32[4,64,128]{2,1,0:T(8,128)S(1)} %get-tuple-element.18), channel_id=1, source_target_pairs={{0,24},{8,16},{16,8},{24,0},{1,25},{9,17},{17,9},{25,1},{2,26},{10... | collective-permute-start | bytes 393224 | tf_op jit(solution)/shard_map/ppermute | solution.py:513
  73.9 0.6 collective-permute-start.8
  74.5 0.3 collective-permute-start.9
  74.7 5.7 %collective-permute-done.10.refs_3_ = f32[4,64,128]{2,1,0:T(8,128)S(1)} collective-permute-done((f32[4,64,128]{2,1,0:T(8,128)S(1)}, f32[4,64,128]{2,1,0:T(8,128)S(1)}, u32[]{:S(2)}, u32[]{:S(2)}) %collective-permute-start.10) | collective-permute-done | bytes 131104 | tf_op jit(solution)/shard_map/ppermute | solution.py:513
  80.4 2.4 %collective-permute-done.8.refs_1_ = f32[4,64,128]{2,1,0:T(8,128)S(1)} collective-permute-done((f32[4,64,128]{2,1,0:T(8,128)S(1)}, f32[4,64,128]{2,1,0:T(8,128)S(1)}, u32[]{:S(2)}, u32[]{:S(2)}) %collective-permute-start.8) | collective-permute-done | bytes 131104 | tf_op jit(solution)/shard_map/ppermute | solution.py:513
  82.9 0.3 collective-permute-done.9.refs_2_
  83.2 0.9 %join.1 = f32[4,64,512]{2,1,0:T(8,128)} custom-call(s32[1]{0:T(128)} %bitcast.me_ref, f32[4,64,128]{2,1,0:T(8,128)S(1)} %get-tuple-element.15.refs_0_, f32[4,64,128]{2,1,0:T(8,128)S(1)} %collective-permute-done.8.refs_1_, f32[4,64,128]{2,1,0:T(8,128)S(1)} %collective-permute-done.9.refs_2_, f32[4,64,128]{2,1,0:T(8,128)S(1)} %collective-permute-done.10.refs_3_), custom_call_target="tpu_custom_call" | custom-call | tf_op jit(solution)/shard_map/join/pallas_call | solution.py:489
  84.0 0.0 all-to-all-done
  84.0 0.6 reduce_sum.9
  (9 shorter events, 0.0 us)
Async XLA Ops:
  4.4 21.9 %collective-permute-start = (f32[153,8,128]{2,1,0:T(8,128)}, f32[153,8,128]{2,1,0:T(8,128)S(1)}, u32[]{:S(2)}, u32[]{:S(2)}) collective-permute-start(f32[153,8,128]{2,1,0:T(8,128)} %get-tuple-element.12.refs_1_), channel_id=1, source_target_pairs={{0,8},{8,0},{16,24},{24,16},{1,9},{9,1},{17,25},{25,17},{2,10},{10... | collective-permute-start | bytes 1880072 | tf_op jit(solution)/shard_map/ppermute | solution.py:513
  7.4 31.2 %collective-permute-start.1 = (f32[153,8,128]{2,1,0:T(8,128)}, f32[153,8,128]{2,1,0:T(8,128)S(1)}, u32[]{:S(2)}, u32[]{:S(2)}) collective-permute-start(f32[153,8,128]{2,1,0:T(8,128)} %get-tuple-element.13.refs_2_), channel_id=1, source_target_pairs={{0,16},{8,24},{16,0},{24,8},{1,17},{9,25},{17,1},{25,9},{2,18},{10... | collective-permute-start | bytes 1880072 | tf_op jit(solution)/shard_map/ppermute | solution.py:513
  8.9 29.6 %collective-permute-start.2 = (f32[153,8,128]{2,1,0:T(8,128)}, f32[153,8,128]{2,1,0:T(8,128)S(1)}, u32[]{:S(2)}, u32[]{:S(2)}) collective-permute-start(f32[153,8,128]{2,1,0:T(8,128)} %get-tuple-element.14.refs_3_), channel_id=1, source_target_pairs={{0,24},{8,16},{16,8},{24,0},{1,25},{9,17},{17,9},{25,1},{2,26},{10... | collective-permute-start | bytes 1880072 | tf_op jit(solution)/shard_map/ppermute | solution.py:513
  9.0 1.1 %copy-start = (f32[153,8,128]{2,1,0:T(8,128)S(1)}, f32[153,8,128]{2,1,0:T(8,128)}, u32[]{:S(2)}) copy-start(f32[153,8,128]{2,1,0:T(8,128)} %get-tuple-element.11.refs_0_) | copy-start | bytes 1880068
  10.0 1.1 %copy-start.3 = (f32[153,8,128]{2,1,0:T(8,128)S(1)}, f32[153,8,128]{2,1,0:T(8,128)}, u32[]{:S(2)}) copy-start(f32[153,8,128]{2,1,0:T(8,128)} %get-tuple-element.14.refs_3_) | copy-start | bytes 1880068
  11.1 1.1 %copy-start.4 = (f32[153,8,128]{2,1,0:T(8,128)S(1)}, f32[153,8,128]{2,1,0:T(8,128)}, u32[]{:S(2)}) copy-start(f32[153,8,128]{2,1,0:T(8,128)} %get-tuple-element.13.refs_2_) | copy-start | bytes 1880068
  12.2 1.1 %copy-start.5 = (f32[153,8,128]{2,1,0:T(8,128)S(1)}, f32[153,8,128]{2,1,0:T(8,128)}, u32[]{:S(2)}) copy-start(f32[153,8,128]{2,1,0:T(8,128)} %get-tuple-element.12.refs_1_) | copy-start | bytes 1880068
  13.3 0.7 copy-start.7
  13.9 24.7 %copy-start.1 = (f32[153,8,128]{2,1,0:T(8,128)S(1)}, f32[153,8,128]{2,1,0:T(8,128)}, u32[]{:S(2)}) copy-start(f32[153,8,128]{2,1,0:T(8,128)} %get-tuple-element.11.refs_0_) | copy-start | bytes 1880068
  16.8 46.6 %copy-start.6 = (s32[32]{0:T(128)S(1)}, s32[32]{0:T(128)}, u32[]{:S(2)}) copy-start(s32[32]{0:T(128)} %owner_ref.1) | copy-start | bytes 388
  16.8 5.8 %collective-permute-start.3 = (f32[21,8,128]{2,1,0:T(8,128)S(1)}, f32[21,8,128]{2,1,0:T(8,128)S(1)}, u32[]{:S(2)}, u32[]{:S(2)}) collective-permute-start(f32[21,8,128]{2,1,0:T(8,128)S(1)} %get-tuple-element.24), channel_id=1, source_target_pairs={{0,1},{1,2},{2,3},{3,4},{4,5},{5,6},{6,7},{7,0},{8,9},{9,10},{10,1... | collective-permute-start | bytes 258056 | tf_op jit(solution)/shard_map/ppermute | solution.py:543
  16.9 5.7 %collective-permute-start.4 = (f32[21,8,128]{2,1,0:T(8,128)S(1)}, f32[21,8,128]{2,1,0:T(8,128)S(1)}, u32[]{:S(2)}, u32[]{:S(2)}) collective-permute-start(f32[21,8,128]{2,1,0:T(8,128)S(1)} %get-tuple-element.25), channel_id=1, source_target_pairs={{1,0},{2,1},{3,2},{4,3},{5,4},{6,5},{7,6},{0,7},{9,8},{10,9},{11,1... | collective-permute-start | bytes 258056 | tf_op jit(solution)/shard_map/ppermute | solution.py:544
  20.4 43.0 %copy-start.2 = (bf16[1,8,4,256,256]{4,3,2,1,0:T(8,128)(2,1)S(1)}, bf16[1,8,4,256,256]{4,3,2,1,0:T(8,128)(2,1)}, u32[]{:S(2)}) copy-start(bf16[1,8,4,256,256]{4,3,2,1,0:T(8,128)(2,1)} %param.11) | copy-start | bytes 12582916
  22.7 26.1 %collective-permute-start.5 = (f32[21,8,128]{2,1,0:T(8,128)S(1)}, f32[21,8,128]{2,1,0:T(8,128)S(1)}, u32[]{:S(2)}, u32[]{:S(2)}) collective-permute-start(f32[21,8,128]{2,1,0:T(8,128)S(1)} %get-tuple-element.22), channel_id=1, source_target_pairs={{0,8},{8,0},{16,24},{24,16},{1,9},{9,1},{17,25},{25,17},{2,10},{10... | collective-permute-start | bytes 258056 | tf_op jit(solution)/shard_map/ppermute | solution.py:513
  24.8 24.0 %collective-permute-start.6 = (f32[21,8,128]{2,1,0:T(8,128)S(1)}, f32[21,8,128]{2,1,0:T(8,128)S(1)}, u32[]{:S(2)}, u32[]{:S(2)}) collective-permute-start(f32[21,8,128]{2,1,0:T(8,128)S(1)} %get-tuple-element.21), channel_id=1, source_target_pairs={{0,16},{8,24},{16,0},{24,8},{1,17},{9,25},{17,1},{25,9},{2,18},{10... | collective-permute-start | bytes 258056 | tf_op jit(solution)/shard_map/ppermute | solution.py:513
  26.3 22.5 %collective-permute-start.7 = (f32[21,8,128]{2,1,0:T(8,128)S(1)}, f32[21,8,128]{2,1,0:T(8,128)S(1)}, u32[]{:S(2)}, u32[]{:S(2)}) collective-permute-start(f32[21,8,128]{2,1,0:T(8,128)S(1)} %get-tuple-element.20), channel_id=1, source_target_pairs={{0,24},{8,16},{16,8},{24,0},{1,25},{9,17},{17,9},{25,1},{2,26},{10... | collective-permute-start | bytes 258056 | tf_op jit(solution)/shard_map/ppermute | solution.py:513
  55.8 3.7 %collective-permute-start.11 = (f32[2,8,128]{2,1,0:T(8,128)S(1)}, f32[2,8,128]{2,1,0:T(8,128)S(1)}, u32[]{:S(2)}, u32[]{:S(2)}) collective-permute-start(f32[2,8,128]{2,1,0:T(8,128)S(1)} %pad_maximum_fusion), channel_id=1, source_target_pairs={{0,8},{8,0},{16,24},{24,16},{1,9},{9,1},{17,25},{25,17},{2,10},{10... | collective-permute-start | bytes 24584 | tf_op jit(solution)/shard_map/ppermute | solution.py:580
  59.5 3.9 %collective-permute-start.12 = (f32[1,8,128]{2,1,0:T(8,128)S(1)}, f32[1,8,128]{2,1,0:T(8,128)S(1)}, u32[]{:S(2)}, u32[]{:S(2)}) collective-permute-start(f32[1,8,128]{2,1,0:T(8,128)S(1)} %slice_add_fusion), channel_id=1, source_target_pairs={{0,16},{8,24},{16,0},{24,8},{1,17},{9,25},{17,1},{25,9},{2,18},{10... | collective-permute-start | bytes 12296 | tf_op jit(solution)/shard_map/ppermute | solution.py:580
  65.7 18.3 %all-to-all-start = ((f32[32,8,256]{2,1,0:T(8,128)}), f32[32,8,256]{2,1,0:T(8,128)S(1)}, u32[]{:S(2)}, u32[]{:S(2)}) async-start(f32[32,8,256]{2,1,0:T(8,128)} %listen.1), calls=%async_computation | async-start | bytes 524288 | tf_op jit(solution)/shard_map/all_to_all | solution.py:598
  71.2 9.3 %collective-permute-start.10 = (f32[4,64,128]{2,1,0:T(8,128)S(1)}, f32[4,64,128]{2,1,0:T(8,128)S(1)}, u32[]{:S(2)}, u32[]{:S(2)}) collective-permute-start(f32[4,64,128]{2,1,0:T(8,128)S(1)} %get-tuple-element.18), channel_id=1, source_target_pairs={{0,24},{8,16},{16,8},{24,0},{1,25},{9,17},{17,9},{25,1},{2,26},{10... | collective-permute-start | bytes 393224 | tf_op jit(solution)/shard_map/ppermute | solution.py:513
  73.9 9.0 %collective-permute-start.8 = (f32[4,64,128]{2,1,0:T(8,128)S(1)}, f32[4,64,128]{2,1,0:T(8,128)S(1)}, u32[]{:S(2)}, u32[]{:S(2)}) collective-permute-start(f32[4,64,128]{2,1,0:T(8,128)S(1)} %get-tuple-element.16), channel_id=1, source_target_pairs={{0,8},{8,0},{16,24},{24,16},{1,9},{9,1},{17,25},{25,17},{2,10},{10... | collective-permute-start | bytes 393224 | tf_op jit(solution)/shard_map/ppermute | solution.py:513
  74.5 8.7 %collective-permute-start.9 = (f32[4,64,128]{2,1,0:T(8,128)S(1)}, f32[4,64,128]{2,1,0:T(8,128)S(1)}, u32[]{:S(2)}, u32[]{:S(2)}) collective-permute-start(f32[4,64,128]{2,1,0:T(8,128)S(1)} %get-tuple-element.17), channel_id=1, source_target_pairs={{0,16},{8,24},{16,0},{24,8},{1,17},{9,25},{17,1},{25,9},{2,18},{10... | collective-permute-start | bytes 393224 | tf_op jit(solution)/shard_map/ppermute | solution.py:513

commit v6 on v5

--- a/solution.py
+++ b/solution.py
@@ -12,7 +12,7 @@
 HALO = STEPS
 LANES = 128
 RELAX = 1.6
-UNROLL = 16
+UNROLL = 32
 
 VELOCITIES = (
     (0, 0, 0),
@@ -374,7 +374,7 @@
                 put(plain[1 - slot], turned[1 - slot], (side, r), out)
             return c
 
-        lax.fori_loop(1, depth + 1, row, 0, unroll=UNROLL // 2)
+        lax.fori_loop(1, depth + 1, row, 0, unroll=min(depth, UNROLL // 4))
         wrap(1 - slot)
 
     last = run_steps(step)
@@ -385,7 +385,7 @@
             means[q, r - 1] = jnp.where(at_left, both[1][q], both[0][q])
         return c
 
-    lax.fori_loop(1, depth + 1, final, 0, unroll=UNROLL // 2)
+    lax.fori_loop(1, depth + 1, final, 0, unroll=min(depth, UNROLL // 4))
 
     ids = jnp.where(lane < width, sub * (n * width) + me * width + lane, -1).astype(F32)
     for m in range(n):

time: 85.1 us -> 83.6 us (0.982)
  Pallas kernels: 27 us -> 25.5 us
    pallas_call x6, Pallas kernels: 27 us -> 25.5 us  [call(): pl.pallas_call(kernel, out_shape=out_shape, in_specs=specs, out_specs=[VM...]
  transfers between devices with their start and end apart: 14 -> 14, of which waited for: 7 -> 7; matrix products, arithmetic and copies ran while one was open for 0% -> 0% of each run, Pallas kernels for 16% -> 15%
where the time goes in v6:
time: 83.6 us; the launch traced here: 83.2 us
  waiting for transfers between devices  27 us (32%)
  Pallas kernels  25.5 us (31%)
  starting transfers between devices  23.6 us (28%)
  local copies, waits for them, and re-layouts  4.99 us (6%)
  between operations  1.4 us (2%)
    pallas_call x6, Pallas kernels, call(): pl.pallas_call(kernel, out_shape=out_shape, in_specs=specs, out_specs=[VM...  25.5 us
    ppermute x9, waiting for transfers between devices, exchange(): lax.ppermute(parts[m], 'gx', swap[m])  20.7 us
    ppermute x9, starting transfers between devices, exchange(): lax.ppermute(parts[m], 'gx', swap[m])  11.7 us
    all_to_all x1, starting transfers between devices, on_device(): gathered = lax.all_to_all(partial_signal, ('gx', 'gy'), 0, 0, tiled=True)  5.43 us
    unnamed x16, local copies, waits for them, and re-layouts  4.98 us
    ppermute x2, waiting for transfers between devices, on_device(): lax.ppermute(jnp.stack([found.pop(m) for m in moving]), 'gx', swap[bit])  4.05 us
    ppermute x1, starting transfers between devices, on_device(): after = lax.ppermute(strips[0], 'gy', down)  3.53 us
    ppermute x2, starting transfers between devices, on_device(): lax.ppermute(jnp.stack([found.pop(m) for m in moving]), 'gx', swap[bit])  2.92 us
  transfers between devices with their start and end apart: 14, of which 7 were waited for; matrix products, arithmetic and copies ran while one was open for 0% of the time, Pallas kernels for 15%

profile of v6, /device:TPU:0, one launch (start us, length us, event | category | flops | bytes accessed | tf_op | source)
XLA Modules:
  0.0 83.2 jit_solution(4385516320673644834)
XLA Ops:
  0.6 3.8 %pack.1 = (f32[153,8,128]{2,1,0:T(8,128)}, f32[153,8,128]{2,1,0:T(8,128)}, f32[153,8,128]{2,1,0:T(8,128)}, f32[153,8,128]{2,1,0:T(8,128)}) custom-call(s32[1]{0:T(128)} %bitcast.me_ref, f32[19,64,512]{2,1,0:T(8,128)} %bitcast.28, s32[64,512]{1,0:T(8,128)} %bitcast.30), custom_call_target="tpu_custom_call" | custom-call | tf_op jit(solution)/shard_map/pack/pallas_call | solution.py:489
  4.4 3.0 %collective-permute-start = (f32[153,8,128]{2,1,0:T(8,128)}, f32[153,8,128]{2,1,0:T(8,128)S(1)}, u32[]{:S(2)}, u32[]{:S(2)}) collective-permute-start(f32[153,8,128]{2,1,0:T(8,128)} %get-tuple-element.12.refs_1_), channel_id=1, source_target_pairs={{0,8},{8,0},{16,24},{24,16},{1,9},{9,1},{17,25},{25,17},{2,10},{10... | collective-permute-start | bytes 1880072 | tf_op jit(solution)/shard_map/ppermute | solution.py:513
  7.4 1.5 %collective-permute-start.1 = (f32[153,8,128]{2,1,0:T(8,128)}, f32[153,8,128]{2,1,0:T(8,128)S(1)}, u32[]{:S(2)}, u32[]{:S(2)}) collective-permute-start(f32[153,8,128]{2,1,0:T(8,128)} %get-tuple-element.13.refs_2_), channel_id=1, source_target_pairs={{0,16},{8,24},{16,0},{24,8},{1,17},{9,25},{17,1},{25,9},{2,18},{10... | collective-permute-start | bytes 1880072 | tf_op jit(solution)/shard_map/ppermute | solution.py:513
  8.9 0.0 collective-permute-start.2
  9.0 0.0 copy-start
  9.0 1.1 %copy-done = f32[153,8,128]{2,1,0:T(8,128)S(1)} copy-done((f32[153,8,128]{2,1,0:T(8,128)S(1)}, f32[153,8,128]{2,1,0:T(8,128)}, u32[]{:S(2)}) %copy-start) | copy-done | bytes 626712
  10.0 0.0 copy-start.3
  10.0 1.1 %copy-done.3 = f32[153,8,128]{2,1,0:T(8,128)S(1)} copy-done((f32[153,8,128]{2,1,0:T(8,128)S(1)}, f32[153,8,128]{2,1,0:T(8,128)}, u32[]{:S(2)}) %copy-start.3) | copy-done | bytes 626712
  11.1 0.0 copy-start.4
  11.1 1.1 %copy-done.4 = f32[153,8,128]{2,1,0:T(8,128)S(1)} copy-done((f32[153,8,128]{2,1,0:T(8,128)S(1)}, f32[153,8,128]{2,1,0:T(8,128)}, u32[]{:S(2)}) %copy-start.4) | copy-done | bytes 626712
  12.2 1.1 %copy-done.5 = f32[153,8,128]{2,1,0:T(8,128)S(1)} copy-done((f32[153,8,128]{2,1,0:T(8,128)S(1)}, f32[153,8,128]{2,1,0:T(8,128)}, u32[]{:S(2)}) %copy-start.5) | copy-done | bytes 626712
  13.3 0.7 copy-done.7
  13.9 2.9 %edges.1 = f32[6,21,8,128]{3,2,1,0:T(8,128)S(1)} custom-call(s32[1]{0:T(128)} %bitcast.me_ref, s32[1,8]{1,0:T(1,128)S(1)} %copy-done.7, f32[153,8,128]{2,1,0:T(8,128)S(1)} %copy-done, f32[153,8,128]{2,1,0:T(8,128)S(1)} %copy-done.5, f32[153,8,128]{2,1,0:T(8,128)S(1)} %copy-done.4, f32[153,8,128]{2,1,0:T(8,128)S(1)} %copy-done.3), custom_call_target="tpu_custom_call" | custom-call | tf_op jit(solution)/shard_map/edges/pallas_call | solution.py:489
  16.8 0.0 copy-start.6
  16.8 0.1 collective-permute-start.3
  16.9 3.5 %collective-permute-start.4 = (f32[21,8,128]{2,1,0:T(8,128)S(1)}, f32[21,8,128]{2,1,0:T(8,128)S(1)}, u32[]{:S(2)}, u32[]{:S(2)}) collective-permute-start(f32[21,8,128]{2,1,0:T(8,128)S(1)} %get-tuple-element.25), channel_id=1, source_target_pairs={{1,0},{2,1},{3,2},{4,3},{5,4},{6,5},{7,6},{0,7},{9,8},{10,9},{11,1... | collective-permute-start | bytes 258056 | tf_op jit(solution)/shard_map/ppermute | solution.py:544
  20.4 2.2 %collective-permute-done.3 = f32[21,8,128]{2,1,0:T(8,128)S(1)} collective-permute-done((f32[21,8,128]{2,1,0:T(8,128)S(1)}, f32[21,8,128]{2,1,0:T(8,128)S(1)}, u32[]{:S(2)}, u32[]{:S(2)}) %collective-permute-start.3) | collective-permute-done | bytes 86048 | tf_op jit(solution)/shard_map/ppermute | solution.py:543
  22.6 0.0 collective-permute-done.4
  22.6 0.1 fusion
  22.7 2.1 %collective-permute-start.5 = (f32[21,8,128]{2,1,0:T(8,128)S(1)}, f32[21,8,128]{2,1,0:T(8,128)S(1)}, u32[]{:S(2)}, u32[]{:S(2)}) collective-permute-start(f32[21,8,128]{2,1,0:T(8,128)S(1)} %get-tuple-element.22), channel_id=1, source_target_pairs={{0,8},{8,0},{16,24},{24,16},{1,9},{9,1},{17,25},{25,17},{2,10},{10... | collective-permute-start | bytes 258056 | tf_op jit(solution)/shard_map/ppermute | solution.py:513
  24.8 1.5 %collective-permute-start.6 = (f32[21,8,128]{2,1,0:T(8,128)S(1)}, f32[21,8,128]{2,1,0:T(8,128)S(1)}, u32[]{:S(2)}, u32[]{:S(2)}) collective-permute-start(f32[21,8,128]{2,1,0:T(8,128)S(1)} %get-tuple-element.21), channel_id=1, source_target_pairs={{0,16},{8,24},{16,0},{24,8},{1,17},{9,25},{17,1},{25,9},{2,18},{10... | collective-permute-start | bytes 258056 | tf_op jit(solution)/shard_map/ppermute | solution.py:513
  26.3 0.0 collective-permute-done.refs_1_
  26.3 0.0 collective-permute-start.7
  26.3 12.3 %collective-permute-done.1.refs_2_ = f32[153,8,128]{2,1,0:T(8,128)S(1)} collective-permute-done((f32[153,8,128]{2,1,0:T(8,128)}, f32[153,8,128]{2,1,0:T(8,128)S(1)}, u32[]{:S(2)}, u32[]{:S(2)}) %collective-permute-start.1) | collective-permute-done | bytes 626720 | tf_op jit(solution)/shard_map/ppermute | solution.py:513
  38.6 0.0 collective-permute-done.2.refs_3_
  38.6 0.0 copy-done.1
  38.6 8.8 %flow.1.refs_8_ = f32[4,32,8,128]{3,2,1,0:T(8,128)S(1)} custom-call(s32[1]{0:T(128)} %bitcast.me_ref, f32[153,8,128]{2,1,0:T(8,128)S(1)} %copy-done.1, f32[153,8,128]{2,1,0:T(8,128)S(1)} %collective-permute-done.refs_1_, f32[153,8,128]{2,1,0:T(8,128)S(1)} %collective-permute-done.1.refs_2_, f32[153,8,128]{2,1,0:T(8,128)S(1)} %collective-permute-done.2.refs_3_), custom_call_target="tpu_custom_call" | custom-call | bytes 76546048 | tf_op jit(solution)/shard_map/flow/pallas_call | solution.py:489
  47.4 0.0 collective-permute-done.5.refs_5_
  47.4 0.0 collective-permute-done.6.refs_6_
  47.4 0.0 collective-permute-done.7.refs_7_
  47.4 6.9 %seam.1 = (f32[4,64,128]{2,1,0:T(8,128)S(1)}, f32[4,64,128]{2,1,0:T(8,128)S(1)}, f32[4,64,128]{2,1,0:T(8,128)S(1)}, f32[4,64,128]{2,1,0:T(8,128)S(1)}, f32[4,8,128]{2,1,0:T(8,128)S(1)}) custom-call(s32[1]{0:T(128)} %bitcast.me_ref, f32[153,8,128]{2,1,0:T(8,128)S(1)} %copy-done.1, f32[153,8,128]{2,1,0:T(8,128)S(1)} %collective-permute-done.refs_1_, ...), custom_call_target="tpu_custom_call" | custom-call | bytes 38273024 | tf_op jit(solution)/shard_map/seam/pallas_call | solution.py:489
  54.4 0.6 collective-permute-start.11
  54.9 3.1 %collective-permute-done.11 = f32[2,8,128]{2,1,0:T(8,128)S(1)} collective-permute-done((f32[2,8,128]{2,1,0:T(8,128)S(1)}, f32[2,8,128]{2,1,0:T(8,128)S(1)}, u32[]{:S(2)}, u32[]{:S(2)}) %collective-permute-start.11) | collective-permute-done | bytes 8224 | tf_op jit(solution)/shard_map/ppermute | solution.py:580
  58.1 2.3 %collective-permute-start.12 = (f32[1,8,128]{2,1,0:T(8,128)S(1)}, f32[1,8,128]{2,1,0:T(8,128)S(1)}, u32[]{:S(2)}, u32[]{:S(2)}) collective-permute-start(f32[1,8,128]{2,1,0:T(8,128)S(1)} %slice_add_fusion), channel_id=1, source_target_pairs={{0,16},{8,24},{16,0},{24,8},{1,17},{9,25},{17,1},{25,9},{2,18},{10... | collective-permute-start | bytes 12296 | tf_op jit(solution)/shard_map/ppermute | solution.py:580
  61.0 0.9 %collective-permute-done.12 = f32[1,8,128]{2,1,0:T(8,128)S(1)} collective-permute-done((f32[1,8,128]{2,1,0:T(8,128)S(1)}, f32[1,8,128]{2,1,0:T(8,128)S(1)}, u32[]{:S(2)}, u32[]{:S(2)}) %collective-permute-start.12) | collective-permute-done | bytes 4128 | tf_op jit(solution)/shard_map/ppermute | solution.py:580
  62.0 0.0 copy-done.6
  62.0 0.0 copy-done.2
  62.0 2.3 %listen.1 = f32[32,8,256]{2,1,0:T(8,128)} custom-call(s32[1]{0:T(128)S(6)} %copy.8.count_ref, s32[32]{0:T(128)S(1)} %copy-done.6, f32[8,128]{1,0:T(8,128)S(1)} %fusion.5.picks, bf16[32,256,256]{2,1,0:T(8,128)(2,1)S(1)} %bitcast.27), custom_call_target="tpu_custom_call" | custom-call | tf_op jit(solution)/shard_map/listen/pallas_call | solution.py:489
  64.3 5.4 %all-to-all-start = ((f32[32,8,256]{2,1,0:T(8,128)}), f32[32,8,256]{2,1,0:T(8,128)S(1)}, u32[]{:S(2)}, u32[]{:S(2)}) async-start(f32[32,8,256]{2,1,0:T(8,128)} %listen.1), calls=%async_computation | async-start | bytes 524288 | tf_op jit(solution)/shard_map/all_to_all | solution.py:598
  69.8 2.7 %collective-permute-start.10 = (f32[4,64,128]{2,1,0:T(8,128)S(1)}, f32[4,64,128]{2,1,0:T(8,128)S(1)}, u32[]{:S(2)}, u32[]{:S(2)}) collective-permute-start(f32[4,64,128]{2,1,0:T(8,128)S(1)} %get-tuple-element.18), channel_id=1, source_target_pairs={{0,24},{8,16},{16,8},{24,0},{1,25},{9,17},{17,9},{25,1},{2,26},{10... | collective-permute-start | bytes 393224 | tf_op jit(solution)/shard_map/ppermute | solution.py:513
  72.5 0.6 collective-permute-start.8
  73.1 0.3 collective-permute-start.9
  73.3 5.7 %collective-permute-done.10.refs_3_ = f32[4,64,128]{2,1,0:T(8,128)S(1)} collective-permute-done((f32[4,64,128]{2,1,0:T(8,128)S(1)}, f32[4,64,128]{2,1,0:T(8,128)S(1)}, u32[]{:S(2)}, u32[]{:S(2)}) %collective-permute-start.10) | collective-permute-done | bytes 131104 | tf_op jit(solution)/shard_map/ppermute | solution.py:513
  79.0 2.4 %collective-permute-done.8.refs_1_ = f32[4,64,128]{2,1,0:T(8,128)S(1)} collective-permute-done((f32[4,64,128]{2,1,0:T(8,128)S(1)}, f32[4,64,128]{2,1,0:T(8,128)S(1)}, u32[]{:S(2)}, u32[]{:S(2)}) %collective-permute-start.8) | collective-permute-done | bytes 131104 | tf_op jit(solution)/shard_map/ppermute | solution.py:513
  81.5 0.3 collective-permute-done.9.refs_2_
  81.7 0.9 %join.1 = f32[4,64,512]{2,1,0:T(8,128)} custom-call(s32[1]{0:T(128)} %bitcast.me_ref, f32[4,64,128]{2,1,0:T(8,128)S(1)} %get-tuple-element.15.refs_0_, f32[4,64,128]{2,1,0:T(8,128)S(1)} %collective-permute-done.8.refs_1_, f32[4,64,128]{2,1,0:T(8,128)S(1)} %collective-permute-done.9.refs_2_, f32[4,64,128]{2,1,0:T(8,128)S(1)} %collective-permute-done.10.refs_3_), custom_call_target="tpu_custom_call" | custom-call | tf_op jit(solution)/shard_map/join/pallas_call | solution.py:489
  82.6 0.0 all-to-all-done
  82.6 0.6 reduce_sum.9
  (9 shorter events, 0.0 us)
Async XLA Ops:
  4.4 21.9 %collective-permute-start = (f32[153,8,128]{2,1,0:T(8,128)}, f32[153,8,128]{2,1,0:T(8,128)S(1)}, u32[]{:S(2)}, u32[]{:S(2)}) collective-permute-start(f32[153,8,128]{2,1,0:T(8,128)} %get-tuple-element.12.refs_1_), channel_id=1, source_target_pairs={{0,8},{8,0},{16,24},{24,16},{1,9},{9,1},{17,25},{25,17},{2,10},{10... | collective-permute-start | bytes 1880072 | tf_op jit(solution)/shard_map/ppermute | solution.py:513
  7.4 31.2 %collective-permute-start.1 = (f32[153,8,128]{2,1,0:T(8,128)}, f32[153,8,128]{2,1,0:T(8,128)S(1)}, u32[]{:S(2)}, u32[]{:S(2)}) collective-permute-start(f32[153,8,128]{2,1,0:T(8,128)} %get-tuple-element.13.refs_2_), channel_id=1, source_target_pairs={{0,16},{8,24},{16,0},{24,8},{1,17},{9,25},{17,1},{25,9},{2,18},{10... | collective-permute-start | bytes 1880072 | tf_op jit(solution)/shard_map/ppermute | solution.py:513
  8.9 29.6 %collective-permute-start.2 = (f32[153,8,128]{2,1,0:T(8,128)}, f32[153,8,128]{2,1,0:T(8,128)S(1)}, u32[]{:S(2)}, u32[]{:S(2)}) collective-permute-start(f32[153,8,128]{2,1,0:T(8,128)} %get-tuple-element.14.refs_3_), channel_id=1, source_target_pairs={{0,24},{8,16},{16,8},{24,0},{1,25},{9,17},{17,9},{25,1},{2,26},{10... | collective-permute-start | bytes 1880072 | tf_op jit(solution)/shard_map/ppermute | solution.py:513
  9.0 1.1 %copy-start = (f32[153,8,128]{2,1,0:T(8,128)S(1)}, f32[153,8,128]{2,1,0:T(8,128)}, u32[]{:S(2)}) copy-start(f32[153,8,128]{2,1,0:T(8,128)} %get-tuple-element.11.refs_0_) | copy-start | bytes 1880068
  10.0 1.1 %copy-start.3 = (f32[153,8,128]{2,1,0:T(8,128)S(1)}, f32[153,8,128]{2,1,0:T(8,128)}, u32[]{:S(2)}) copy-start(f32[153,8,128]{2,1,0:T(8,128)} %get-tuple-element.14.refs_3_) | copy-start | bytes 1880068
  11.1 1.1 %copy-start.4 = (f32[153,8,128]{2,1,0:T(8,128)S(1)}, f32[153,8,128]{2,1,0:T(8,128)}, u32[]{:S(2)}) copy-start(f32[153,8,128]{2,1,0:T(8,128)} %get-tuple-element.13.refs_2_) | copy-start | bytes 1880068
  12.2 1.1 %copy-start.5 = (f32[153,8,128]{2,1,0:T(8,128)S(1)}, f32[153,8,128]{2,1,0:T(8,128)}, u32[]{:S(2)}) copy-start(f32[153,8,128]{2,1,0:T(8,128)} %get-tuple-element.12.refs_1_) | copy-start | bytes 1880068
  13.3 0.7 copy-start.7
  13.9 24.7 %copy-start.1 = (f32[153,8,128]{2,1,0:T(8,128)S(1)}, f32[153,8,128]{2,1,0:T(8,128)}, u32[]{:S(2)}) copy-start(f32[153,8,128]{2,1,0:T(8,128)} %get-tuple-element.11.refs_0_) | copy-start | bytes 1880068
  16.8 45.2 %copy-start.6 = (s32[32]{0:T(128)S(1)}, s32[32]{0:T(128)}, u32[]{:S(2)}) copy-start(s32[32]{0:T(128)} %owner_ref.1) | copy-start | bytes 388
  16.8 5.8 %collective-permute-start.3 = (f32[21,8,128]{2,1,0:T(8,128)S(1)}, f32[21,8,128]{2,1,0:T(8,128)S(1)}, u32[]{:S(2)}, u32[]{:S(2)}) collective-permute-start(f32[21,8,128]{2,1,0:T(8,128)S(1)} %get-tuple-element.24), channel_id=1, source_target_pairs={{0,1},{1,2},{2,3},{3,4},{4,5},{5,6},{6,7},{7,0},{8,9},{9,10},{10,1... | collective-permute-start | bytes 258056 | tf_op jit(solution)/shard_map/ppermute | solution.py:543
  16.9 5.7 %collective-permute-start.4 = (f32[21,8,128]{2,1,0:T(8,128)S(1)}, f32[21,8,128]{2,1,0:T(8,128)S(1)}, u32[]{:S(2)}, u32[]{:S(2)}) collective-permute-start(f32[21,8,128]{2,1,0:T(8,128)S(1)} %get-tuple-element.25), channel_id=1, source_target_pairs={{1,0},{2,1},{3,2},{4,3},{5,4},{6,5},{7,6},{0,7},{9,8},{10,9},{11,1... | collective-permute-start | bytes 258056 | tf_op jit(solution)/shard_map/ppermute | solution.py:544
  20.4 41.6 %copy-start.2 = (bf16[1,8,4,256,256]{4,3,2,1,0:T(8,128)(2,1)S(1)}, bf16[1,8,4,256,256]{4,3,2,1,0:T(8,128)(2,1)}, u32[]{:S(2)}) copy-start(bf16[1,8,4,256,256]{4,3,2,1,0:T(8,128)(2,1)} %param.11) | copy-start | bytes 12582916
  22.7 24.7 %collective-permute-start.5 = (f32[21,8,128]{2,1,0:T(8,128)S(1)}, f32[21,8,128]{2,1,0:T(8,128)S(1)}, u32[]{:S(2)}, u32[]{:S(2)}) collective-permute-start(f32[21,8,128]{2,1,0:T(8,128)S(1)} %get-tuple-element.22), channel_id=1, source_target_pairs={{0,8},{8,0},{16,24},{24,16},{1,9},{9,1},{17,25},{25,17},{2,10},{10... | collective-permute-start | bytes 258056 | tf_op jit(solution)/shard_map/ppermute | solution.py:513
  24.8 22.6 %collective-permute-start.6 = (f32[21,8,128]{2,1,0:T(8,128)S(1)}, f32[21,8,128]{2,1,0:T(8,128)S(1)}, u32[]{:S(2)}, u32[]{:S(2)}) collective-permute-start(f32[21,8,128]{2,1,0:T(8,128)S(1)} %get-tuple-element.21), channel_id=1, source_target_pairs={{0,16},{8,24},{16,0},{24,8},{1,17},{9,25},{17,1},{25,9},{2,18},{10... | collective-permute-start | bytes 258056 | tf_op jit(solution)/shard_map/ppermute | solution.py:513
  26.3 21.1 %collective-permute-start.7 = (f32[21,8,128]{2,1,0:T(8,128)S(1)}, f32[21,8,128]{2,1,0:T(8,128)S(1)}, u32[]{:S(2)}, u32[]{:S(2)}) collective-permute-start(f32[21,8,128]{2,1,0:T(8,128)S(1)} %get-tuple-element.20), channel_id=1, source_target_pairs={{0,24},{8,16},{16,8},{24,0},{1,25},{9,17},{17,9},{25,1},{2,26},{10... | collective-permute-start | bytes 258056 | tf_op jit(solution)/shard_map/ppermute | solution.py:513
  54.4 3.7 %collective-permute-start.11 = (f32[2,8,128]{2,1,0:T(8,128)S(1)}, f32[2,8,128]{2,1,0:T(8,128)S(1)}, u32[]{:S(2)}, u32[]{:S(2)}) collective-permute-start(f32[2,8,128]{2,1,0:T(8,128)S(1)} %pad_maximum_fusion), channel_id=1, source_target_pairs={{0,8},{8,0},{16,24},{24,16},{1,9},{9,1},{17,25},{25,17},{2,10},{10... | collective-permute-start | bytes 24584 | tf_op jit(solution)/shard_map/ppermute | solution.py:580
  58.1 3.9 %collective-permute-start.12 = (f32[1,8,128]{2,1,0:T(8,128)S(1)}, f32[1,8,128]{2,1,0:T(8,128)S(1)}, u32[]{:S(2)}, u32[]{:S(2)}) collective-permute-start(f32[1,8,128]{2,1,0:T(8,128)S(1)} %slice_add_fusion), channel_id=1, source_target_pairs={{0,16},{8,24},{16,0},{24,8},{1,17},{9,25},{17,1},{25,9},{2,18},{10... | collective-permute-start | bytes 12296 | tf_op jit(solution)/shard_map/ppermute | solution.py:580
  64.3 18.3 %all-to-all-start = ((f32[32,8,256]{2,1,0:T(8,128)}), f32[32,8,256]{2,1,0:T(8,128)S(1)}, u32[]{:S(2)}, u32[]{:S(2)}) async-start(f32[32,8,256]{2,1,0:T(8,128)} %listen.1), calls=%async_computation | async-start | bytes 524288 | tf_op jit(solution)/shard_map/all_to_all | solution.py:598
  69.8 9.3 %collective-permute-start.10 = (f32[4,64,128]{2,1,0:T(8,128)S(1)}, f32[4,64,128]{2,1,0:T(8,128)S(1)}, u32[]{:S(2)}, u32[]{:S(2)}) collective-permute-start(f32[4,64,128]{2,1,0:T(8,128)S(1)} %get-tuple-element.18), channel_id=1, source_target_pairs={{0,24},{8,16},{16,8},{24,0},{1,25},{9,17},{17,9},{25,1},{2,26},{10... | collective-permute-start | bytes 393224 | tf_op jit(solution)/shard_map/ppermute | solution.py:513
  72.5 9.0 %collective-permute-start.8 = (f32[4,64,128]{2,1,0:T(8,128)S(1)}, f32[4,64,128]{2,1,0:T(8,128)S(1)}, u32[]{:S(2)}, u32[]{:S(2)}) collective-permute-start(f32[4,64,128]{2,1,0:T(8,128)S(1)} %get-tuple-element.16), channel_id=1, source_target_pairs={{0,8},{8,0},{16,24},{24,16},{1,9},{9,1},{17,25},{25,17},{2,10},{10... | collective-permute-start | bytes 393224 | tf_op jit(solution)/shard_map/ppermute | solution.py:513
  73.1 8.7 %collective-permute-start.9 = (f32[4,64,128]{2,1,0:T(8,128)S(1)}, f32[4,64,128]{2,1,0:T(8,128)S(1)}, u32[]{:S(2)}, u32[]{:S(2)}) collective-permute-start(f32[4,64,128]{2,1,0:T(8,128)S(1)} %get-tuple-element.17), channel_id=1, source_target_pairs={{0,16},{8,24},{16,0},{24,8},{1,17},{9,25},{17,1},{25,9},{2,18},{10... | collective-permute-start | bytes 393224 | tf_op jit(solution)/shard_map/ppermute | solution.py:513

commit v7 on v6

--- a/solution.py
+++ b/solution.py
@@ -585,6 +585,8 @@
     parts = exchange(parts)
 
     listeners, bins = retarded.shape[3:]
+    if weights.size <= 2**22:
+        weights = weights.astype(F32)
     tiles = n * ny
     partial_signal = call(
         listen_kernel,

time: 83.6 us -> 83.7 us (level)
  other arithmetic: 0.7 us -> 2.02 us
    convert_element_type x0 -> x1, other arithmetic: none -> 1.32 us  [on_device(): weights = weights.astype(F32)]
    ppermute x2, waiting for transfers between devices: 4.05 us -> 3.14 us  [on_device(): lax.ppermute(jnp.stack([found.pop(m) for m in moving]), 'gx', swap[bit])]
  transfers between devices with their start and end apart: 14 -> 14, of which waited for: 7 -> 6; matrix products, arithmetic and copies ran while one was open for 0% -> 2% of each run, Pallas kernels for 15% -> 15%
where the time goes in v7:
time: 83.7 us; the launch traced here: 83.3 us
  waiting for transfers between devices  26.2 us (31%)
  Pallas kernels  25.4 us (30%)
  starting transfers between devices  23.3 us (28%)
  local copies, waits for them, and re-layouts  4.99 us (6%)
  other arithmetic  2.02 us (2%)
  between operations  1.42 us (2%)
    pallas_call x6, Pallas kernels, call(): pl.pallas_call(kernel, out_shape=out_shape, in_specs=specs, out_specs=[VM...  25.4 us
    ppermute x9, waiting for transfers between devices, exchange(): lax.ppermute(parts[m], 'gx', swap[m])  20.8 us
    ppermute x9, starting transfers between devices, exchange(): lax.ppermute(parts[m], 'gx', swap[m])  11.8 us
    all_to_all x1, starting transfers between devices, on_device(): gathered = lax.all_to_all(partial_signal, ('gx', 'gy'), 0, 0, tiled=True)  5 us
    unnamed x16, local copies, waits for them, and re-layouts  4.97 us
    ppermute x1, starting transfers between devices, on_device(): after = lax.ppermute(strips[0], 'gy', down)  3.53 us
    ppermute x2, waiting for transfers between devices, on_device(): lax.ppermute(jnp.stack([found.pop(m) for m in moving]), 'gx', swap[bit])  3.14 us
    ppermute x2, starting transfers between devices, on_device(): lax.ppermute(jnp.stack([found.pop(m) for m in moving]), 'gx', swap[bit])  2.94 us
  transfers between devices with their start and end apart: 14, of which 6 were waited for; matrix products, arithmetic and copies ran while one was open for 2% of the time, Pallas kernels for 15%

profile of v7, /device:TPU:0, one launch (start us, length us, event | category | flops | bytes accessed | tf_op | source)
XLA Modules:
  0.0 83.3 jit_solution(12028355961580039884)
XLA Ops:
  0.6 3.8 %pack.1 = (f32[153,8,128]{2,1,0:T(8,128)}, f32[153,8,128]{2,1,0:T(8,128)}, f32[153,8,128]{2,1,0:T(8,128)}, f32[153,8,128]{2,1,0:T(8,128)}) custom-call(s32[1]{0:T(128)} %bitcast.me_ref, f32[19,64,512]{2,1,0:T(8,128)} %bitcast.29, s32[64,512]{1,0:T(8,128)} %bitcast.31), custom_call_target="tpu_custom_call" | custom-call | tf_op jit(solution)/shard_map/pack/pallas_call | solution.py:489
  4.4 3.0 %collective-permute-start = (f32[153,8,128]{2,1,0:T(8,128)}, f32[153,8,128]{2,1,0:T(8,128)S(1)}, u32[]{:S(2)}, u32[]{:S(2)}) collective-permute-start(f32[153,8,128]{2,1,0:T(8,128)} %get-tuple-element.12.refs_1_), channel_id=1, source_target_pairs={{0,8},{8,0},{16,24},{24,16},{1,9},{9,1},{17,25},{25,17},{2,10},{10... | collective-permute-start | bytes 1880072 | tf_op jit(solution)/shard_map/ppermute | solution.py:513
  7.4 1.5 %collective-permute-start.1 = (f32[153,8,128]{2,1,0:T(8,128)}, f32[153,8,128]{2,1,0:T(8,128)S(1)}, u32[]{:S(2)}, u32[]{:S(2)}) collective-permute-start(f32[153,8,128]{2,1,0:T(8,128)} %get-tuple-element.13.refs_2_), channel_id=1, source_target_pairs={{0,16},{8,24},{16,0},{24,8},{1,17},{9,25},{17,1},{25,9},{2,18},{10... | collective-permute-start | bytes 1880072 | tf_op jit(solution)/shard_map/ppermute | solution.py:513
  8.9 0.0 collective-permute-start.2
  9.0 0.0 copy-start
  9.0 1.1 %copy-done = f32[153,8,128]{2,1,0:T(8,128)S(1)} copy-done((f32[153,8,128]{2,1,0:T(8,128)S(1)}, f32[153,8,128]{2,1,0:T(8,128)}, u32[]{:S(2)}) %copy-start) | copy-done | bytes 626712
  10.0 0.0 copy-start.2
  10.0 1.1 %copy-done.2 = f32[153,8,128]{2,1,0:T(8,128)S(1)} copy-done((f32[153,8,128]{2,1,0:T(8,128)S(1)}, f32[153,8,128]{2,1,0:T(8,128)}, u32[]{:S(2)}) %copy-start.2) | copy-done | bytes 626712
  11.1 0.0 copy-start.3
  11.1 1.1 %copy-done.3 = f32[153,8,128]{2,1,0:T(8,128)S(1)} copy-done((f32[153,8,128]{2,1,0:T(8,128)S(1)}, f32[153,8,128]{2,1,0:T(8,128)}, u32[]{:S(2)}) %copy-start.3) | copy-done | bytes 626712
  12.2 1.1 %copy-done.4 = f32[153,8,128]{2,1,0:T(8,128)S(1)} copy-done((f32[153,8,128]{2,1,0:T(8,128)S(1)}, f32[153,8,128]{2,1,0:T(8,128)}, u32[]{:S(2)}) %copy-start.4) | copy-done | bytes 626712
  13.3 0.7 copy-done.6
  13.9 2.9 %edges.1 = f32[6,21,8,128]{3,2,1,0:T(8,128)S(1)} custom-call(s32[1]{0:T(128)} %bitcast.me_ref, s32[1,8]{1,0:T(1,128)S(1)} %copy-done.6, f32[153,8,128]{2,1,0:T(8,128)S(1)} %copy-done, f32[153,8,128]{2,1,0:T(8,128)S(1)} %copy-done.4, f32[153,8,128]{2,1,0:T(8,128)S(1)} %copy-done.3, f32[153,8,128]{2,1,0:T(8,128)S(1)} %copy-done.2), custom_call_target="tpu_custom_call" | custom-call | tf_op jit(solution)/shard_map/edges/pallas_call | solution.py:489
  16.8 0.1 collective-permute-start.3
  16.9 3.5 %collective-permute-start.4 = (f32[21,8,128]{2,1,0:T(8,128)S(1)}, f32[21,8,128]{2,1,0:T(8,128)S(1)}, u32[]{:S(2)}, u32[]{:S(2)}) collective-permute-start(f32[21,8,128]{2,1,0:T(8,128)S(1)} %get-tuple-element.25), channel_id=1, source_target_pairs={{1,0},{2,1},{3,2},{4,3},{5,4},{6,5},{7,6},{0,7},{9,8},{10,9},{11,1... | collective-permute-start | bytes 258056 | tf_op jit(solution)/shard_map/ppermute | solution.py:544
  20.4 2.2 %collective-permute-done.3 = f32[21,8,128]{2,1,0:T(8,128)S(1)} collective-permute-done((f32[21,8,128]{2,1,0:T(8,128)S(1)}, f32[21,8,128]{2,1,0:T(8,128)S(1)}, u32[]{:S(2)}, u32[]{:S(2)}) %collective-permute-start.3) | collective-permute-done | bytes 86048 | tf_op jit(solution)/shard_map/ppermute | solution.py:543
  22.6 0.0 collective-permute-done.4
  22.6 0.1 fusion
  22.7 3.0 %collective-permute-start.7 = (f32[21,8,128]{2,1,0:T(8,128)S(1)}, f32[21,8,128]{2,1,0:T(8,128)S(1)}, u32[]{:S(2)}, u32[]{:S(2)}) collective-permute-start(f32[21,8,128]{2,1,0:T(8,128)S(1)} %get-tuple-element.20), channel_id=1, source_target_pairs={{0,24},{8,16},{16,8},{24,0},{1,25},{9,17},{17,9},{25,1},{2,26},{10... | collective-permute-start | bytes 258056 | tf_op jit(solution)/shard_map/ppermute | solution.py:513
  25.7 0.5 collective-permute-start.6
  26.2 0.0 collective-permute-done.refs_1_
  26.2 0.1 collective-permute-start.5
  26.4 12.2 %collective-permute-done.1.refs_2_ = f32[153,8,128]{2,1,0:T(8,128)S(1)} collective-permute-done((f32[153,8,128]{2,1,0:T(8,128)}, f32[153,8,128]{2,1,0:T(8,128)S(1)}, u32[]{:S(2)}, u32[]{:S(2)}) %collective-permute-start.1) | collective-permute-done | bytes 626720 | tf_op jit(solution)/shard_map/ppermute | solution.py:513
  38.5 0.0 collective-permute-done.2.refs_3_
  38.5 0.0 copy-done.1
  38.6 8.8 %flow.1.refs_8_ = f32[4,32,8,128]{3,2,1,0:T(8,128)S(1)} custom-call(s32[1]{0:T(128)} %bitcast.me_ref, f32[153,8,128]{2,1,0:T(8,128)S(1)} %copy-done.1, f32[153,8,128]{2,1,0:T(8,128)S(1)} %collective-permute-done.refs_1_, f32[153,8,128]{2,1,0:T(8,128)S(1)} %collective-permute-done.1.refs_2_, f32[153,8,128]{2,1,0:T(8,128)S(1)} %collective-permute-done.2.refs_3_), custom_call_target="tpu_custom_call" | custom-call | bytes 76546048 | tf_op jit(solution)/shard_map/flow/pallas_call | solution.py:489
  47.4 0.0 collective-permute-done.7.refs_7_
  47.4 0.0 collective-permute-done.6.refs_6_
  47.4 0.0 collective-permute-done.5.refs_5_
  47.4 6.9 %seam.1 = (f32[4,64,128]{2,1,0:T(8,128)S(1)}, f32[4,64,128]{2,1,0:T(8,128)S(1)}, f32[4,64,128]{2,1,0:T(8,128)S(1)}, f32[4,64,128]{2,1,0:T(8,128)S(1)}, f32[4,8,128]{2,1,0:T(8,128)S(1)}) custom-call(s32[1]{0:T(128)} %bitcast.me_ref, f32[153,8,128]{2,1,0:T(8,128)S(1)} %copy-done.1, f32[153,8,128]{2,1,0:T(8,128)S(1)} %collective-permute-done.refs_1_, ...), custom_call_target="tpu_custom_call" | custom-call | bytes 38273024 | tf_op jit(solution)/shard_map/seam/pallas_call | solution.py:489
  54.3 0.6 collective-permute-start.11
  54.9 3.1 %collective-permute-done.11 = f32[2,8,128]{2,1,0:T(8,128)S(1)} collective-permute-done((f32[2,8,128]{2,1,0:T(8,128)S(1)}, f32[2,8,128]{2,1,0:T(8,128)S(1)}, u32[]{:S(2)}, u32[]{:S(2)}) %collective-permute-start.11) | collective-permute-done | bytes 8224 | tf_op jit(solution)/shard_map/ppermute | solution.py:580
  58.0 2.4 %collective-permute-start.12 = (f32[1,8,128]{2,1,0:T(8,128)S(1)}, f32[1,8,128]{2,1,0:T(8,128)S(1)}, u32[]{:S(2)}, u32[]{:S(2)}) collective-permute-start(f32[1,8,128]{2,1,0:T(8,128)S(1)} %slice_add_fusion), channel_id=1, source_target_pairs={{0,16},{8,24},{16,0},{24,8},{1,17},{9,25},{17,1},{25,9},{2,18},{10... | collective-permute-start | bytes 12296 | tf_op jit(solution)/shard_map/ppermute | solution.py:580
  60.4 0.0 copy-done.7
  60.4 1.3 %bitcast_convert_fusion.weights = f32[32,256,256]{2,1,0:T(8,128)S(1)} fusion(bf16[1,8,4,256,256]{4,3,2,1,0:T(8,128)(2,1)S(1)} %copy-done.7), kind=kLoop, calls=%fused_computation | loop fusion | flops 2097152 | bytes 12582912 | tf_op jit(solution)/shard_map/convert_element_type | solution.py:589
  62.4 0.0 collective-permute-done.12
  62.4 0.0 copy-done.5
  62.4 2.2 %listen.1 = f32[32,8,256]{2,1,0:T(8,128)} custom-call(s32[1]{0:T(128)S(6)} %copy.8.count_ref, s32[32]{0:T(128)S(1)} %copy-done.5, f32[8,128]{1,0:T(8,128)S(1)} %fusion.5.picks, f32[32,256,256]{2,1,0:T(8,128)S(1)} %bitcast_convert_fusion.weights), custom_call_target="tpu_custom_call" | custom-call | tf_op jit(solution)/shard_map/listen/pallas_call | solution.py:489
  64.6 5.0 %all-to-all-start = ((f32[32,8,256]{2,1,0:T(8,128)}), f32[32,8,256]{2,1,0:T(8,128)S(1)}, u32[]{:S(2)}, u32[]{:S(2)}) async-start(f32[32,8,256]{2,1,0:T(8,128)} %listen.1), calls=%async_computation | async-start | bytes 524288 | tf_op jit(solution)/shard_map/all_to_all | solution.py:600
  69.6 1.8 %collective-permute-start.8 = (f32[4,64,128]{2,1,0:T(8,128)S(1)}, f32[4,64,128]{2,1,0:T(8,128)S(1)}, u32[]{:S(2)}, u32[]{:S(2)}) collective-permute-start(f32[4,64,128]{2,1,0:T(8,128)S(1)} %get-tuple-element.16), channel_id=1, source_target_pairs={{0,8},{8,0},{16,24},{24,16},{1,9},{9,1},{17,25},{25,17},{2,10},{10... | collective-permute-start | bytes 393224 | tf_op jit(solution)/shard_map/ppermute | solution.py:513
  71.4 1.5 %collective-permute-start.9 = (f32[4,64,128]{2,1,0:T(8,128)S(1)}, f32[4,64,128]{2,1,0:T(8,128)S(1)}, u32[]{:S(2)}, u32[]{:S(2)}) collective-permute-start(f32[4,64,128]{2,1,0:T(8,128)S(1)} %get-tuple-element.17), channel_id=1, source_target_pairs={{0,16},{8,24},{16,0},{24,8},{1,17},{9,25},{17,1},{25,9},{2,18},{10... | collective-permute-start | bytes 393224 | tf_op jit(solution)/shard_map/ppermute | solution.py:513
  72.9 0.3 collective-permute-start.10
  73.2 4.7 %collective-permute-done.8.refs_1_ = f32[4,64,128]{2,1,0:T(8,128)S(1)} collective-permute-done((f32[4,64,128]{2,1,0:T(8,128)S(1)}, f32[4,64,128]{2,1,0:T(8,128)S(1)}, u32[]{:S(2)}, u32[]{:S(2)}) %collective-permute-start.8) | collective-permute-done | bytes 131104 | tf_op jit(solution)/shard_map/ppermute | solution.py:513
  77.9 1.4 %collective-permute-done.9.refs_2_ = f32[4,64,128]{2,1,0:T(8,128)S(1)} collective-permute-done((f32[4,64,128]{2,1,0:T(8,128)S(1)}, f32[4,64,128]{2,1,0:T(8,128)S(1)}, u32[]{:S(2)}, u32[]{:S(2)}) %collective-permute-start.9) | collective-permute-done | bytes 131104 | tf_op jit(solution)/shard_map/ppermute | solution.py:513
  79.3 2.5 %collective-permute-done.10.refs_3_ = f32[4,64,128]{2,1,0:T(8,128)S(1)} collective-permute-done((f32[4,64,128]{2,1,0:T(8,128)S(1)}, f32[4,64,128]{2,1,0:T(8,128)S(1)}, u32[]{:S(2)}, u32[]{:S(2)}) %collective-permute-start.10) | collective-permute-done | bytes 131104 | tf_op jit(solution)/shard_map/ppermute | solution.py:513
  81.8 0.9 %join.1 = f32[4,64,512]{2,1,0:T(8,128)} custom-call(s32[1]{0:T(128)} %bitcast.me_ref, f32[4,64,128]{2,1,0:T(8,128)S(1)} %get-tuple-element.15.refs_0_, f32[4,64,128]{2,1,0:T(8,128)S(1)} %collective-permute-done.8.refs_1_, f32[4,64,128]{2,1,0:T(8,128)S(1)} %collective-permute-done.9.refs_2_, f32[4,64,128]{2,1,0:T(8,128)S(1)} %collective-permute-done.10.refs_3_), custom_call_target="tpu_custom_call" | custom-call | tf_op jit(solution)/shard_map/join/pallas_call | solution.py:489
  82.7 0.0 all-to-all-done
  82.7 0.6 reduce_sum.9
  (10 shorter events, 0.0 us)
Async XLA Ops:
  4.4 21.8 %collective-permute-start = (f32[153,8,128]{2,1,0:T(8,128)}, f32[153,8,128]{2,1,0:T(8,128)S(1)}, u32[]{:S(2)}, u32[]{:S(2)}) collective-permute-start(f32[153,8,128]{2,1,0:T(8,128)} %get-tuple-element.12.refs_1_), channel_id=1, source_target_pairs={{0,8},{8,0},{16,24},{24,16},{1,9},{9,1},{17,25},{25,17},{2,10},{10... | collective-permute-start | bytes 1880072 | tf_op jit(solution)/shard_map/ppermute | solution.py:513
  7.4 31.1 %collective-permute-start.1 = (f32[153,8,128]{2,1,0:T(8,128)}, f32[153,8,128]{2,1,0:T(8,128)S(1)}, u32[]{:S(2)}, u32[]{:S(2)}) collective-permute-start(f32[153,8,128]{2,1,0:T(8,128)} %get-tuple-element.13.refs_2_), channel_id=1, source_target_pairs={{0,16},{8,24},{16,0},{24,8},{1,17},{9,25},{17,1},{25,9},{2,18},{10... | collective-permute-start | bytes 1880072 | tf_op jit(solution)/shard_map/ppermute | solution.py:513
  8.9 29.6 %collective-permute-start.2 = (f32[153,8,128]{2,1,0:T(8,128)}, f32[153,8,128]{2,1,0:T(8,128)S(1)}, u32[]{:S(2)}, u32[]{:S(2)}) collective-permute-start(f32[153,8,128]{2,1,0:T(8,128)} %get-tuple-element.14.refs_3_), channel_id=1, source_target_pairs={{0,24},{8,16},{16,8},{24,0},{1,25},{9,17},{17,9},{25,1},{2,26},{10... | collective-permute-start | bytes 1880072 | tf_op jit(solution)/shard_map/ppermute | solution.py:513
  9.0 1.1 %copy-start = (f32[153,8,128]{2,1,0:T(8,128)S(1)}, f32[153,8,128]{2,1,0:T(8,128)}, u32[]{:S(2)}) copy-start(f32[153,8,128]{2,1,0:T(8,128)} %get-tuple-element.11.refs_0_) | copy-start | bytes 1880068
  10.0 1.1 %copy-start.2 = (f32[153,8,128]{2,1,0:T(8,128)S(1)}, f32[153,8,128]{2,1,0:T(8,128)}, u32[]{:S(2)}) copy-start(f32[153,8,128]{2,1,0:T(8,128)} %get-tuple-element.14.refs_3_) | copy-start | bytes 1880068
  11.1 1.1 %copy-start.3 = (f32[153,8,128]{2,1,0:T(8,128)S(1)}, f32[153,8,128]{2,1,0:T(8,128)}, u32[]{:S(2)}) copy-start(f32[153,8,128]{2,1,0:T(8,128)} %get-tuple-element.13.refs_2_) | copy-start | bytes 1880068
  12.2 1.1 %copy-start.4 = (f32[153,8,128]{2,1,0:T(8,128)S(1)}, f32[153,8,128]{2,1,0:T(8,128)}, u32[]{:S(2)}) copy-start(f32[153,8,128]{2,1,0:T(8,128)} %get-tuple-element.12.refs_1_) | copy-start | bytes 1880068
  13.3 0.7 copy-start.6
  13.9 24.6 %copy-start.1 = (f32[153,8,128]{2,1,0:T(8,128)S(1)}, f32[153,8,128]{2,1,0:T(8,128)}, u32[]{:S(2)}) copy-start(f32[153,8,128]{2,1,0:T(8,128)} %get-tuple-element.11.refs_0_) | copy-start | bytes 1880068
  16.8 5.8 %collective-permute-start.3 = (f32[21,8,128]{2,1,0:T(8,128)S(1)}, f32[21,8,128]{2,1,0:T(8,128)S(1)}, u32[]{:S(2)}, u32[]{:S(2)}) collective-permute-start(f32[21,8,128]{2,1,0:T(8,128)S(1)} %get-tuple-element.24), channel_id=1, source_target_pairs={{0,1},{1,2},{2,3},{3,4},{4,5},{5,6},{6,7},{7,0},{8,9},{9,10},{10,1... | collective-permute-start | bytes 258056 | tf_op jit(solution)/shard_map/ppermute | solution.py:543
  16.9 5.7 %collective-permute-start.4 = (f32[21,8,128]{2,1,0:T(8,128)S(1)}, f32[21,8,128]{2,1,0:T(8,128)S(1)}, u32[]{:S(2)}, u32[]{:S(2)}) collective-permute-start(f32[21,8,128]{2,1,0:T(8,128)S(1)} %get-tuple-element.25), channel_id=1, source_target_pairs={{1,0},{2,1},{3,2},{4,3},{5,4},{6,5},{7,6},{0,7},{9,8},{10,9},{11,1... | collective-permute-start | bytes 258056 | tf_op jit(solution)/shard_map/ppermute | solution.py:544
  20.4 40.0 %copy-start.7 = (bf16[1,8,4,256,256]{4,3,2,1,0:T(8,128)(2,1)S(1)}, bf16[1,8,4,256,256]{4,3,2,1,0:T(8,128)(2,1)}, u32[]{:S(2)}) copy-start(bf16[1,8,4,256,256]{4,3,2,1,0:T(8,128)(2,1)} %param.11) | copy-start | bytes 12582916
  22.7 24.7 %collective-permute-start.7 = (f32[21,8,128]{2,1,0:T(8,128)S(1)}, f32[21,8,128]{2,1,0:T(8,128)S(1)}, u32[]{:S(2)}, u32[]{:S(2)}) collective-permute-start(f32[21,8,128]{2,1,0:T(8,128)S(1)} %get-tuple-element.20), channel_id=1, source_target_pairs={{0,24},{8,16},{16,8},{24,0},{1,25},{9,17},{17,9},{25,1},{2,26},{10... | collective-permute-start | bytes 258056 | tf_op jit(solution)/shard_map/ppermute | solution.py:513
  25.7 21.7 %collective-permute-start.6 = (f32[21,8,128]{2,1,0:T(8,128)S(1)}, f32[21,8,128]{2,1,0:T(8,128)S(1)}, u32[]{:S(2)}, u32[]{:S(2)}) collective-permute-start(f32[21,8,128]{2,1,0:T(8,128)S(1)} %get-tuple-element.21), channel_id=1, source_target_pairs={{0,16},{8,24},{16,0},{24,8},{1,17},{9,25},{17,1},{25,9},{2,18},{10... | collective-permute-start | bytes 258056 | tf_op jit(solution)/shard_map/ppermute | solution.py:513
  26.2 21.1 %collective-permute-start.5 = (f32[21,8,128]{2,1,0:T(8,128)S(1)}, f32[21,8,128]{2,1,0:T(8,128)S(1)}, u32[]{:S(2)}, u32[]{:S(2)}) collective-permute-start(f32[21,8,128]{2,1,0:T(8,128)S(1)} %get-tuple-element.22), channel_id=1, source_target_pairs={{0,8},{8,0},{16,24},{24,16},{1,9},{9,1},{17,25},{25,17},{2,10},{10... | collective-permute-start | bytes 258056 | tf_op jit(solution)/shard_map/ppermute | solution.py:513
  54.3 3.7 %collective-permute-start.11 = (f32[2,8,128]{2,1,0:T(8,128)S(1)}, f32[2,8,128]{2,1,0:T(8,128)S(1)}, u32[]{:S(2)}, u32[]{:S(2)}) collective-permute-start(f32[2,8,128]{2,1,0:T(8,128)S(1)} %pad_maximum_fusion), channel_id=1, source_target_pairs={{0,8},{8,0},{16,24},{24,16},{1,9},{9,1},{17,25},{25,17},{2,10},{10... | collective-permute-start | bytes 24584 | tf_op jit(solution)/shard_map/ppermute | solution.py:580
  58.0 4.4 %copy-start.5 = (s32[32]{0:T(128)S(1)}, s32[32]{0:T(128)}, u32[]{:S(2)}) copy-start(s32[32]{0:T(128)} %owner_ref.1) | copy-start | bytes 388
  58.0 4.4 %collective-permute-start.12 = (f32[1,8,128]{2,1,0:T(8,128)S(1)}, f32[1,8,128]{2,1,0:T(8,128)S(1)}, u32[]{:S(2)}, u32[]{:S(2)}) collective-permute-start(f32[1,8,128]{2,1,0:T(8,128)S(1)} %slice_add_fusion), channel_id=1, source_target_pairs={{0,16},{8,24},{16,0},{24,8},{1,17},{9,25},{17,1},{25,9},{2,18},{10... | collective-permute-start | bytes 12296 | tf_op jit(solution)/shard_map/ppermute | solution.py:580
  64.6 18.1 %all-to-all-start = ((f32[32,8,256]{2,1,0:T(8,128)}), f32[32,8,256]{2,1,0:T(8,128)S(1)}, u32[]{:S(2)}, u32[]{:S(2)}) async-start(f32[32,8,256]{2,1,0:T(8,128)} %listen.1), calls=%async_computation | async-start | bytes 524288 | tf_op jit(solution)/shard_map/all_to_all | solution.py:600
  69.6 8.3 %collective-permute-start.8 = (f32[4,64,128]{2,1,0:T(8,128)S(1)}, f32[4,64,128]{2,1,0:T(8,128)S(1)}, u32[]{:S(2)}, u32[]{:S(2)}) collective-permute-start(f32[4,64,128]{2,1,0:T(8,128)S(1)} %get-tuple-element.16), channel_id=1, source_target_pairs={{0,8},{8,0},{16,24},{24,16},{1,9},{9,1},{17,25},{25,17},{2,10},{10... | collective-permute-start | bytes 393224 | tf_op jit(solution)/shard_map/ppermute | solution.py:513
  71.4 7.8 %collective-permute-start.9 = (f32[4,64,128]{2,1,0:T(8,128)S(1)}, f32[4,64,128]{2,1,0:T(8,128)S(1)}, u32[]{:S(2)}, u32[]{:S(2)}) collective-permute-start(f32[4,64,128]{2,1,0:T(8,128)S(1)} %get-tuple-element.17), channel_id=1, source_target_pairs={{0,16},{8,24},{16,0},{24,8},{1,17},{9,25},{17,1},{25,9},{2,18},{10... | collective-permute-start | bytes 393224 | tf_op jit(solution)/shard_map/ppermute | solution.py:513
  72.9 8.9 %collective-permute-start.10 = (f32[4,64,128]{2,1,0:T(8,128)S(1)}, f32[4,64,128]{2,1,0:T(8,128)S(1)}, u32[]{:S(2)}, u32[]{:S(2)}) collective-permute-start(f32[4,64,128]{2,1,0:T(8,128)S(1)} %get-tuple-element.18), channel_id=1, source_target_pairs={{0,24},{8,16},{16,8},{24,0},{1,25},{9,17},{17,9},{25,1},{2,26},{10... | collective-permute-start | bytes 393224 | tf_op jit(solution)/shard_map/ppermute | solution.py:513
